TPU v7x, 512 devices: a whole 4x8x8 slice. The times are simulated.
512 devices in a mesh: rows: 256 (over x, y, z), sub: 2 (over core).
Axes of the slice: x: 4, y: 8, z: 8, core: 2. Of those that a mesh axis runs over, the one named last changes fastest.
Arguments:
- embeddings: float32 [688128, 768], P(('rows', 'sub')), may hold values from -350 to 350, as said below
- test_matrix: float32 [768, 80], replicated, may hold values from -6 to 6
Outputs:
- basis: float32 [688128, 80], P(('rows', 'sub'))
- projected: float32 [80, 768], replicated
Inputs may be any that keep to these rules, and one draw needn't show every extreme that they name: `embeddings`: entries are drawn independently within a row; each column, and possibly each row, carries its own scale, and the entries need not be centred.
All inputs are finite; a program needn't handle non-finite values.
Results may differ from a plain program's by a relative error of at most 0.00005.
Values sent between devices are 32-bit elements; how exact they have to be, the bound alone decides.
No kernel may reach another device: no remote copies, remote signals or barrier semaphores. Data moves between devices by JAX's collectives and lax.ppermute only.
A program may use at most 64 MiB of HBM per device.

v0:
```python
import jax
import jax.numpy as jnp
from jax import lax
from jax.sharding import PartitionSpec as P

HIGH = lax.Precision.HIGHEST


def product(left, right):
    return jnp.dot(left, right, precision=HIGH, preferred_element_type=jnp.float32)


def right_solve(matrix, lower):
    return lax.linalg.triangular_solve(lower, matrix, left_side=False, lower=True, transpose_a=True)


def orthonormal(matrix):
    gram = lax.psum(product(matrix.T, matrix), ("rows", "sub"))
    lower = jnp.linalg.cholesky(gram)
    return right_solve(matrix, lower)


def local(embeddings, test_matrix):
    row_total = embeddings.shape[0] * lax.axis_size("rows") * lax.axis_size("sub")
    factor = jnp.sqrt(jnp.float32(row_total))
    sketch = product(embeddings, test_matrix)
    first = orthonormal(sketch)
    spanned = lax.psum(product(embeddings.T, first), ("rows", "sub"))
    powered = product(embeddings, spanned)
    second = orthonormal(powered)
    projected = lax.psum(product(second.T, embeddings), ("rows", "sub"))
    return (second * factor, projected / factor)


def solution(mesh):
    in_specs = (P(("rows", "sub"), None), P())
    out_specs = (P(("rows", "sub"), None), P())
    return jax.shard_map(local, mesh=mesh, in_specs=in_specs, out_specs=out_specs, check_vma=False)
```

profile of v0, /device:TPU:1, one launch (start us, length us, event | category | flops | bytes accessed | tf_op | source)
XLA Modules:
  0.0 796.0 jit_solution(12338018808254575287)
XLA Ops:
  7.2 0.9 copy-done
  8.1 6.0 fusion.9
  14.1 0.6 fusion.10
  14.7 106.2 %psum.28 = f32[80,80]{0,1:T(8,128)S(1)} all-reduce(f32[80,80]{0,1:T(8,128)S(1)} %fusion.10), channel_id=1, replica_groups=mesh['rows'=256,'sub'=2] {'rows','sub'}, use_global_device_ids=true, to_apply=%region_0.0 | all-reduce | flops 6400 | bytes 51200 | tf_op jit(solution)/shard_map/psum | solution.py:18
  120.9 0.1 copy.5
  121.0 7.3 cholesky.44
  128.4 0.6 compare_reduce_fusion.1
  129.0 0.7 fusion.1
  129.7 6.1 custom-call.6
  135.8 0.6 convolution_bitcast_fusion.1
  136.4 5.6 convolution_bitcast_fusion.2
  142.0 0.2 all-reduce.5.cloned.1.call-start
  142.2 260.0 %all-reduce.3.cloned.1.call-done = f32[768,80]{0,1:T(8,128)} async-done(((f32[768,80]{0,1:T(8,128)}), f32[768,80]{0,1:T(8,128)}) %all-reduce.3.cloned.1.call-update) | async-done | bytes 245776 | tf_op jit(solution)/shard_map/psum | solution.py:28
  402.2 6.1 fusion.11
  408.4 0.6 fusion.12
  409.0 96.0 %psum.30 = f32[80,80]{0,1:T(8,128)S(1)} all-reduce(f32[80,80]{0,1:T(8,128)S(1)} %fusion.12), channel_id=1, replica_groups=mesh['rows'=256,'sub'=2] {'rows','sub'}, use_global_device_ids=true, to_apply=%region_4.7 | all-reduce | flops 6400 | bytes 51200 | tf_op jit(solution)/shard_map/psum | solution.py:18
  505.0 7.3 cholesky.55
  512.4 0.6 compare_reduce_fusion
  513.0 0.7 fusion.2
  513.7 6.1 custom-call.7
  519.8 1.3 broadcast_multiply_fusion
  521.2 5.6 fusion.13
  526.8 260.7 %all-reduce.5.cloned.1.call-done = f32[80,768]{1,0:T(8,128)} async-done(((f32[80,768]{1,0:T(8,128)}), f32[80,768]{1,0:T(8,128)}) %all-reduce.5.cloned.1.call-update) | async-done | bytes 245776 | tf_op jit(solution)/shard_map/psum | solution.py:31
  787.5 1.7 broadcast_multiply_fusion.1
  (9 shorter events, 0.2 us)
Async XLA Ops:
  7.2 1.0 copy-start
  7.2 395.1 %all-reduce.3.cloned.1.call-start = ((), (), s32[]{:S(2)}) async-start(), calls=%async_computation | async-start | bytes 491520 | tf_op jit(solution)/shard_map/psum | solution.py:28
  142.0 645.5 %all-reduce.5.cloned.1.call-start = ((), (), s32[]{:S(2)}) async-start(), calls=%async_computation.1 | async-start | bytes 491520 | tf_op jit(solution)/shard_map/psum | solution.py:31
Sparse Core Ops, SparseCore 0:
  142.1 260.0 all-reduce.2
  526.9 260.5 all-reduce.4
where the time goes:
time: 796 us
  waiting for transfers between devices  521 us (65%)
  blocking collectives  202 us (25%)
  other arithmetic  31.2 us (4%)
  matrix products  26.4 us (3%)
  between operations  14.2 us (2%)
    psum x1, waiting for transfers between devices, local(): projected = lax.psum(product(second.T, embeddings), ('rows', 'sub'))  261 us
    psum x1, waiting for transfers between devices, local(): spanned = lax.psum(product(embeddings.T, first), ('rows', 'sub'))  260 us
    psum x2, blocking collectives, orthonormal(): gram = lax.psum(product(matrix.T, matrix), ('rows', 'sub'))  202 us
    dot_general x6, matrix products, product(): jnp.dot(left, right, precision=HIGH, preferred_element_type=jnp.float32)  24.5 us
    another operation x6, other arithmetic, orthonormal(): lower = jnp.linalg.cholesky(gram)  16 us
  transfers between devices with their start and end apart: 2, of which 2 were waited for; matrix products, arithmetic and copies ran while one was open for 0% of the time, Pallas kernels for 0%

commit v1 on v0

v1 whole, which is shorter than its diff:
```python
import jax
import jax.numpy as jnp
from jax import lax
from jax.sharding import PartitionSpec as P

HIGH = lax.Precision.HIGHEST
SX, SY, SZ = 4, 8, 8


def product(left, right):
    return jnp.dot(left, right, precision=HIGH, preferred_element_type=jnp.float32)


def right_solve(matrix, lower):
    return lax.linalg.triangular_solve(lower, matrix, left_side=False, lower=True, transpose_a=True)


def partner(axis, k):
    pairs = []
    for x in range(SX):
        for y in range(SY):
            for z in range(SZ):
                to = [x, y, z]
                to[axis] ^= k
                pairs.append(((x * SY + y) * SZ + z, (to[0] * SY + to[1]) * SZ + to[2]))
    return pairs


def tree(parts):
    while len(parts) > 1:
        parts = [parts[i] + parts[i + 1] for i in range(0, len(parts), 2)]
    return parts[0]


def exchange(value, axis, size):
    return tree([value] + [lax.ppermute(value, "rows", partner(axis, k)) for k in range(1, size)])


def total(matrix):
    core = lax.axis_index("sub")
    y = lax.axis_index("rows") // SZ % SY
    tiles = matrix.reshape(10, 8, 6, 128).transpose(0, 2, 1, 3).reshape(60, 8, 128)
    tiles = jnp.pad(tiles, ((0, 4), (0, 0), (0, 0))).reshape(2, 8, 32, 128)
    swap = [(0, 1), (1, 0)]
    pick = lambda a, i: lax.dynamic_index_in_dim(a, i, 0, keepdims=False)
    half = pick(tiles, core) + lax.ppermute(pick(tiles, 1 - core), "sub", swap)
    parts = [pick(half, y)]
    for k in range(1, SY):
        parts.append(lax.ppermute(pick(half, y ^ k), "rows", partner(1, k)))
    piece = tree(parts)
    piece = exchange(piece, 2, SZ)
    piece = exchange(piece, 0, SX)
    half = jnp.zeros((8, 32, 128), jnp.float32)
    half = lax.dynamic_update_index_in_dim(half, piece, y, 0)
    for k in range(1, SY):
        half = lax.dynamic_update_index_in_dim(half, lax.ppermute(piece, "rows", partner(1, k)), y ^ k, 0)
    other = lax.ppermute(half, "sub", swap)
    tiles = jnp.where(core == 0, jnp.stack([half, other]), jnp.stack([other, half]))
    tiles = tiles.reshape(64, 8, 128)[:60]
    return tiles.reshape(10, 6, 8, 128).transpose(0, 2, 1, 3).reshape(80, 768)


def local(embeddings, test_matrix):
    row_total = embeddings.shape[0] * lax.axis_size("rows") * lax.axis_size("sub")
    factor = jnp.sqrt(jnp.float32(row_total))
    sketch = product(embeddings, test_matrix)
    image = total(product(sketch.T, embeddings)).T
    lower = jnp.linalg.cholesky(product(test_matrix.T, image))
    spanned = right_solve(image, lower)
    powered = product(embeddings, spanned)
    reach = total(product(powered.T, embeddings))
    gram = product(reach, spanned)
    gram = 0.5 * (gram + gram.T)
    lower = jnp.linalg.cholesky(gram)
    projected = lax.linalg.triangular_solve(lower, reach, left_side=True, lower=True)
    second = right_solve(powered, lower)
    return (second * factor, projected / factor)


def solution(mesh):
    in_specs = (P(("rows", "sub"), None), P())
    out_specs = (P(("rows", "sub"), None), P())
    return jax.shard_map(local, mesh=mesh, in_specs=in_specs, out_specs=out_specs, check_vma=False)
```

time: 796 us -> 287 us (0.36)
  waiting for transfers between devices: 521 us -> 21.6 us
  starting transfers between devices: 0.26 us -> 210 us
  blocking collectives: 202 us -> 0 us
  between operations: 14.2 us -> 1.83 us
    psum x2 -> x0, waiting for transfers between devices: 521 us -> none  [the longest x1 261 us: local(): projected = lax.psum(product(second.T, embeddings), ('rows', 'sub'))]
    ppermute x0 -> x52, starting transfers between devices: none -> 210 us  [the longest x20 73 us: exchange(): lax.ppermute(value, 'rows', partner(axis, k))]
    psum x2 -> x0, blocking collectives: 202 us -> none  [orthonormal(): gram = lax.psum(product(matrix.T, matrix), ('rows', 'sub'))]
    ppermute x0 -> x52, waiting for transfers between devices: none -> 21.6 us  [the longest x20 10.6 us: exchange(): lax.ppermute(value, 'rows', partner(axis, k))]
  transfers between devices with their start and end apart: 2 -> 52, of which waited for: 2 -> 12; matrix products, arithmetic and copies ran while one was open for 0% -> 0% of each run, Pallas kernels for 0% -> 0%
where the time goes in v1:
time: 287 us; the launch traced here: 285 us
  starting transfers between devices  210 us (73%)
  other arithmetic  29.7 us (10%)
  waiting for transfers between devices  21.6 us (8%)
  matrix products  20.3 us (7%)
    ppermute x20, starting transfers between devices, exchange(): lax.ppermute(value, 'rows', partner(axis, k))  73 us
    ppermute x14, starting transfers between devices, total(): lax.ppermute(piece, 'rows', partner(1, k))  51.4 us
    ppermute x14, starting transfers between devices, total(): parts.append(lax.ppermute(pick(half, y ^ k), 'rows', partner(1, k)))  51.1 us
    ppermute x2, starting transfers between devices, total(): other = lax.ppermute(half, 'sub', swap)  23.8 us
    dot_general x6, matrix products, product(): jnp.dot(left, right, precision=HIGH, preferred_element_type=jnp.float32)  17.5 us
    another operation x4, other arithmetic, right_solve(): lax.linalg.triangular_solve(lower, matrix, left_side=False, lower=True, t...  13.6 us
    ppermute x2, starting transfers between devices, total(): half = pick(tiles, core) + lax.ppermute(pick(tiles, 1 - core), 'sub', swap)  11.1 us
    ppermute x20, waiting for transfers between devices, exchange(): lax.ppermute(value, 'rows', partner(axis, k))  10.6 us
  transfers between devices with their start and end apart: 52, of which 12 were waited for; matrix products, arithmetic and copies ran while one was open for 0% of the time, Pallas kernels for 0%

profile of v1, /device:TPU:1, one launch (start us, length us, event | category | flops | bytes accessed | tf_op | source)
XLA Modules:
  0.0 285.2 jit_solution(6986983484039480748)
XLA Ops:
  1.6 5.4 %fusion.12 = f32[1344,80]{1,0:T(8,128)S(1)} fusion(f32[1344,768]{1,0:T(8,128)} %param.3, f32[768,80]{0,1:T(8,128)S(1)} %copy-done), kind=kOutput, calls=%fused_computation.67 | convolution fusion | flops 990904320 | bytes 4804608 | tf_op jit(solution)/shard_map/dot_general | solution.py:11
  9.5 8.8 %collective-permute-start = (f32[8,32,128]{2,1,0:T(8,128)S(1)}, f32[8,32,128]{2,1,0:T(8,128)S(1)}, u32[]{:S(2)}, u32[]{:S(2)}) collective-permute-start(f32[8,32,128]{2,1,0:T(8,128)S(1)} %dynamic-slice_bitcast_fusion.1), channel_id=1, source_target_pairs={{0,1},{1,0},{2,3},{3,2},{4,5},{5,4},{6,7},{7,6},{8,9},{9,8},{10,11... | collective-permute-start | bytes 393224 | tf_op jit(solution)/shard_map/ppermute | solution.py:46
  23.2 5.4 %collective-permute-start.3 = (f32[32,128]{1,0:T(8,128)S(1)}, f32[32,128]{1,0:T(8,128)S(1)}, u32[]{:S(2)}, u32[]{:S(2)}) collective-permute-start(f32[32,128]{1,0:T(8,128)S(1)} %get-tuple-element.14), channel_id=1, source_target_pairs={{0,48},{2,50},{4,52},{6,54},{8,56},{10,58},{12,60},{14,62},{16,32}... | collective-permute-start | bytes 49160 | tf_op jit(solution)/shard_map/ppermute | solution.py:49
  30.7 5.0 %collective-permute-start.5 = (f32[32,128]{1,0:T(8,128)S(1)}, f32[32,128]{1,0:T(8,128)S(1)}, u32[]{:S(2)}, u32[]{:S(2)}) collective-permute-start(f32[32,128]{1,0:T(8,128)S(1)} %get-tuple-element.17), channel_id=1, source_target_pairs={{0,80},{2,82},{4,84},{6,86},{8,88},{10,90},{12,92},{14,94},{16,64}... | collective-permute-start | bytes 49160 | tf_op jit(solution)/shard_map/ppermute | solution.py:49
  37.7 6.6 %collective-permute-start.7 = (f32[32,128]{1,0:T(8,128)S(1)}, f32[32,128]{1,0:T(8,128)S(1)}, u32[]{:S(2)}, u32[]{:S(2)}) collective-permute-start(f32[32,128]{1,0:T(8,128)S(1)} %get-tuple-element.15), channel_id=1, source_target_pairs={{0,112},{2,114},{4,116},{6,118},{8,120},{10,122},{12,124},{14,126}... | collective-permute-start | bytes 49160 | tf_op jit(solution)/shard_map/ppermute | solution.py:49
  45.5 5.4 %collective-permute-start.10 = (f32[32,128]{1,0:T(8,128)S(1)}, f32[32,128]{1,0:T(8,128)S(1)}, u32[]{:S(2)}, u32[]{:S(2)}) collective-permute-start(f32[32,128]{1,0:T(8,128)S(1)} %fusion.11), channel_id=1, source_target_pairs={{0,6},{2,4},{4,2},{6,0},{8,14},{10,12},{12,10},{14,8},{16,22},{18,... | collective-permute-start | bytes 49160 | tf_op jit(solution)/shard_map/ppermute | solution.py:36
  50.9 7.9 %collective-permute-start.11 = (f32[32,128]{1,0:T(8,128)S(1)}, f32[32,128]{1,0:T(8,128)S(1)}, u32[]{:S(2)}, u32[]{:S(2)}) collective-permute-start(f32[32,128]{1,0:T(8,128)S(1)} %fusion.11), channel_id=1, source_target_pairs={{0,8},{2,10},{4,12},{6,14},{8,0},{10,2},{12,4},{14,6},{16,24},{18,... | collective-permute-start | bytes 49160 | tf_op jit(solution)/shard_map/ppermute | solution.py:36
  60.8 4.5 %collective-permute-start.13 = (f32[32,128]{1,0:T(8,128)S(1)}, f32[32,128]{1,0:T(8,128)S(1)}, u32[]{:S(2)}, u32[]{:S(2)}) collective-permute-start(f32[32,128]{1,0:T(8,128)S(1)} %fusion.11), channel_id=1, source_target_pairs={{0,12},{2,14},{4,8},{6,10},{8,4},{10,6},{12,0},{14,2},{16,28},{18,... | collective-permute-start | bytes 49160 | tf_op jit(solution)/shard_map/ppermute | solution.py:36
  99.7 4.5 %collective-permute-start.21 = (f32[32,128]{1,0:T(8,128)S(1)}, f32[32,128]{1,0:T(8,128)S(1)}, u32[]{:S(2)}, u32[]{:S(2)}) collective-permute-start(f32[32,128]{1,0:T(8,128)S(1)} %get-tuple-element.6), channel_id=1, source_target_pairs={{0,64},{2,66},{4,68},{6,70},{8,72},{10,74},{12,76},{14,78},{16,80}... | collective-permute-start | bytes 49160 | tf_op jit(solution)/shard_map/ppermute | solution.py:56
  117.4 11.7 %collective-permute-start.25 = (f32[8,32,128]{2,1,0:T(8,128)S(1)}, f32[8,32,128]{2,1,0:T(8,128)S(1)}, u32[]{:S(2)}, u32[]{:S(2)}) collective-permute-start(f32[8,32,128]{2,1,0:T(8,128)S(1)} %bitcast_dynamic-update-slice_fusion.8), channel_id=1, source_target_pairs={{0,1},{1,0},{2,3},{3,2},{4,5},{5,4},{6,7},{7,6},{8,9},{9,8},{10,11... | collective-permute-start | bytes 393224 | tf_op jit(solution)/shard_map/ppermute | solution.py:57
  130.4 7.3 %cholesky.44 = f32[80,80]{1,0:T(8,128)S(1)} custom-call(f32[80,80]{1,0:T(8,128)S(1)} %add_multiply_fusion), custom_call_target="Cholesky" | custom-call | tf_op jit(solution)/shard_map/jit(cholesky)/cholesky | solution.py:68
  139.0 6.1 %custom-call.10 = f32[1,80,80]{1,2,0:T(8,128)S(1)} custom-call(f32[1,80,80]{2,1,0:T(8,128)S(1)} %fusion), custom_call_target="InvertDiagBlocksLowerTriangular" | custom-call | tf_op jit(solution)/shard_map/triangular_solve | solution.py:15
  145.6 6.2 %fusion.15 = f32[80,1344]{1,0:T(8,128)S(1)} fusion(f32[768,80]{0,1:T(8,128)S(1)} %fusion.6, f32[1344,768]{1,0:T(8,128)} %param.3), kind=kOutput, calls=%fused_computation.70 | convolution fusion | flops 990904320 | bytes 4804608 | tf_op jit(solution)/shard_map/dot_general | solution.py:11
  157.9 4.5 %collective-permute-start.27 = (f32[32,128]{1,0:T(8,128)S(1)}, f32[32,128]{1,0:T(8,128)S(1)}, u32[]{:S(2)}, u32[]{:S(2)}) collective-permute-start(f32[32,128]{1,0:T(8,128)S(1)} %get-tuple-element.13), channel_id=1, source_target_pairs={{0,16},{2,18},{4,20},{6,22},{8,24},{10,26},{12,28},{14,30},{16,0},... | collective-permute-start | bytes 49160 | tf_op jit(solution)/shard_map/ppermute | solution.py:49
  168.4 5.9 %collective-permute-start.30 = (f32[32,128]{1,0:T(8,128)S(1)}, f32[32,128]{1,0:T(8,128)S(1)}, u32[]{:S(2)}, u32[]{:S(2)}) collective-permute-start(f32[32,128]{1,0:T(8,128)S(1)} %get-tuple-element.11), channel_id=1, source_target_pairs={{0,64},{2,66},{4,68},{6,70},{8,72},{10,74},{12,76},{14,78},{16,80}... | collective-permute-start | bytes 49160 | tf_op jit(solution)/shard_map/ppermute | solution.py:49
  177.0 4.8 %collective-permute-start.32 = (f32[32,128]{1,0:T(8,128)S(1)}, f32[32,128]{1,0:T(8,128)S(1)}, u32[]{:S(2)}, u32[]{:S(2)}) collective-permute-start(f32[32,128]{1,0:T(8,128)S(1)} %get-tuple-element.9), channel_id=1, source_target_pairs={{0,96},{2,98},{4,100},{6,102},{8,104},{10,106},{12,108},{14,110},{... | collective-permute-start | bytes 49160 | tf_op jit(solution)/shard_map/ppermute | solution.py:49
  189.4 4.4 %collective-permute-start.35 = (f32[32,128]{1,0:T(8,128)S(1)}, f32[32,128]{1,0:T(8,128)S(1)}, u32[]{:S(2)}, u32[]{:S(2)}) collective-permute-start(f32[32,128]{1,0:T(8,128)S(1)} %fusion.9), channel_id=1, source_target_pairs={{0,4},{2,6},{4,0},{6,2},{8,12},{10,14},{12,8},{14,10},{16,20},{18,... | collective-permute-start | bytes 49160 | tf_op jit(solution)/shard_map/ppermute | solution.py:36
  196.8 5.7 %collective-permute-start.37 = (f32[32,128]{1,0:T(8,128)S(1)}, f32[32,128]{1,0:T(8,128)S(1)}, u32[]{:S(2)}, u32[]{:S(2)}) collective-permute-start(f32[32,128]{1,0:T(8,128)S(1)} %fusion.9), channel_id=1, source_target_pairs={{0,8},{2,10},{4,12},{6,14},{8,0},{10,2},{12,4},{14,6},{16,24},{18,... | collective-permute-start | bytes 49160 | tf_op jit(solution)/shard_map/ppermute | solution.py:36
  204.5 5.6 %collective-permute-start.39 = (f32[32,128]{1,0:T(8,128)S(1)}, f32[32,128]{1,0:T(8,128)S(1)}, u32[]{:S(2)}, u32[]{:S(2)}) collective-permute-start(f32[32,128]{1,0:T(8,128)S(1)} %fusion.9), channel_id=1, source_target_pairs={{0,12},{2,14},{4,8},{6,10},{8,4},{10,6},{12,0},{14,2},{16,28},{18,... | collective-permute-start | bytes 49160 | tf_op jit(solution)/shard_map/ppermute | solution.py:36
  221.3 4.4 %collective-permute-start.43 = (f32[32,128]{1,0:T(8,128)S(1)}, f32[32,128]{1,0:T(8,128)S(1)}, u32[]{:S(2)}, u32[]{:S(2)}) collective-permute-start(f32[32,128]{1,0:T(8,128)S(1)} %add_add_fusion.1), channel_id=1, source_target_pairs={{0,384},{2,386},{4,388},{6,390},{8,392},{10,394},{12,396},{14,398}... | collective-permute-start | bytes 49160 | tf_op jit(solution)/shard_map/ppermute | solution.py:36
  241.4 4.5 %collective-permute-start.48 = (f32[32,128]{1,0:T(8,128)S(1)}, f32[32,128]{1,0:T(8,128)S(1)}, u32[]{:S(2)}, u32[]{:S(2)}) collective-permute-start(f32[32,128]{1,0:T(8,128)S(1)} %get-tuple-element.4), channel_id=1, source_target_pairs={{0,80},{2,82},{4,84},{6,86},{8,88},{10,90},{12,92},{14,94},{16,64}... | collective-permute-start | bytes 49160 | tf_op jit(solution)/shard_map/ppermute | solution.py:56
  254.6 12.1 %collective-permute-start.51 = (f32[8,32,128]{2,1,0:T(8,128)S(1)}, f32[8,32,128]{2,1,0:T(8,128)S(1)}, u32[]{:S(2)}, u32[]{:S(2)}) collective-permute-start(f32[8,32,128]{2,1,0:T(8,128)S(1)} %bitcast_dynamic-update-slice_fusion), channel_id=1, source_target_pairs={{0,1},{1,0},{2,3},{3,2},{4,5},{5,4},{6,7},{7,6},{8,9},{9,8},{10,11... | collective-permute-start | bytes 393224 | tf_op jit(solution)/shard_map/ppermute | solution.py:57
  268.0 7.3 %cholesky.55 = f32[80,80]{1,0:T(8,128)S(1)} custom-call(f32[80,80]{1,0:T(8,128)S(1)} %fusion.4), custom_call_target="Cholesky" | custom-call | tf_op jit(solution)/shard_map/jit(cholesky)/cholesky | solution.py:74
  276.6 6.1 %custom-call.11 = f32[1,80,80]{1,2,0:T(8,128)S(1)} custom-call(f32[1,80,80]{2,1,0:T(8,128)S(1)} %fusion.1), custom_call_target="InvertDiagBlocksLowerTriangular" | custom-call | tf_op jit(solution)/shard_map/triangular_solve | solution.py:15
  (145 shorter events, 132.9 us)
Async XLA Ops:
  19.3 16.4 %collective-permute-start.1 = (f32[32,128]{1,0:T(8,128)S(1)}, f32[32,128]{1,0:T(8,128)S(1)}, u32[]{:S(2)}, u32[]{:S(2)}) collective-permute-start(f32[32,128]{1,0:T(8,128)S(1)} %get-tuple-element.20), channel_id=1, source_target_pairs={{0,16},{2,18},{4,20},{6,22},{8,24},{10,26},{12,28},{14,30},{16,0},... | collective-permute-start | bytes 49160 | tf_op jit(solution)/shard_map/ppermute | solution.py:49
  21.2 16.4 %collective-permute-start.2 = (f32[32,128]{1,0:T(8,128)S(1)}, f32[32,128]{1,0:T(8,128)S(1)}, u32[]{:S(2)}, u32[]{:S(2)}) collective-permute-start(f32[32,128]{1,0:T(8,128)S(1)} %get-tuple-element.19), channel_id=1, source_target_pairs={{0,32},{2,34},{4,36},{6,38},{8,40},{10,42},{12,44},{14,46},{16,48}... | collective-permute-start | bytes 49160 | tf_op jit(solution)/shard_map/ppermute | solution.py:49
  23.2 21.2 %collective-permute-start.3 = (f32[32,128]{1,0:T(8,128)S(1)}, f32[32,128]{1,0:T(8,128)S(1)}, u32[]{:S(2)}, u32[]{:S(2)}) collective-permute-start(f32[32,128]{1,0:T(8,128)S(1)} %get-tuple-element.14), channel_id=1, source_target_pairs={{0,48},{2,50},{4,52},{6,54},{8,56},{10,58},{12,60},{14,62},{16,32}... | collective-permute-start | bytes 49160 | tf_op jit(solution)/shard_map/ppermute | solution.py:49
  28.6 15.8 %collective-permute-start.4 = (f32[32,128]{1,0:T(8,128)S(1)}, f32[32,128]{1,0:T(8,128)S(1)}, u32[]{:S(2)}, u32[]{:S(2)}) collective-permute-start(f32[32,128]{1,0:T(8,128)S(1)} %get-tuple-element.18), channel_id=1, source_target_pairs={{0,64},{2,66},{4,68},{6,70},{8,72},{10,74},{12,76},{14,78},{16,80}... | collective-permute-start | bytes 49160 | tf_op jit(solution)/shard_map/ppermute | solution.py:49
  30.7 13.7 %collective-permute-start.5 = (f32[32,128]{1,0:T(8,128)S(1)}, f32[32,128]{1,0:T(8,128)S(1)}, u32[]{:S(2)}, u32[]{:S(2)}) collective-permute-start(f32[32,128]{1,0:T(8,128)S(1)} %get-tuple-element.17), channel_id=1, source_target_pairs={{0,80},{2,82},{4,84},{6,86},{8,88},{10,90},{12,92},{14,94},{16,64}... | collective-permute-start | bytes 49160 | tf_op jit(solution)/shard_map/ppermute | solution.py:49
  45.5 21.8 %collective-permute-start.10 = (f32[32,128]{1,0:T(8,128)S(1)}, f32[32,128]{1,0:T(8,128)S(1)}, u32[]{:S(2)}, u32[]{:S(2)}) collective-permute-start(f32[32,128]{1,0:T(8,128)S(1)} %fusion.11), channel_id=1, source_target_pairs={{0,6},{2,4},{4,2},{6,0},{8,14},{10,12},{12,10},{14,8},{16,22},{18,... | collective-permute-start | bytes 49160 | tf_op jit(solution)/shard_map/ppermute | solution.py:36
  50.9 20.4 %collective-permute-start.11 = (f32[32,128]{1,0:T(8,128)S(1)}, f32[32,128]{1,0:T(8,128)S(1)}, u32[]{:S(2)}, u32[]{:S(2)}) collective-permute-start(f32[32,128]{1,0:T(8,128)S(1)} %fusion.11), channel_id=1, source_target_pairs={{0,8},{2,10},{4,12},{6,14},{8,0},{10,2},{12,4},{14,6},{16,24},{18,... | collective-permute-start | bytes 49160 | tf_op jit(solution)/shard_map/ppermute | solution.py:36
  58.9 15.6 %collective-permute-start.12 = (f32[32,128]{1,0:T(8,128)S(1)}, f32[32,128]{1,0:T(8,128)S(1)}, u32[]{:S(2)}, u32[]{:S(2)}) collective-permute-start(f32[32,128]{1,0:T(8,128)S(1)} %fusion.11), channel_id=1, source_target_pairs={{0,10},{2,8},{4,14},{6,12},{8,2},{10,0},{12,6},{14,4},{16,26},{18,... | collective-permute-start | bytes 49160 | tf_op jit(solution)/shard_map/ppermute | solution.py:36
  89.9 18.4 %collective-permute-start.18 = (f32[32,128]{1,0:T(8,128)S(1)}, f32[32,128]{1,0:T(8,128)S(1)}, u32[]{:S(2)}, u32[]{:S(2)}) collective-permute-start(f32[32,128]{1,0:T(8,128)S(1)} %get-tuple-element.6), channel_id=1, source_target_pairs={{0,16},{2,18},{4,20},{6,22},{8,24},{10,26},{12,28},{14,30},{16,0},... | collective-permute-start | bytes 49160 | tf_op jit(solution)/shard_map/ppermute | solution.py:56
  93.8 17.9 %collective-permute-start.19 = (f32[32,128]{1,0:T(8,128)S(1)}, f32[32,128]{1,0:T(8,128)S(1)}, u32[]{:S(2)}, u32[]{:S(2)}) collective-permute-start(f32[32,128]{1,0:T(8,128)S(1)} %get-tuple-element.6), channel_id=1, source_target_pairs={{0,32},{2,34},{4,36},{6,38},{8,40},{10,42},{12,44},{14,46},{16,48}... | collective-permute-start | bytes 49160 | tf_op jit(solution)/shard_map/ppermute | solution.py:56
  96.7 18.8 %collective-permute-start.20 = (f32[32,128]{1,0:T(8,128)S(1)}, f32[32,128]{1,0:T(8,128)S(1)}, u32[]{:S(2)}, u32[]{:S(2)}) collective-permute-start(f32[32,128]{1,0:T(8,128)S(1)} %get-tuple-element.6), channel_id=1, source_target_pairs={{0,48},{2,50},{4,52},{6,54},{8,56},{10,58},{12,60},{14,62},{16,32}... | collective-permute-start | bytes 49160 | tf_op jit(solution)/shard_map/ppermute | solution.py:56
  99.7 15.8 %collective-permute-start.21 = (f32[32,128]{1,0:T(8,128)S(1)}, f32[32,128]{1,0:T(8,128)S(1)}, u32[]{:S(2)}, u32[]{:S(2)}) collective-permute-start(f32[32,128]{1,0:T(8,128)S(1)} %get-tuple-element.6), channel_id=1, source_target_pairs={{0,64},{2,66},{4,68},{6,70},{8,72},{10,74},{12,76},{14,78},{16,80}... | collective-permute-start | bytes 49160 | tf_op jit(solution)/shard_map/ppermute | solution.py:56
  157.9 19.1 %collective-permute-start.27 = (f32[32,128]{1,0:T(8,128)S(1)}, f32[32,128]{1,0:T(8,128)S(1)}, u32[]{:S(2)}, u32[]{:S(2)}) collective-permute-start(f32[32,128]{1,0:T(8,128)S(1)} %get-tuple-element.13), channel_id=1, source_target_pairs={{0,16},{2,18},{4,20},{6,22},{8,24},{10,26},{12,28},{14,30},{16,0},... | collective-permute-start | bytes 49160 | tf_op jit(solution)/shard_map/ppermute | solution.py:49
  162.5 19.3 %collective-permute-start.28 = (f32[32,128]{1,0:T(8,128)S(1)}, f32[32,128]{1,0:T(8,128)S(1)}, u32[]{:S(2)}, u32[]{:S(2)}) collective-permute-start(f32[32,128]{1,0:T(8,128)S(1)} %get-tuple-element.12), channel_id=1, source_target_pairs={{0,32},{2,34},{4,36},{6,38},{8,40},{10,42},{12,44},{14,46},{16,48}... | collective-permute-start | bytes 49160 | tf_op jit(solution)/shard_map/ppermute | solution.py:49
  165.3 18.8 %collective-permute-start.29 = (f32[32,128]{1,0:T(8,128)S(1)}, f32[32,128]{1,0:T(8,128)S(1)}, u32[]{:S(2)}, u32[]{:S(2)}) collective-permute-start(f32[32,128]{1,0:T(8,128)S(1)} %get-tuple-element.7), channel_id=1, source_target_pairs={{0,48},{2,50},{4,52},{6,54},{8,56},{10,58},{12,60},{14,62},{16,32}... | collective-permute-start | bytes 49160 | tf_op jit(solution)/shard_map/ppermute | solution.py:49
  168.4 15.7 %collective-permute-start.30 = (f32[32,128]{1,0:T(8,128)S(1)}, f32[32,128]{1,0:T(8,128)S(1)}, u32[]{:S(2)}, u32[]{:S(2)}) collective-permute-start(f32[32,128]{1,0:T(8,128)S(1)} %get-tuple-element.11), channel_id=1, source_target_pairs={{0,64},{2,66},{4,68},{6,70},{8,72},{10,74},{12,76},{14,78},{16,80}... | collective-permute-start | bytes 49160 | tf_op jit(solution)/shard_map/ppermute | solution.py:49
  187.5 17.0 %collective-permute-start.34 = (f32[32,128]{1,0:T(8,128)S(1)}, f32[32,128]{1,0:T(8,128)S(1)}, u32[]{:S(2)}, u32[]{:S(2)}) collective-permute-start(f32[32,128]{1,0:T(8,128)S(1)} %fusion.9), channel_id=1, source_target_pairs={{0,2},{2,0},{4,6},{6,4},{8,10},{10,8},{12,14},{14,12},{16,18},{18,... | collective-permute-start | bytes 49160 | tf_op jit(solution)/shard_map/ppermute | solution.py:36
  189.4 20.7 %collective-permute-start.35 = (f32[32,128]{1,0:T(8,128)S(1)}, f32[32,128]{1,0:T(8,128)S(1)}, u32[]{:S(2)}, u32[]{:S(2)}) collective-permute-start(f32[32,128]{1,0:T(8,128)S(1)} %fusion.9), channel_id=1, source_target_pairs={{0,4},{2,6},{4,0},{6,2},{8,12},{10,14},{12,8},{14,10},{16,20},{18,... | collective-permute-start | bytes 49160 | tf_op jit(solution)/shard_map/ppermute | solution.py:36
  193.9 18.7 %collective-permute-start.36 = (f32[32,128]{1,0:T(8,128)S(1)}, f32[32,128]{1,0:T(8,128)S(1)}, u32[]{:S(2)}, u32[]{:S(2)}) collective-permute-start(f32[32,128]{1,0:T(8,128)S(1)} %fusion.9), channel_id=1, source_target_pairs={{0,6},{2,4},{4,2},{6,0},{8,14},{10,12},{12,10},{14,8},{16,22},{18,... | collective-permute-start | bytes 49160 | tf_op jit(solution)/shard_map/ppermute | solution.py:36
  196.8 15.7 %collective-permute-start.37 = (f32[32,128]{1,0:T(8,128)S(1)}, f32[32,128]{1,0:T(8,128)S(1)}, u32[]{:S(2)}, u32[]{:S(2)}) collective-permute-start(f32[32,128]{1,0:T(8,128)S(1)} %fusion.9), channel_id=1, source_target_pairs={{0,8},{2,10},{4,12},{6,14},{8,0},{10,2},{12,4},{14,6},{16,24},{18,... | collective-permute-start | bytes 49160 | tf_op jit(solution)/shard_map/ppermute | solution.py:36
  227.0 18.9 %collective-permute-start.44 = (f32[32,128]{1,0:T(8,128)S(1)}, f32[32,128]{1,0:T(8,128)S(1)}, u32[]{:S(2)}, u32[]{:S(2)}) collective-permute-start(f32[32,128]{1,0:T(8,128)S(1)} %get-tuple-element.4), channel_id=1, source_target_pairs={{0,16},{2,18},{4,20},{6,22},{8,24},{10,26},{12,28},{14,30},{16,0},... | collective-permute-start | bytes 49160 | tf_op jit(solution)/shard_map/ppermute | solution.py:56
  231.3 17.5 %collective-permute-start.45 = (f32[32,128]{1,0:T(8,128)S(1)}, f32[32,128]{1,0:T(8,128)S(1)}, u32[]{:S(2)}, u32[]{:S(2)}) collective-permute-start(f32[32,128]{1,0:T(8,128)S(1)} %get-tuple-element.4), channel_id=1, source_target_pairs={{0,32},{2,34},{4,36},{6,38},{8,40},{10,42},{12,44},{14,46},{16,48}... | collective-permute-start | bytes 49160 | tf_op jit(solution)/shard_map/ppermute | solution.py:56
  234.1 18.9 %collective-permute-start.46 = (f32[32,128]{1,0:T(8,128)S(1)}, f32[32,128]{1,0:T(8,128)S(1)}, u32[]{:S(2)}, u32[]{:S(2)}) collective-permute-start(f32[32,128]{1,0:T(8,128)S(1)} %get-tuple-element.4), channel_id=1, source_target_pairs={{0,48},{2,50},{4,52},{6,54},{8,56},{10,58},{12,60},{14,62},{16,32}... | collective-permute-start | bytes 49160 | tf_op jit(solution)/shard_map/ppermute | solution.py:56
  237.3 15.8 %collective-permute-start.47 = (f32[32,128]{1,0:T(8,128)S(1)}, f32[32,128]{1,0:T(8,128)S(1)}, u32[]{:S(2)}, u32[]{:S(2)}) collective-permute-start(f32[32,128]{1,0:T(8,128)S(1)} %get-tuple-element.4), channel_id=1, source_target_pairs={{0,64},{2,66},{4,68},{6,70},{8,72},{10,74},{12,76},{14,78},{16,80}... | collective-permute-start | bytes 49160 | tf_op jit(solution)/shard_map/ppermute | solution.py:56
  (31 other events, 243.4 us)

commit v2 on v0

v2 whole, which is shorter than its diff:
```python
import jax
import jax.numpy as jnp
import numpy as np
from jax import lax
from jax.experimental import pallas as pl
from jax.experimental.pallas import tpu as pltpu
from jax.sharding import Mesh, PartitionSpec as P

SX, SY, SZ = 4, 8, 8
D, RANK = 768, 80
BLOCK = 128
NB = D // BLOCK
UPPER = [(a, b) for a in range(NB) for b in range(a + 1, NB)]
PACKED = len(UPPER) * BLOCK
DIAGS = PACKED + NB // 2 * BLOCK
FLAT = 2560
CHUNK = 448


def split(value):
    high = value.astype(jnp.bfloat16)
    rest = value - high.astype(jnp.float32)
    mid = rest.astype(jnp.bfloat16)
    low = (rest - mid.astype(jnp.float32)).astype(jnp.bfloat16)
    return high, mid, low


def dot(left, right):
    return jnp.dot(left, right, preferred_element_type=jnp.float32)


def exact(left, right, dims):
    return lax.dot_general(left, right, (dims, ((), ())), precision=lax.Precision.HIGHEST,
                           preferred_element_type=jnp.float32)


def iota(axis):
    return lax.broadcasted_iota(jnp.int32, (BLOCK, BLOCK), axis)


def gram_kernel(x_ref, flat_ref, even_ref, odd_ref):
    step = pl.program_id(0)
    high, mid, low = split(x_ref[...])
    high_t, mid_t, low_t = high.T, mid.T, low.T
    slot = 0
    for i in range(3):
        rows = slice(256 * i, 256 * (i + 1))
        for j in range(i, 3):
            cols = slice(256 * j, 256 * (j + 1))
            main = dot(high_t[rows], high[:, cols]) + dot(mid_t[rows], mid[:, cols])
            side = dot(high_t[rows], mid[:, cols]) + dot(high_t[rows], low[:, cols])
            if i != j:
                main = main + side + dot(mid_t[rows], high[:, cols]) + dot(low_t[rows], high[:, cols])

            @pl.when(step == 0)
            def _():
                even_ref[slot] = main
                if i == j:
                    odd_ref[i] = side

            @pl.when(step > 0)
            def _():
                even_ref[slot] += main
                if i == j:
                    odd_ref[i] += side
            slot += 1

    @pl.when(step == pl.num_programs(0) - 1)
    def _():
        row, col = iota(0), iota(1)
        slot = 0
        diagonals = []
        for i in range(3):
            for j in range(i, 3):
                value = even_ref[slot]
                slot += 1
                if i == j:
                    value = value + (odd_ref[i] + odd_ref[i].T)
                for p in range(2):
                    for q in range(2):
                        a, b = 2 * i + p, 2 * j + q
                        if a < b:
                            at = UPPER.index((a, b)) * BLOCK
                            flat_ref[at:at + BLOCK, :] = value[p * BLOCK:(p + 1) * BLOCK, q * BLOCK:(q + 1) * BLOCK]
                if i == j:
                    first, second = value[:BLOCK, :BLOCK], value[BLOCK:, BLOCK:]
                    at = PACKED + i * BLOCK
                    flat_ref[at:at + BLOCK, :] = jnp.where(row <= col, first, second)
                    diagonals.append(jnp.sum(jnp.where(row == col, second, 0.0), axis=0, keepdims=True))
        flat_ref[DIAGS:, :] = jnp.zeros((FLAT - DIAGS, BLOCK), jnp.float32)
        for i in range(3):
            flat_ref[DIAGS + i:DIAGS + i + 1, :] = diagonals[i]


def inverse_factor(gram):
    row = lax.broadcasted_iota(jnp.int32, (RANK, RANK), 0)
    col = lax.broadcasted_iota(jnp.int32, (RANK, RANK), 1)
    lane = lax.broadcasted_iota(jnp.int32, (1, RANK), 1)
    state = gram
    for j in range(RANK):
        pivot = state[j:j + 1, :]
        inverse = 1.0 / state[j:j + 1, j:j + 1]
        factor = jnp.where(row[:, :1] > j, state[:, j:j + 1] * inverse, 0.0)
        cleared = jnp.where((col == j) & (row > j), 0.0, state)
        state = cleared - factor * jnp.where(lane == j, 1.0, pivot)
    scale = lax.rsqrt(jnp.sum(jnp.where(row == col, state, 0.0), axis=1, keepdims=True))
    return jnp.where(row > col, state, jnp.where(row == col, 1.0, 0.0)) * scale


def finish_kernel(factor, flat_ref, test_ref, x_hbm, basis_ref, projected_ref, x_ref, c_ref, sem):
    copy = pltpu.make_async_copy(x_hbm, x_ref, sem)
    copy.start()
    row, col = iota(0), iota(1)
    for n, (a, b) in enumerate(UPPER):
        value = flat_ref[n * BLOCK:(n + 1) * BLOCK, :]
        c_ref[a * BLOCK:(a + 1) * BLOCK, b * BLOCK:(b + 1) * BLOCK] = value
        c_ref[b * BLOCK:(b + 1) * BLOCK, a * BLOCK:(a + 1) * BLOCK] = value.T
    for i in range(NB // 2):
        value = flat_ref[PACKED + i * BLOCK:PACKED + (i + 1) * BLOCK, :]
        flipped = value.T
        at = 2 * i * BLOCK
        c_ref[at:at + BLOCK, at:at + BLOCK] = jnp.where(row <= col, value, flipped)
        at += BLOCK
        other = jnp.where(row > col, value, flipped)
        c_ref[at:at + BLOCK, at:at + BLOCK] = jnp.where(row == col, flat_ref[DIAGS + i:DIAGS + i + 1, :], other)
    test = test_ref[...]
    image = exact(c_ref[...], test, ((1,), (0,)))
    first = inverse_factor(exact(test, image, ((0,), (0,))))
    spanned = exact(image, first, ((1,), (1,)))
    reach = exact(c_ref[...], spanned, ((1,), (0,)))
    second = inverse_factor(exact(spanned, reach, ((0,), (0,))))
    projected_ref[...] = exact(second, reach, ((1,), (1,))) / factor
    weight = exact(spanned, second, ((1,), (1,))) * factor
    copy.wait()
    basis_ref[...] = exact(x_ref[...], weight, ((1,), (0,)))


def tree(parts):
    while len(parts) > 1:
        parts = [parts[i] + parts[i + 1] for i in range(0, len(parts), 2)]
    return parts[0]


def everyone(value, axis, size):
    return lax.all_to_all(jnp.broadcast_to(value, (size,) + value.shape), axis, 0, 0)


def pick(array, i):
    return lax.dynamic_index_in_dim(array, i, 0, keepdims=False)


def stacked_sum(values):
    return tree([values[i] for i in range(values.shape[0])])


def total(flat):
    core = lax.axis_index("core")
    swap = [(0, 1), (1, 0)]
    halves = flat.reshape(2, FLAT // 2, BLOCK)
    value = pick(halves, core) + lax.ppermute(pick(halves, 1 - core), "core", swap)
    value = stacked_sum(lax.all_to_all(value.reshape(SX, -1, BLOCK), "x", 0, 0))
    value = stacked_sum(lax.all_to_all(value.reshape(SY, -1, BLOCK), "y", 0, 0))
    value = stacked_sum(everyone(value, "z", SZ))
    value = everyone(value, "y", SY).reshape(-1, BLOCK)
    value = everyone(value, "x", SX).reshape(-1, BLOCK)
    other = lax.ppermute(value, "core", swap)
    low = jnp.where(core == 0, value, other)
    high = jnp.where(core == 0, other, value)
    return jnp.concatenate([low, high])


def local(embeddings, test_matrix):
    rows = embeddings.shape[0]
    factor = float(np.sqrt(np.float32(rows * 2 * SX * SY * SZ)))
    flat = pl.pallas_call(
        gram_kernel,
        grid=(rows // CHUNK,),
        in_specs=[pl.BlockSpec((CHUNK, D), lambda i: (i, 0))],
        out_specs=pl.BlockSpec((FLAT, BLOCK), lambda i: (0, 0)),
        out_shape=jax.ShapeDtypeStruct((FLAT, BLOCK), jnp.float32),
        scratch_shapes=[pltpu.VMEM((6, 256, 256), jnp.float32), pltpu.VMEM((3, 256, 256), jnp.float32)],
        compiler_params=pltpu.CompilerParams(vmem_limit_bytes=32 * 2 ** 20),
        cost_estimate=pl.CostEstimate(flops=2 * rows * D * D * 4, bytes_accessed=4 * rows * D, transcendentals=0),
    )(embeddings)
    flat = total(flat)
    return pl.pallas_call(
        lambda *refs: finish_kernel(factor, *refs),
        in_specs=[pl.BlockSpec(memory_space=pltpu.VMEM)] * 2 + [pl.BlockSpec(memory_space=pl.ANY)],
        out_specs=[pl.BlockSpec(memory_space=pltpu.VMEM)] * 2,
        out_shape=[jax.ShapeDtypeStruct((rows, RANK), jnp.float32), jax.ShapeDtypeStruct((RANK, D), jnp.float32)],
        scratch_shapes=[pltpu.VMEM((rows, D), jnp.float32), pltpu.VMEM((D, D), jnp.float32), pltpu.SemaphoreType.DMA],
        compiler_params=pltpu.CompilerParams(vmem_limit_bytes=48 * 2 ** 20),
        cost_estimate=pl.CostEstimate(flops=2 * rows * D * RANK * 8, bytes_accessed=4 * rows * D, transcendentals=0),
    )(flat, test_matrix, embeddings)


def solution(mesh):
    grid = Mesh(mesh.devices.reshape(SX, SY, SZ, 2), ("x", "y", "z", "core"))
    in_specs = (P(("x", "y", "z", "core"), None), P())
    out_specs = (P(("x", "y", "z", "core"), None), P())
    return jax.shard_map(local, mesh=grid, in_specs=in_specs, out_specs=out_specs, check_vma=False)
```

time: 796 us -> 130 us (0.16)
  waiting for transfers between devices: 521 us -> 3.04 us
  blocking collectives: 202 us -> 62.5 us
  Pallas kernels: 0 us -> 41.6 us
  other arithmetic: 31.2 us -> 0.3 us
  matrix products: 26.4 us -> 0 us
  starting transfers between devices: 0.26 us -> 17.6 us
  between operations: 14.2 us -> 0.75 us
    psum x2 -> x0, waiting for transfers between devices: 521 us -> none  [the longest x1 261 us: local(): projected = lax.psum(product(second.T, embeddings), ('rows', 'sub'))]
    psum x2 -> x0, blocking collectives: 202 us -> none  [orthonormal(): gram = lax.psum(product(matrix.T, matrix), ('rows', 'sub'))]
    all_to_all x0 -> x5, blocking collectives: none -> 62.5 us  [the longest x3 38.7 us: everyone(): lax.all_to_all(jnp.broadcast_to(value, (size,) + value.shape), axis, 0, 0)]
    pallas_call x0 -> x2, Pallas kernels: none -> 41.6 us  [the longest x1 27.1 us: local(): pl.pallas_call(lambda *refs: finish_kernel(factor, *refs), in_specs=[pl.B...]
    another operation x10 -> x0, other arithmetic: 29.5 us -> none  [the longest x6 16 us: orthonormal(): lower = jnp.linalg.cholesky(gram)]
    dot_general x6 -> x0, matrix products: 24.5 us -> none  [product(): jnp.dot(left, right, precision=HIGH, preferred_element_type=jnp.float32)]
    ppermute x0 -> x2, starting transfers between devices: none -> 17.6 us  [the longest x1 8.84 us: total(): other = lax.ppermute(value, 'core', swap)]
where the time goes in v2:
time: 130 us; the launch traced here: 129 us
  blocking collectives  62.5 us (48%)
  Pallas kernels  41.6 us (32%)
  starting transfers between devices  17.6 us (14%)
  local copies, waits for them, and re-layouts  3.48 us (3%)
  waiting for transfers between devices  3.04 us (2%)
    all_to_all x3, blocking collectives, everyone(): lax.all_to_all(jnp.broadcast_to(value, (size,) + value.shape), axis, 0, 0)  38.7 us
    pallas_call x1, Pallas kernels, local(): pl.pallas_call(lambda *refs: finish_kernel(factor, *refs), in_specs=[pl.B...  27.1 us
    pallas_call x1, Pallas kernels, local(): pl.pallas_call(gram_kernel, grid=(rows // CHUNK,), in_specs=[pl.BlockSpec...  14.5 us
    all_to_all x1, blocking collectives, total(): value = stacked_sum(lax.all_to_all(value.reshape(SX, -1, BLOCK), 'x', 0, 0))  13 us
    all_to_all x1, blocking collectives, total(): value = stacked_sum(lax.all_to_all(value.reshape(SY, -1, BLOCK), 'y', 0, 0))  10.8 us
    ppermute x1, starting transfers between devices, total(): other = lax.ppermute(value, 'core', swap)  8.84 us
    ppermute x1, starting transfers between devices, total(): lax.ppermute(pick(halves, 1 - core), 'core', swap)  8.79 us
  transfers between devices with their start and end apart: 2, of which 2 were waited for; matrix products, arithmetic and copies ran while one was open for 0% of the time, Pallas kernels for 0%

profile of v2, /device:TPU:1, one launch (start us, length us, event | category | flops | bytes accessed | tf_op | source)
XLA Modules:
  0.0 129.3 jit_solution(534000474326491829)
XLA Ops:
  0.6 0.0 copy-start
  0.6 2.2 %copy-done = f32[1344,768]{1,0:T(8,128)S(1)} copy-done((f32[1344,768]{1,0:T(8,128)S(1)}, f32[1344,768]{1,0:T(8,128)}, u32[]{:S(2)}) %copy-start) | copy-done | bytes 4128792
  2.8 14.5 %shard_map.41 = f32[2560,128]{1,0:T(8,128)S(1)} custom-call(f32[1344,768]{1,0:T(8,128)S(1)} %copy-done), custom_call_target="tpu_custom_call" | custom-call | flops 6341787648 | bytes 4128768 | tf_op jit(solution)/shard_map/pallas_call | solution.py:175
  17.3 0.1 dynamic-slice_bitcast_fusion
  17.4 8.8 %collective-permute-start = (f32[1280,128]{1,0:T(8,128)S(1)}, f32[1280,128]{1,0:T(8,128)S(1)}, u32[]{:S(2)}, u32[]{:S(2)}) collective-permute-start(f32[1280,128]{1,0:T(8,128)S(1)} %dynamic-slice_bitcast_fusion), channel_id=1, source_target_pairs={{0,1},{1,0},{2,3},{3,2},{4,5},{5,4},{6,7},{7,6},{8,9},{9,8},{10,11... | collective-permute-start | bytes 1966088 | tf_op jit(solution)/shard_map/ppermute | solution.py:160
  26.2 1.7 %collective-permute-done = f32[1280,128]{1,0:T(8,128)S(1)} collective-permute-done((f32[1280,128]{1,0:T(8,128)S(1)}, f32[1280,128]{1,0:T(8,128)S(1)}, u32[]{:S(2)}, u32[]{:S(2)}) %collective-permute-start) | collective-permute-done | bytes 655392 | tf_op jit(solution)/shard_map/ppermute | solution.py:160
  27.9 0.1 bitcast_add_fusion
  27.9 13.0 %all_to_all.25 = f32[4,320,128]{2,1,0:T(8,128)S(1)} all-to-all(f32[4,320,128]{2,1,0:T(8,128)S(1)} %bitcast.17), channel_id=1, replica_groups=mesh['x'=4,'y'=8,'z'=8,'core'=2] {'x'}, dimensions={0} | all-to-all | bytes 1310720 | tf_op jit(solution)/shard_map/all_to_all | solution.py:161
  41.0 10.8 %all_to_all.26 = f32[8,40,128]{2,1,0:T(8,128)S(1)} all-to-all(f32[8,40,128]{2,1,0:T(8,128)S(1)} %bitcast.19), channel_id=1, replica_groups=mesh['x'=4,'y'=8,'z'=8,'core'=2] {'y'}, dimensions={0} | all-to-all | bytes 327680 | tf_op jit(solution)/shard_map/all_to_all | solution.py:162
  51.8 17.9 %all_to_all.27 = f32[8,40,128]{2,1,0:T(8,128)S(1)} all-to-all(f32[8,40,128]{2,1,0:T(8,128)S(1)} %broadcast_in_dim.9), channel_id=1, replica_groups=mesh['x'=4,'y'=8,'z'=8,'core'=2] {'z'}, dimensions={0} | all-to-all | bytes 327680 | tf_op jit(solution)/shard_map/all_to_all | solution.py:145
  69.7 0.0 copy-start.1
  69.8 10.8 %all_to_all.28 = f32[8,40,128]{2,1,0:T(8,128)S(1)} all-to-all(f32[8,40,128]{2,1,0:T(8,128)S(1)} %broadcast_in_dim.10), channel_id=1, replica_groups=mesh['x'=4,'y'=8,'z'=8,'core'=2] {'y'}, dimensions={0} | all-to-all | bytes 327680 | tf_op jit(solution)/shard_map/all_to_all | solution.py:145
  80.6 10.0 %all_to_all.29 = f32[4,320,128]{2,1,0:T(8,128)S(1)} all-to-all(f32[4,320,128]{2,1,0:T(8,128)S(1)} %broadcast_in_dim.11), channel_id=1, replica_groups=mesh['x'=4,'y'=8,'z'=8,'core'=2] {'x'}, dimensions={0} | all-to-all | bytes 1310720 | tf_op jit(solution)/shard_map/all_to_all | solution.py:145
  90.6 8.8 %collective-permute-start.1 = (f32[1280,128]{1,0:T(8,128)S(1)}, f32[1280,128]{1,0:T(8,128)S(1)}, u32[]{:S(2)}, u32[]{:S(2)}) collective-permute-start(f32[1280,128]{1,0:T(8,128)S(1)} %bitcast.18), channel_id=1, source_target_pairs={{0,1},{1,0},{2,3},{3,2},{4,5},{5,4},{6,7},{7,6},{8,9},{9,8},{10,11... | collective-permute-start | bytes 1966088 | tf_op jit(solution)/shard_map/ppermute | solution.py:166
  99.5 0.0 copy-done.1
  99.5 0.2 copy.4.refs_1_
  99.7 1.3 %collective-permute-done.1 = f32[1280,128]{1,0:T(8,128)S(1)} collective-permute-done((f32[1280,128]{1,0:T(8,128)S(1)}, f32[1280,128]{1,0:T(8,128)S(1)}, u32[]{:S(2)}, u32[]{:S(2)}) %collective-permute-start.1) | collective-permute-done | bytes 655392 | tf_op jit(solution)/shard_map/ppermute | solution.py:166
  101.0 0.1 broadcast_select_fusion.1
  101.1 0.1 pad_maximum_fusion.refs_0_
  101.2 27.1 %shard_map.42 = (f32[1344,80]{1,0:T(8,128)S(1)}, f32[80,768]{1,0:T(8,128)}) custom-call(f32[2560,128]{1,0:T(8,128)S(1)} %pad_maximum_fusion.refs_0_, f32[768,80]{1,0:T(8,128)S(1)} %copy.4.refs_1_, f32[1344,768]{1,0:T(8,128)} %refs_2_.1), custom_call_target="tpu_custom_call" | custom-call | flops 1321205760 | bytes 4128768 | tf_op jit(solution)/shard_map/pallas_call | solution.py:186
  128.3 1.0 copy.5
  (6 shorter events, 0.1 us)
Async XLA Ops:
  0.6 2.2 %copy-start = (f32[1344,768]{1,0:T(8,128)S(1)}, f32[1344,768]{1,0:T(8,128)}, u32[]{:S(2)}) copy-start(f32[1344,768]{1,0:T(8,128)} %refs_2_.1) | copy-start | bytes 12386308
  17.4 10.5 %collective-permute-start = (f32[1280,128]{1,0:T(8,128)S(1)}, f32[1280,128]{1,0:T(8,128)S(1)}, u32[]{:S(2)}, u32[]{:S(2)}) collective-permute-start(f32[1280,128]{1,0:T(8,128)S(1)} %dynamic-slice_bitcast_fusion), channel_id=1, source_target_pairs={{0,1},{1,0},{2,3},{3,2},{4,5},{5,4},{6,7},{7,6},{8,9},{9,8},{10,11... | collective-permute-start | bytes 1966088 | tf_op jit(solution)/shard_map/ppermute | solution.py:160
  69.7 29.8 %copy-start.1 = (f32[768,80]{0,1:T(8,128)S(1)}, f32[768,80]{0,1:T(8,128)}, u32[]{:S(2)}) copy-start(f32[768,80]{0,1:T(8,128)} %param.3) | copy-start | bytes 737284
  90.6 10.4 %collective-permute-start.1 = (f32[1280,128]{1,0:T(8,128)S(1)}, f32[1280,128]{1,0:T(8,128)S(1)}, u32[]{:S(2)}, u32[]{:S(2)}) collective-permute-start(f32[1280,128]{1,0:T(8,128)S(1)} %bitcast.18), channel_id=1, source_target_pairs={{0,1},{1,0},{2,3},{3,2},{4,5},{5,4},{6,7},{7,6},{8,9},{9,8},{10,11... | collective-permute-start | bytes 1966088 | tf_op jit(solution)/shard_map/ppermute | solution.py:166

commit v3 on v2

v3 whole, which is shorter than its diff:
```python
import jax
import jax.numpy as jnp
import numpy as np
from jax import lax
from jax.experimental import pallas as pl
from jax.experimental.pallas import tpu as pltpu
from jax.sharding import Mesh, PartitionSpec as P

SX, SY, SZ = 4, 8, 8
D, RANK = 768, 80
BLOCK = 128
NB = D // BLOCK
UPPER = [(a, b) for a in range(NB) for b in range(a + 1, NB)]
PACKED = len(UPPER) * BLOCK
DIAGS = PACKED + NB // 2 * BLOCK
FLAT = 2560
CHUNK, DEEP = 448, 512


def split(value):
    high = value.astype(jnp.bfloat16)
    rest = value - high.astype(jnp.float32)
    mid = rest.astype(jnp.bfloat16)
    low = (rest - mid.astype(jnp.float32)).astype(jnp.bfloat16)
    return high, mid, low


def halves(value):
    high = value.astype(jnp.bfloat16)
    return high, (value - high.astype(jnp.float32)).astype(jnp.bfloat16)


def dot(left, right, dim=0):
    return lax.dot_general(left, right, (((1,), (dim,)), ((), ())), preferred_element_type=jnp.float32)


def iota(axis):
    return lax.broadcasted_iota(jnp.int32, (BLOCK, BLOCK), axis)


def gram_kernel(x_ref, flat_ref, high_ref, mid_ref, even_ref, odd_ref):
    step = pl.program_id(0)

    @pl.when(step == 0)
    def _():
        for ref in (high_ref, mid_ref):
            ref[CHUNK:, :] = jnp.zeros((DEEP - CHUNK, D), jnp.bfloat16)
        even_ref[...] = jnp.zeros(even_ref.shape, jnp.float32)
        odd_ref[...] = jnp.zeros(odd_ref.shape, jnp.float32)

    high_ref[:CHUNK, :], mid_ref[:CHUNK, :] = halves(x_ref[...])
    slot = 0
    for i in range(3):
        rows = slice(256 * i, 256 * (i + 1))
        high_t = high_ref[:, rows].T
        if i < 2:
            mid_t = mid_ref[:, rows].T
        for j in range(i, 3):
            cols = slice(256 * j, 256 * (j + 1))
            if i == j:
                even_ref[slot] += dot(high_t, high_ref[:, cols])
                odd_ref[i] += dot(high_t, mid_ref[:, cols])
            else:
                even_ref[slot] += (dot(high_t, high_ref[:, cols]) + dot(high_t, mid_ref[:, cols])
                                   + dot(mid_t, high_ref[:, cols]))
            slot += 1

    @pl.when(step == pl.num_programs(0) - 1)
    def _():
        row, col = iota(0), iota(1)
        slot = 0
        diagonals = []
        for i in range(3):
            for j in range(i, 3):
                value = even_ref[slot]
                slot += 1
                if i == j:
                    value = value + (odd_ref[i] + odd_ref[i].T)
                for p in range(2):
                    for q in range(2):
                        a, b = 2 * i + p, 2 * j + q
                        if a < b:
                            at = UPPER.index((a, b)) * BLOCK
                            flat_ref[at:at + BLOCK, :] = value[p * BLOCK:(p + 1) * BLOCK, q * BLOCK:(q + 1) * BLOCK]
                if i == j:
                    first, second = value[:BLOCK, :BLOCK], value[BLOCK:, BLOCK:]
                    at = PACKED + i * BLOCK
                    flat_ref[at:at + BLOCK, :] = jnp.where(row <= col, first, second)
                    diagonals.append(jnp.sum(jnp.where(row == col, second, 0.0), axis=0, keepdims=True))
        flat_ref[DIAGS:, :] = jnp.zeros((FLAT - DIAGS, BLOCK), jnp.float32)
        for i in range(3):
            flat_ref[DIAGS + i:DIAGS + i + 1, :] = diagonals[i]


def inverse_factor(gram, beside):
    groups = RANK // 8
    lane = lax.broadcasted_iota(jnp.int32, (1, RANK), 1)
    sub = lax.broadcasted_iota(jnp.int32, (8, RANK), 0)
    state = [gram[8 * g:8 * g + 8, :] for g in range(groups)]
    scales = []
    for g in range(groups):
        at = 8 * g
        columns = [[jnp.broadcast_to(state[h][:, at + k:at + k + 1], (8, RANK)) for k in range(8)] for h in range(g, groups)]
        head = columns[0]
        own = state[g]
        pivots = jnp.zeros((8, RANK), jnp.float32)
        rows, inverses = [], []
        for k in range(8):
            pivot = head[k][k:k + 1, :]
            inverse = 1.0 / pivot
            inverses.append(inverse)
            pivots = jnp.where(sub == k, pivot, pivots)
            line = jnp.where(lane == at + k, 1.0, own[k:k + 1, :])
            rows.append(line)
            factor = jnp.where(sub > k, head[k] * inverse, 0.0)
            for m in range(k + 1, 8):
                head[m] = head[m] - factor * head[m][k:k + 1, :]
            own = jnp.where((sub > k) & (lane == at + k), 0.0, own) - factor * line
        state[g] = own
        scales.append(lax.rsqrt(pivots))
        rows = [jnp.where((lane > at + k) & (lane < at + 8), 0.0, rows[k]) for k in range(8)]
        inside = (lane >= at) & (lane < at + 8)
        for h in range(g + 1, groups):
            below = columns[h - g]
            value = jnp.where(inside, 0.0, state[h])
            for k in range(8):
                factor = below[k] * inverses[k]
                for m in range(k + 1, 8):
                    below[m] = below[m] - factor * head[m][k:k + 1, :]
                value = value - factor * rows[k]
            state[h] = value
        beside(g)
    result = []
    for g in range(groups):
        value = jnp.where(lane < 8 * g + sub, state[g], jnp.where(lane == 8 * g + sub, 1.0, 0.0))
        result.append(value * scales[g])
    return jnp.concatenate(result, axis=0)


def stack(value):
    return jnp.concatenate(split(value), axis=0)


def times(stacked, parts, dim=0):
    high, mid, low = parts
    n = RANK
    first, second, third = dot(stacked, high, dim), dot(stacked[:2 * n], mid, dim), dot(stacked[:n], low, dim)
    small = first[2 * n:] + second[n:] + third
    return first[:n] + (first[n:2 * n] + second[:n] + small)


def finish_kernel(factor, flat_ref, test_ref, x_hbm, basis_ref, projected_ref, x_ref, c_ref, parts_ref, sem):
    copy = pltpu.make_async_copy(x_hbm, x_ref, sem)
    copy.start()
    row, col = iota(0), iota(1)

    def place(a, b, value):
        for k, part in enumerate(split(value)):
            c_ref[k, a * BLOCK:(a + 1) * BLOCK, b * BLOCK:(b + 1) * BLOCK] = part

    for n, (a, b) in enumerate(UPPER):
        value = flat_ref[n * BLOCK:(n + 1) * BLOCK, :]
        place(a, b, value)
        place(b, a, value.T)
    for i in range(NB // 2):
        value = flat_ref[PACKED + i * BLOCK:PACKED + (i + 1) * BLOCK, :]
        flipped = value.T
        place(2 * i, 2 * i, jnp.where(row <= col, value, flipped))
        other = jnp.where(row > col, value, flipped)
        place(2 * i + 1, 2 * i + 1, jnp.where(row == col, flat_ref[DIAGS + i:DIAGS + i + 1, :], other))

    def part_rows(start, size):
        at = slice(start, start + size)
        parts_ref[0, at, :], parts_ref[1, at, :] = halves(x_ref[at, :])

    covariance = [c_ref.at[k] for k in range(3)]
    test = stack(test_ref[...])
    image = times(test, [part[...] for part in covariance])
    gram = times(test, split(image), 1)
    copy.wait()
    first = inverse_factor(gram, lambda g: part_rows(128 * g, 128))
    spanned = times(stack(first), split(image))
    spanned_stack = stack(spanned)
    reach = times(spanned_stack, [part[...] for part in covariance])
    gram = times(spanned_stack, split(reach), 1)
    done = 128 * (RANK // 8)
    second = inverse_factor(gram, lambda g: part_rows(done, x_ref.shape[0] - done) if g == 0 else None)
    second_stack = stack(second)
    projected_ref[...] = times(second_stack, split(reach)) * (1.0 / factor)
    weight = jnp.concatenate(halves(times(second_stack, split(spanned)) * factor), axis=0)
    main, rest = dot(weight, parts_ref[0], 1), dot(weight, parts_ref[1], 1)
    basis_ref[...] = main[:RANK] + (main[RANK:] + rest[:RANK] + rest[RANK:])


def tree(parts):
    while len(parts) > 1:
        parts = [parts[i] + parts[i + 1] for i in range(0, len(parts), 2)]
    return parts[0]


def everyone(value, axis, size):
    return lax.all_to_all(jnp.broadcast_to(value, (size,) + value.shape), axis, 0, 0)


def pick(array, i):
    return lax.dynamic_index_in_dim(array, i, 0, keepdims=False)


def stacked_sum(values):
    return tree([values[i] for i in range(values.shape[0])])


def total(flat):
    core = lax.axis_index("core")
    swap = [(0, 1), (1, 0)]
    pair = flat.reshape(2, FLAT // 2, BLOCK)
    value = pick(pair, core) + lax.ppermute(pick(pair, 1 - core), "core", swap)
    value = stacked_sum(lax.all_to_all(value.reshape(SX, -1, BLOCK), "x", 0, 0))
    value = stacked_sum(lax.all_to_all(value.reshape(SY, -1, BLOCK), "y", 0, 0))
    value = stacked_sum(everyone(value, "z", SZ))
    value = everyone(value, "y", SY).reshape(-1, BLOCK)
    value = everyone(value, "x", SX).reshape(-1, BLOCK)
    other = lax.ppermute(value, "core", swap)
    low = jnp.where(core == 0, value, other)
    high = jnp.where(core == 0, other, value)
    return jnp.concatenate([low, high])


def local(embeddings, test_matrix):
    rows = embeddings.shape[0]
    factor = float(np.sqrt(np.float32(rows * 2 * SX * SY * SZ)))
    flat = pl.pallas_call(
        gram_kernel,
        grid=(rows // CHUNK,),
        in_specs=[pl.BlockSpec((CHUNK, D), lambda i: (i, 0))],
        out_specs=pl.BlockSpec((FLAT, BLOCK), lambda i: (0, 0)),
        out_shape=jax.ShapeDtypeStruct((FLAT, BLOCK), jnp.float32),
        scratch_shapes=[pltpu.VMEM((DEEP, D), jnp.bfloat16)] * 2
        + [pltpu.VMEM((6, 256, 256), jnp.float32), pltpu.VMEM((3, 256, 256), jnp.float32)],
        compiler_params=pltpu.CompilerParams(vmem_limit_bytes=60 * 2 ** 20),
        cost_estimate=pl.CostEstimate(flops=2 * rows * D * D * 2, bytes_accessed=4 * rows * D, transcendentals=0),
    )(embeddings)
    flat = total(flat)
    basis, projected = pl.pallas_call(
        lambda *refs: finish_kernel(factor, *refs),
        in_specs=[pl.BlockSpec(memory_space=pltpu.VMEM)] * 2 + [pl.BlockSpec(memory_space=pl.ANY)],
        out_specs=[pl.BlockSpec(memory_space=pltpu.VMEM)] * 2,
        out_shape=[jax.ShapeDtypeStruct((RANK, rows), jnp.float32), jax.ShapeDtypeStruct((RANK, D), jnp.float32)],
        scratch_shapes=[
            pltpu.VMEM((rows, D), jnp.float32),
            pltpu.VMEM((3, D, D), jnp.bfloat16),
            pltpu.VMEM((2, rows, D), jnp.bfloat16),
            pltpu.SemaphoreType.DMA,
        ],
        compiler_params=pltpu.CompilerParams(vmem_limit_bytes=48 * 2 ** 20),
        cost_estimate=pl.CostEstimate(flops=2 * rows * D * RANK * 8, bytes_accessed=4 * rows * D, transcendentals=0),
    )(flat, test_matrix.T, embeddings)
    return basis.T, projected


def solution(mesh):
    grid = Mesh(mesh.devices.reshape(SX, SY, SZ, 2), ("x", "y", "z", "core"))
    in_specs = (P(("x", "y", "z", "core"), None), P())
    out_specs = (P(("x", "y", "z", "core"), None), P())
    return jax.shard_map(local, mesh=grid, in_specs=in_specs, out_specs=out_specs, check_vma=False)
```

time: 130 us -> 106 us (0.82)
  Pallas kernels: 41.6 us -> 18 us
    pallas_call x1, Pallas kernels: 27.1 us -> 11.3 us  [local(): pl.pallas_call(lambda *refs: finish_kernel(factor, *refs), in_specs=[pl.B...]
    pallas_call x1, Pallas kernels: 14.5 us -> 6.68 us  [local(): pl.pallas_call(gram_kernel, grid=(rows // CHUNK,), in_specs=[pl.BlockSpec...]
where the time goes in v3:
time: 106 us
  blocking collectives  62.4 us (59%)
  Pallas kernels  18 us (17%)
  starting transfers between devices  17.4 us (16%)
  waiting for transfers between devices  3.4 us (3%)
  local copies, waits for them, and re-layouts  3.31 us (3%)
    all_to_all x3, blocking collectives, everyone(): lax.all_to_all(jnp.broadcast_to(value, (size,) + value.shape), axis, 0, 0)  38.6 us
    all_to_all x1, blocking collectives, total(): value = stacked_sum(lax.all_to_all(value.reshape(SX, -1, BLOCK), 'x', 0, 0))  13 us
    pallas_call x1, Pallas kernels, local(): pl.pallas_call(lambda *refs: finish_kernel(factor, *refs), in_specs=[pl.B...  11.3 us
    all_to_all x1, blocking collectives, total(): value = stacked_sum(lax.all_to_all(value.reshape(SY, -1, BLOCK), 'y', 0, 0))  10.8 us
    ppermute x1, starting transfers between devices, total(): value = pick(pair, core) + lax.ppermute(pick(pair, 1 - core), 'core', swap)  8.78 us
    ppermute x1, starting transfers between devices, total(): other = lax.ppermute(value, 'core', swap)  8.66 us
    pallas_call x1, Pallas kernels, local(): pl.pallas_call(gram_kernel, grid=(rows // CHUNK,), in_specs=[pl.BlockSpec...  6.68 us
  transfers between devices with their start and end apart: 2, of which 2 were waited for; matrix products, arithmetic and copies ran while one was open for 0% of the time, Pallas kernels for 0%

profile of v3, /device:TPU:1, one launch (start us, length us, event | category | flops | bytes accessed | tf_op | source)
XLA Modules:
  0.0 105.6 jit_solution(11050356082843721294)
XLA Ops:
  0.6 6.7 %shard_map.41 = f32[2560,128]{1,0:T(8,128)} custom-call(f32[1344,768]{1,0:T(8,128)} %refs_2_.1), custom_call_target="tpu_custom_call" | custom-call | flops 3170893824 | bytes 4128768 | tf_op jit(solution)/shard_map/pallas_call | solution.py:232
  7.3 0.0 copy-start.2
  7.3 1.2 %dynamic-slice_bitcast_fusion = f32[1280,128]{1,0:T(8,128)S(1)} fusion(f32[2,1280,128]{2,1,0:T(8,128)} %bitcast.20, s32[]{:T(128)S(6)} %select_n.21), kind=kLoop, calls=%fused_computation.2 | loop fusion | bytes 1310724 | tf_op jit(solution)/shard_map/jit(dynamic_index_in_dim)/squeeze | solution.py:206
  8.6 8.8 %collective-permute-start = (f32[1280,128]{1,0:T(8,128)S(1)}, f32[1280,128]{1,0:T(8,128)S(1)}, u32[]{:S(2)}, u32[]{:S(2)}) collective-permute-start(f32[1280,128]{1,0:T(8,128)S(1)} %dynamic-slice_bitcast_fusion), channel_id=1, source_target_pairs={{0,1},{1,0},{2,3},{3,2},{4,5},{5,4},{6,7},{7,6},{8,9},{9,8},{10,11... | collective-permute-start | bytes 1966088 | tf_op jit(solution)/shard_map/ppermute | solution.py:217
  17.3 1.7 %collective-permute-done = f32[1280,128]{1,0:T(8,128)S(1)} collective-permute-done((f32[1280,128]{1,0:T(8,128)S(1)}, f32[1280,128]{1,0:T(8,128)S(1)}, u32[]{:S(2)}, u32[]{:S(2)}) %collective-permute-start) | collective-permute-done | bytes 655392 | tf_op jit(solution)/shard_map/ppermute | solution.py:217
  19.0 0.0 copy-done.2
  19.0 0.1 bitcast_add_fusion
  19.1 13.0 %all_to_all.25 = f32[4,320,128]{2,1,0:T(8,128)S(1)} all-to-all(f32[4,320,128]{2,1,0:T(8,128)S(1)} %bitcast.18), channel_id=1, replica_groups=mesh['x'=4,'y'=8,'z'=8,'core'=2] {'x'}, dimensions={0} | all-to-all | bytes 1310720 | tf_op jit(solution)/shard_map/all_to_all | solution.py:218
  32.2 10.8 %all_to_all.26 = f32[8,40,128]{2,1,0:T(8,128)S(1)} all-to-all(f32[8,40,128]{2,1,0:T(8,128)S(1)} %bitcast.22), channel_id=1, replica_groups=mesh['x'=4,'y'=8,'z'=8,'core'=2] {'y'}, dimensions={0} | all-to-all | bytes 327680 | tf_op jit(solution)/shard_map/all_to_all | solution.py:219
  43.0 17.9 %all_to_all.27 = f32[8,40,128]{2,1,0:T(8,128)S(1)} all-to-all(f32[8,40,128]{2,1,0:T(8,128)S(1)} %broadcast_in_dim.9), channel_id=1, replica_groups=mesh['x'=4,'y'=8,'z'=8,'core'=2] {'z'}, dimensions={0} | all-to-all | bytes 327680 | tf_op jit(solution)/shard_map/all_to_all | solution.py:202
  60.9 10.7 %all_to_all.28 = f32[8,40,128]{2,1,0:T(8,128)S(1)} all-to-all(f32[8,40,128]{2,1,0:T(8,128)S(1)} %broadcast_in_dim.10), channel_id=1, replica_groups=mesh['x'=4,'y'=8,'z'=8,'core'=2] {'y'}, dimensions={0} | all-to-all | bytes 327680 | tf_op jit(solution)/shard_map/all_to_all | solution.py:202
  71.6 10.0 %all_to_all.29 = f32[4,320,128]{2,1,0:T(8,128)S(1)} all-to-all(f32[4,320,128]{2,1,0:T(8,128)S(1)} %broadcast_in_dim.11), channel_id=1, replica_groups=mesh['x'=4,'y'=8,'z'=8,'core'=2] {'x'}, dimensions={0} | all-to-all | bytes 1310720 | tf_op jit(solution)/shard_map/all_to_all | solution.py:202
  81.7 8.7 %collective-permute-start.1 = (f32[1280,128]{1,0:T(8,128)S(1)}, f32[1280,128]{1,0:T(8,128)S(1)}, u32[]{:S(2)}, u32[]{:S(2)}) collective-permute-start(f32[1280,128]{1,0:T(8,128)S(1)} %bitcast.19), channel_id=1, source_target_pairs={{0,1},{1,0},{2,3},{3,2},{4,5},{5,4},{6,7},{7,6},{8,9},{9,8},{10,11... | collective-permute-start | bytes 1966088 | tf_op jit(solution)/shard_map/ppermute | solution.py:223
  90.3 1.7 %collective-permute-done.1 = f32[1280,128]{1,0:T(8,128)S(1)} collective-permute-done((f32[1280,128]{1,0:T(8,128)S(1)}, f32[1280,128]{1,0:T(8,128)S(1)}, u32[]{:S(2)}, u32[]{:S(2)}) %collective-permute-start.1) | collective-permute-done | bytes 655392 | tf_op jit(solution)/shard_map/ppermute | solution.py:223
  92.0 0.0 copy-start
  92.0 0.1 broadcast_select_fusion.1
  92.1 0.0 copy-start.1
  92.1 0.1 pad_maximum_fusion.refs_0_
  92.2 2.0 %copy-done = f32[1344,768]{1,0:T(8,128)S(1)} copy-done((f32[1344,768]{1,0:T(8,128)S(1)}, f32[1344,768]{1,0:T(8,128)}, u32[]{:S(2)}) %copy-start) | copy-done | bytes 4128792
  94.2 0.0 copy-done.1
  94.2 11.3 %shard_map.42 = (f32[80,1344]{1,0:T(8,128)}, f32[80,768]{1,0:T(8,128)}) custom-call(f32[2560,128]{1,0:T(8,128)S(1)} %pad_maximum_fusion.refs_0_, f32[80,768]{1,0:T(8,128)S(1)} %bitcast.17, f32[1344,768]{1,0:T(8,128)S(1)} %copy-done), custom_call_target="tpu_custom_call" | custom-call | flops 1321205760 | bytes 4128768 | tf_op jit(solution)/shard_map/pallas_call | solution.py:244
  (6 shorter events, 0.1 us)
Async XLA Ops:
  7.3 11.7 %copy-start.2 = (f32[2560,128]{1,0:T(8,128)S(1)}, f32[2560,128]{1,0:T(8,128)}, u32[]{:S(2)}) copy-start(f32[2560,128]{1,0:T(8,128)} %shard_map.41) | copy-start | bytes 3932164
  8.6 10.5 %collective-permute-start = (f32[1280,128]{1,0:T(8,128)S(1)}, f32[1280,128]{1,0:T(8,128)S(1)}, u32[]{:S(2)}, u32[]{:S(2)}) collective-permute-start(f32[1280,128]{1,0:T(8,128)S(1)} %dynamic-slice_bitcast_fusion), channel_id=1, source_target_pairs={{0,1},{1,0},{2,3},{3,2},{4,5},{5,4},{6,7},{7,6},{8,9},{9,8},{10,11... | collective-permute-start | bytes 1966088 | tf_op jit(solution)/shard_map/ppermute | solution.py:217
  81.7 10.4 %collective-permute-start.1 = (f32[1280,128]{1,0:T(8,128)S(1)}, f32[1280,128]{1,0:T(8,128)S(1)}, u32[]{:S(2)}, u32[]{:S(2)}) collective-permute-start(f32[1280,128]{1,0:T(8,128)S(1)} %bitcast.19), channel_id=1, source_target_pairs={{0,1},{1,0},{2,3},{3,2},{4,5},{5,4},{6,7},{7,6},{8,9},{9,8},{10,11... | collective-permute-start | bytes 1966088 | tf_op jit(solution)/shard_map/ppermute | solution.py:223
  92.0 2.2 %copy-start = (f32[1344,768]{1,0:T(8,128)S(1)}, f32[1344,768]{1,0:T(8,128)}, u32[]{:S(2)}) copy-start(f32[1344,768]{1,0:T(8,128)} %refs_2_.1) | copy-start | bytes 12386308
  92.1 2.1 %copy-start.1 = (f32[768,80]{0,1:T(8,128)S(1)}, f32[768,80]{0,1:T(8,128)}, u32[]{:S(2)}) copy-start(f32[768,80]{0,1:T(8,128)} %param.3) | copy-start | bytes 737284

commit v4 on v3

--- a/solution.py
+++ b/solution.py
@@ -14,7 +14,7 @@
 PACKED = len(UPPER) * BLOCK
 DIAGS = PACKED + NB // 2 * BLOCK
 FLAT = 2560
-CHUNK, DEEP = 448, 512
+CHUNKS = ((0, 512), (512, 512), (1024, 320))
 
 
 def split(value):
@@ -38,95 +38,90 @@
     return lax.broadcasted_iota(jnp.int32, (BLOCK, BLOCK), axis)
 
 
-def gram_kernel(x_ref, flat_ref, high_ref, mid_ref, even_ref, odd_ref):
-    step = pl.program_id(0)
-
-    @pl.when(step == 0)
-    def _():
-        for ref in (high_ref, mid_ref):
-            ref[CHUNK:, :] = jnp.zeros((DEEP - CHUNK, D), jnp.bfloat16)
-        even_ref[...] = jnp.zeros(even_ref.shape, jnp.float32)
-        odd_ref[...] = jnp.zeros(odd_ref.shape, jnp.float32)
-
-    high_ref[:CHUNK, :], mid_ref[:CHUNK, :] = halves(x_ref[...])
-    slot = 0
+def gram_kernel(x_hbm, flat_ref, x_ref, high_ref, mid_ref, even_ref, odd_ref, sem):
+    copies = []
+    for n, (start, size) in enumerate(CHUNKS):
+        at = pl.ds(start, size)
+        copies.append(pltpu.make_async_copy(x_hbm.at[at, :], x_ref.at[at, :], sem.at[n]))
+        copies[-1].start()
+    used = x_ref.shape[0]
+    for ref in (high_ref, mid_ref):
+        ref[used:, :] = jnp.zeros((ref.shape[0] - used, D), jnp.bfloat16)
+
+    def products(n):
+        start, size = CHUNKS[n]
+        deep = slice(start, start + (size + 127) // 128 * 128)
+        for i in range(3):
+            high_t = high_ref[deep, 256 * i:256 * (i + 1)].T
+            for j in range(3):
+                cols = slice(256 * j, 256 * (j + 1))
+                if i <= j:
+                    value = dot(high_t, high_ref[deep, cols])
+                    even_ref[3 * i + j] = value if n == 0 else even_ref[3 * i + j] + value
+                value = dot(high_t, mid_ref[deep, cols])
+                odd_ref[3 * i + j] = value if n == 0 else odd_ref[3 * i + j] + value
+
+    for n, (start, size) in enumerate(CHUNKS):
+        copies[n].wait()
+        at = slice(start, start + size)
+        high_ref[at, :], mid_ref[at, :] = halves(x_ref[at, :])
+        if n:
+            products(n - 1)
+    products(len(CHUNKS) - 1)
+
+    row, col = iota(0), iota(1)
+    flat_ref[DIAGS:, :] = jnp.zeros((FLAT - DIAGS, BLOCK), jnp.float32)
     for i in range(3):
-        rows = slice(256 * i, 256 * (i + 1))
-        high_t = high_ref[:, rows].T
-        if i < 2:
-            mid_t = mid_ref[:, rows].T
         for j in range(i, 3):
-            cols = slice(256 * j, 256 * (j + 1))
+            value = even_ref[3 * i + j] + (odd_ref[3 * i + j] + odd_ref[3 * j + i].T)
+            for p in range(2):
+                for q in range(2):
+                    a, b = 2 * i + p, 2 * j + q
+                    if a < b:
+                        at = UPPER.index((a, b)) * BLOCK
+                        flat_ref[at:at + BLOCK, :] = value[p * BLOCK:(p + 1) * BLOCK, q * BLOCK:(q + 1) * BLOCK]
             if i == j:
-                even_ref[slot] += dot(high_t, high_ref[:, cols])
-                odd_ref[i] += dot(high_t, mid_ref[:, cols])
-            else:
-                even_ref[slot] += (dot(high_t, high_ref[:, cols]) + dot(high_t, mid_ref[:, cols])
-                                   + dot(mid_t, high_ref[:, cols]))
-            slot += 1
-
-    @pl.when(step == pl.num_programs(0) - 1)
-    def _():
-        row, col = iota(0), iota(1)
-        slot = 0
-        diagonals = []
-        for i in range(3):
-            for j in range(i, 3):
-                value = even_ref[slot]
-                slot += 1
-                if i == j:
-                    value = value + (odd_ref[i] + odd_ref[i].T)
-                for p in range(2):
-                    for q in range(2):
-                        a, b = 2 * i + p, 2 * j + q
-                        if a < b:
-                            at = UPPER.index((a, b)) * BLOCK
-                            flat_ref[at:at + BLOCK, :] = value[p * BLOCK:(p + 1) * BLOCK, q * BLOCK:(q + 1) * BLOCK]
-                if i == j:
-                    first, second = value[:BLOCK, :BLOCK], value[BLOCK:, BLOCK:]
-                    at = PACKED + i * BLOCK
-                    flat_ref[at:at + BLOCK, :] = jnp.where(row <= col, first, second)
-                    diagonals.append(jnp.sum(jnp.where(row == col, second, 0.0), axis=0, keepdims=True))
-        flat_ref[DIAGS:, :] = jnp.zeros((FLAT - DIAGS, BLOCK), jnp.float32)
-        for i in range(3):
-            flat_ref[DIAGS + i:DIAGS + i + 1, :] = diagonals[i]
+                first, second = value[:BLOCK, :BLOCK], value[BLOCK:, BLOCK:]
+                at = PACKED + i * BLOCK
+                flat_ref[at:at + BLOCK, :] = jnp.where(row <= col, first, second)
+                flat_ref[DIAGS + i:DIAGS + i + 1, :] = jnp.sum(jnp.where(row == col, second, 0.0), axis=0, keepdims=True)
 
 
 def inverse_factor(gram, beside):
-    groups = RANK // 8
-    lane = lax.broadcasted_iota(jnp.int32, (1, RANK), 1)
-    sub = lax.broadcasted_iota(jnp.int32, (8, RANK), 0)
+    groups, shape = RANK // 8, (8, RANK)
+    lane = lax.broadcasted_iota(jnp.int32, shape, 1)
+    sub = lax.broadcasted_iota(jnp.int32, shape, 0)
     state = [gram[8 * g:8 * g + 8, :] for g in range(groups)]
     scales = []
     for g in range(groups):
         at = 8 * g
-        columns = [[jnp.broadcast_to(state[h][:, at + k:at + k + 1], (8, RANK)) for k in range(8)] for h in range(g, groups)]
-        head = columns[0]
-        own = state[g]
-        pivots = jnp.zeros((8, RANK), jnp.float32)
-        rows, inverses = [], []
+        spread = [[jnp.broadcast_to(state[h][:, at + k:at + k + 1], shape) for k in range(8)] for h in range(g, groups)]
+        block = [[jnp.broadcast_to(spread[0][j][i:i + 1, :], shape) if i <= j else None for j in range(8)] for i in range(8)]
+        lines = [jnp.broadcast_to(state[g][k:k + 1, :], shape) for k in range(8)]
+        own, pivots, inverses, rows = state[g], block[0][0], [], []
         for k in range(8):
-            pivot = head[k][k:k + 1, :]
-            inverse = 1.0 / pivot
+            inverse = 1.0 / block[k][k]
             inverses.append(inverse)
-            pivots = jnp.where(sub == k, pivot, pivots)
-            line = jnp.where(lane == at + k, 1.0, own[k:k + 1, :])
-            rows.append(line)
-            factor = jnp.where(sub > k, head[k] * inverse, 0.0)
+            unit = jnp.where(lane == at + k, 1.0, lines[k])
+            rows.append(jnp.where((lane > at + k) & (lane < at + 8), 0.0, unit))
             for m in range(k + 1, 8):
-                head[m] = head[m] - factor * head[m][k:k + 1, :]
-            own = jnp.where((sub > k) & (lane == at + k), 0.0, own) - factor * line
+                factor = block[k][m] * inverse
+                for n in range(m, 8):
+                    block[m][n] = block[m][n] - factor * block[k][n]
+                lines[m] = jnp.where(lane == at + k, 0.0, lines[m]) - factor * unit
+            if k:
+                own = jnp.where(sub == k, lines[k], own)
+                pivots = jnp.where(sub == k, block[k][k], pivots)
         state[g] = own
         scales.append(lax.rsqrt(pivots))
-        rows = [jnp.where((lane > at + k) & (lane < at + 8), 0.0, rows[k]) for k in range(8)]
         inside = (lane >= at) & (lane < at + 8)
         for h in range(g + 1, groups):
-            below = columns[h - g]
+            below = spread[h - g]
             value = jnp.where(inside, 0.0, state[h])
             for k in range(8):
                 factor = below[k] * inverses[k]
                 for m in range(k + 1, 8):
-                    below[m] = below[m] - factor * head[m][k:k + 1, :]
+                    below[m] = below[m] - factor * block[k][m]
                 value = value - factor * rows[k]
             state[h] = value
         beside(g)
@@ -231,13 +226,14 @@
     factor = float(np.sqrt(np.float32(rows * 2 * SX * SY * SZ)))
     flat = pl.pallas_call(
         gram_kernel,
-        grid=(rows // CHUNK,),
-        in_specs=[pl.BlockSpec((CHUNK, D), lambda i: (i, 0))],
-        out_specs=pl.BlockSpec((FLAT, BLOCK), lambda i: (0, 0)),
+        in_specs=[pl.BlockSpec(memory_space=pl.ANY)],
+        out_specs=pl.BlockSpec(memory_space=pltpu.VMEM),
         out_shape=jax.ShapeDtypeStruct((FLAT, BLOCK), jnp.float32),
-        scratch_shapes=[pltpu.VMEM((DEEP, D), jnp.bfloat16)] * 2
-        + [pltpu.VMEM((6, 256, 256), jnp.float32), pltpu.VMEM((3, 256, 256), jnp.float32)],
-        compiler_params=pltpu.CompilerParams(vmem_limit_bytes=60 * 2 ** 20),
+        scratch_shapes=[pltpu.VMEM((rows, D), jnp.float32)]
+        + [pltpu.VMEM((CHUNKS[-1][0] + 512, D), jnp.bfloat16)] * 2
+        + [pltpu.VMEM((9, 256, 256), jnp.float32)] * 2
+        + [pltpu.SemaphoreType.DMA((len(CHUNKS),))],
+        compiler_params=pltpu.CompilerParams(vmem_limit_bytes=50 * 2 ** 20),
         cost_estimate=pl.CostEstimate(flops=2 * rows * D * D * 2, bytes_accessed=4 * rows * D, transcendentals=0),
     )(embeddings)
     flat = total(flat)
@@ -252,7 +248,7 @@
             pltpu.VMEM((2, rows, D), jnp.bfloat16),
             pltpu.SemaphoreType.DMA,
         ],
-        compiler_params=pltpu.CompilerParams(vmem_limit_bytes=48 * 2 ** 20),
+        compiler_params=pltpu.CompilerParams(vmem_limit_bytes=50 * 2 ** 20),
         cost_estimate=pl.CostEstimate(flops=2 * rows * D * RANK * 8, bytes_accessed=4 * rows * D, transcendentals=0),
     )(flat, test_matrix.T, embeddings)
     return basis.T, projected

time: 106 us -> 104 us (0.981)
  local copies, waits for them, and re-layouts: 3.31 us -> 0.97 us
    squeeze x1, local copies, waits for them, and re-layouts: 1.23 us -> 0.05 us  [pick(): return lax.dynamic_index_in_dim(array, i, 0, keepdims=False)]
    unnamed x6 -> x2, local copies, waits for them, and re-layouts: 2 us -> 0.84 us
where the time goes in v4:
time: 104 us
  blocking collectives  62.4 us (60%)
  Pallas kernels  18.1 us (17%)
  starting transfers between devices  17.6 us (17%)
  waiting for transfers between devices  3.22 us (3%)
    all_to_all x3, blocking collectives, everyone(): lax.all_to_all(jnp.broadcast_to(value, (size,) + value.shape), axis, 0, 0)  38.6 us
    all_to_all x1, blocking collectives, total(): value = stacked_sum(lax.all_to_all(value.reshape(SX, -1, BLOCK), 'x', 0, 0))  13 us
    pallas_call x1, Pallas kernels, local(): pl.pallas_call(lambda *refs: finish_kernel(factor, *refs), in_specs=[pl.B...  12.2 us
    all_to_all x1, blocking collectives, total(): value = stacked_sum(lax.all_to_all(value.reshape(SY, -1, BLOCK), 'y', 0, 0))  10.8 us
    ppermute x1, starting transfers between devices, total(): other = lax.ppermute(value, 'core', swap)  8.84 us
    ppermute x1, starting transfers between devices, total(): value = pick(pair, core) + lax.ppermute(pick(pair, 1 - core), 'core', swap)  8.78 us
    pallas_call x1, Pallas kernels, local(): pl.pallas_call(gram_kernel, in_specs=[pl.BlockSpec(memory_space=pl.ANY)],...  5.89 us
  transfers between devices with their start and end apart: 2, of which 2 were waited for; matrix products, arithmetic and copies ran while one was open for 0% of the time, Pallas kernels for 0%

profile of v4, /device:TPU:1, one launch (start us, length us, event | category | flops | bytes accessed | tf_op | source)
XLA Modules:
  0.0 103.5 jit_solution(8814901581120110842)
XLA Ops:
  0.6 5.9 %shard_map.41 = f32[2560,128]{1,0:T(8,128)S(1)} custom-call(f32[1344,768]{1,0:T(8,128)} %refs_2_.1), custom_call_target="tpu_custom_call" | custom-call | flops 3170893824 | bytes 4128768 | tf_op jit(solution)/shard_map/pallas_call | solution.py:227
  6.5 0.1 dynamic-slice_bitcast_fusion
  6.6 8.8 %collective-permute-start = (f32[1280,128]{1,0:T(8,128)S(1)}, f32[1280,128]{1,0:T(8,128)S(1)}, u32[]{:S(2)}, u32[]{:S(2)}) collective-permute-start(f32[1280,128]{1,0:T(8,128)S(1)} %dynamic-slice_bitcast_fusion), channel_id=1, source_target_pairs={{0,1},{1,0},{2,3},{3,2},{4,5},{5,4},{6,7},{7,6},{8,9},{9,8},{10,11... | collective-permute-start | bytes 1966088 | tf_op jit(solution)/shard_map/ppermute | solution.py:212
  15.4 1.7 %collective-permute-done = f32[1280,128]{1,0:T(8,128)S(1)} collective-permute-done((f32[1280,128]{1,0:T(8,128)S(1)}, f32[1280,128]{1,0:T(8,128)S(1)}, u32[]{:S(2)}, u32[]{:S(2)}) %collective-permute-start) | collective-permute-done | bytes 655392 | tf_op jit(solution)/shard_map/ppermute | solution.py:212
  17.1 0.1 bitcast_add_fusion
  17.2 13.0 %all_to_all.25 = f32[4,320,128]{2,1,0:T(8,128)S(1)} all-to-all(f32[4,320,128]{2,1,0:T(8,128)S(1)} %bitcast.20), channel_id=1, replica_groups=mesh['x'=4,'y'=8,'z'=8,'core'=2] {'x'}, dimensions={0} | all-to-all | bytes 1310720 | tf_op jit(solution)/shard_map/all_to_all | solution.py:213
  30.2 10.8 %all_to_all.26 = f32[8,40,128]{2,1,0:T(8,128)S(1)} all-to-all(f32[8,40,128]{2,1,0:T(8,128)S(1)} %bitcast.22), channel_id=1, replica_groups=mesh['x'=4,'y'=8,'z'=8,'core'=2] {'y'}, dimensions={0} | all-to-all | bytes 327680 | tf_op jit(solution)/shard_map/all_to_all | solution.py:214
  41.0 17.9 %all_to_all.27 = f32[8,40,128]{2,1,0:T(8,128)S(1)} all-to-all(f32[8,40,128]{2,1,0:T(8,128)S(1)} %broadcast_in_dim.9), channel_id=1, replica_groups=mesh['x'=4,'y'=8,'z'=8,'core'=2] {'z'}, dimensions={0} | all-to-all | bytes 327680 | tf_op jit(solution)/shard_map/all_to_all | solution.py:197
  59.0 10.7 %all_to_all.28 = f32[8,40,128]{2,1,0:T(8,128)S(1)} all-to-all(f32[8,40,128]{2,1,0:T(8,128)S(1)} %broadcast_in_dim.10), channel_id=1, replica_groups=mesh['x'=4,'y'=8,'z'=8,'core'=2] {'y'}, dimensions={0} | all-to-all | bytes 327680 | tf_op jit(solution)/shard_map/all_to_all | solution.py:197
  69.7 10.0 %all_to_all.29 = f32[4,320,128]{2,1,0:T(8,128)S(1)} all-to-all(f32[4,320,128]{2,1,0:T(8,128)S(1)} %broadcast_in_dim.11), channel_id=1, replica_groups=mesh['x'=4,'y'=8,'z'=8,'core'=2] {'x'}, dimensions={0} | all-to-all | bytes 1310720 | tf_op jit(solution)/shard_map/all_to_all | solution.py:197
  79.7 8.8 %collective-permute-start.1 = (f32[1280,128]{1,0:T(8,128)S(1)}, f32[1280,128]{1,0:T(8,128)S(1)}, u32[]{:S(2)}, u32[]{:S(2)}) collective-permute-start(f32[1280,128]{1,0:T(8,128)S(1)} %bitcast.21), channel_id=1, source_target_pairs={{0,1},{1,0},{2,3},{3,2},{4,5},{5,4},{6,7},{7,6},{8,9},{9,8},{10,11... | collective-permute-start | bytes 1966088 | tf_op jit(solution)/shard_map/ppermute | solution.py:218
  88.6 1.5 %collective-permute-done.1 = f32[1280,128]{1,0:T(8,128)S(1)} collective-permute-done((f32[1280,128]{1,0:T(8,128)S(1)}, f32[1280,128]{1,0:T(8,128)S(1)}, u32[]{:S(2)}, u32[]{:S(2)}) %collective-permute-start.1) | collective-permute-done | bytes 655392 | tf_op jit(solution)/shard_map/ppermute | solution.py:218
  90.1 0.1 broadcast_select_fusion.1
  90.2 0.0 copy-start
  90.2 0.1 pad_maximum_fusion.refs_0_
  90.3 0.8 copy-done
  91.1 12.2 %shard_map.42 = (f32[80,1344]{1,0:T(8,128)}, f32[80,768]{1,0:T(8,128)}) custom-call(f32[2560,128]{1,0:T(8,128)S(1)} %pad_maximum_fusion.refs_0_, f32[80,768]{1,0:T(8,128)S(1)} %bitcast.19, f32[1344,768]{1,0:T(8,128)} %refs_2_.1), custom_call_target="tpu_custom_call" | custom-call | flops 1321205760 | bytes 4128768 | tf_op jit(solution)/shard_map/pallas_call | solution.py:240
  (6 shorter events, 0.1 us)
Async XLA Ops:
  6.6 10.5 %collective-permute-start = (f32[1280,128]{1,0:T(8,128)S(1)}, f32[1280,128]{1,0:T(8,128)S(1)}, u32[]{:S(2)}, u32[]{:S(2)}) collective-permute-start(f32[1280,128]{1,0:T(8,128)S(1)} %dynamic-slice_bitcast_fusion), channel_id=1, source_target_pairs={{0,1},{1,0},{2,3},{3,2},{4,5},{5,4},{6,7},{7,6},{8,9},{9,8},{10,11... | collective-permute-start | bytes 1966088 | tf_op jit(solution)/shard_map/ppermute | solution.py:212
  79.7 10.4 %collective-permute-start.1 = (f32[1280,128]{1,0:T(8,128)S(1)}, f32[1280,128]{1,0:T(8,128)S(1)}, u32[]{:S(2)}, u32[]{:S(2)}) collective-permute-start(f32[1280,128]{1,0:T(8,128)S(1)} %bitcast.21), channel_id=1, source_target_pairs={{0,1},{1,0},{2,3},{3,2},{4,5},{5,4},{6,7},{7,6},{8,9},{9,8},{10,11... | collective-permute-start | bytes 1966088 | tf_op jit(solution)/shard_map/ppermute | solution.py:218
  90.2 0.9 copy-start

commit v5 on v4

--- a/solution.py
+++ b/solution.py
@@ -92,43 +92,57 @@
     lane = lax.broadcasted_iota(jnp.int32, shape, 1)
     sub = lax.broadcasted_iota(jnp.int32, shape, 0)
     state = [gram[8 * g:8 * g + 8, :] for g in range(groups)]
+    diagonal = [jnp.where(lane == 8 * g + sub, state[g], 0.0) for g in range(groups)]
+    along = lax.rsqrt(jnp.sum(sum(diagonal[1:], diagonal[0]), axis=0, keepdims=True))
+    state = [state[g] * lax.rsqrt(jnp.sum(diagonal[g], axis=1, keepdims=True)) * along for g in range(groups)]
+
+    def column(h, j):
+        return jnp.broadcast_to(state[h][:, j:j + 1], shape)
+
     scales = []
     for g in range(groups):
         at = 8 * g
-        spread = [[jnp.broadcast_to(state[h][:, at + k:at + k + 1], shape) for k in range(8)] for h in range(g, groups)]
-        block = [[jnp.broadcast_to(spread[0][j][i:i + 1, :], shape) if i <= j else None for j in range(8)] for i in range(8)]
-        lines = [jnp.broadcast_to(state[g][k:k + 1, :], shape) for k in range(8)]
-        own, pivots, inverses, rows = state[g], block[0][0], [], []
-        for k in range(8):
-            inverse = 1.0 / block[k][k]
-            inverses.append(inverse)
-            unit = jnp.where(lane == at + k, 1.0, lines[k])
-            rows.append(jnp.where((lane > at + k) & (lane < at + 8), 0.0, unit))
-            for m in range(k + 1, 8):
-                factor = block[k][m] * inverse
-                for n in range(m, 8):
-                    block[m][n] = block[m][n] - factor * block[k][n]
-                lines[m] = jnp.where(lane == at + k, 0.0, lines[m]) - factor * unit
-            if k:
-                own = jnp.where(sub == k, lines[k], own)
-                pivots = jnp.where(sub == k, block[k][k], pivots)
+        head = [column(g, at + k) for k in range(8)]
+        own, pivots, steps = state[g], None, []
+        for k in range(0, 8, 2):
+            u, v = head[k], head[k + 1]
+            a, b, c = u[k:k + 1, :], v[k:k + 1, :], v[k + 1:k + 2, :]
+            inverse = 1.0 / (a * c - b * b)
+            rest = sub > k + 1
+            first = jnp.where(rest, u * c - v * b, 0.0) * inverse
+            second = jnp.where(rest, v * a - u * b, 0.0) * inverse
+            here, there = lane == at + k, lane == at + k + 1
+            lines = own[k:k + 1, :], own[k + 1:k + 2, :]
+            rows = (jnp.where(here, 1.0, jnp.where(there, 0.0, lines[0])),
+                    jnp.where(here, 0.0, jnp.where(there, 1.0, lines[1])))
+            for m in range(k + 2, 8):
+                head[m] = head[m] - (first * head[m][k:k + 1, :] + second * head[m][k + 1:k + 2, :])
+            own = jnp.where(rest & (here | there), 0.0, own) - (first * rows[0] + second * rows[1])
+            ratio = b / a
+            own = jnp.where(sub == k + 1, rows[1] - ratio * rows[0], own)
+            pivots = a if k == 0 else jnp.where(sub >= k, a, pivots)
+            pivots = jnp.where(sub > k, c - b * ratio, pivots)
+            later = (lane > at + k + 1) & (lane < at + 8)
+            rows = [jnp.where(later, 0.0, row) for row in rows]
+            steps.append((k, c * inverse, b * inverse, a * inverse, rows))
         state[g] = own
         scales.append(lax.rsqrt(pivots))
         inside = (lane >= at) & (lane < at + 8)
         for h in range(g + 1, groups):
-            below = spread[h - g]
+            below = [column(h, at + k) for k in range(8)]
             value = jnp.where(inside, 0.0, state[h])
-            for k in range(8):
-                factor = below[k] * inverses[k]
-                for m in range(k + 1, 8):
-                    below[m] = below[m] - factor * block[k][m]
-                value = value - factor * rows[k]
+            for k, p, q, r, rows in steps:
+                u, v = below[k], below[k + 1]
+                first, second = u * p - v * q, v * r - u * q
+                for m in range(k + 2, 8):
+                    below[m] = below[m] - (first * head[m][k:k + 1, :] + second * head[m][k + 1:k + 2, :])
+                value = value - (first * rows[0] + second * rows[1])
             state[h] = value
         beside(g)
     result = []
     for g in range(groups):
         value = jnp.where(lane < 8 * g + sub, state[g], jnp.where(lane == 8 * g + sub, 1.0, 0.0))
-        result.append(value * scales[g])
+        result.append(value * scales[g] * along)
     return jnp.concatenate(result, axis=0)
 
 
@@ -145,8 +159,8 @@
 
 
 def finish_kernel(factor, flat_ref, test_ref, x_hbm, basis_ref, projected_ref, x_ref, c_ref, parts_ref, sem):
-    copy = pltpu.make_async_copy(x_hbm, x_ref, sem)
-    copy.start()
+    x_copy = pltpu.make_async_copy(x_hbm, x_ref, sem)
+    x_copy.start()
     row, col = iota(0), iota(1)
 
     def place(a, b, value):
@@ -169,17 +183,17 @@
         parts_ref[0, at, :], parts_ref[1, at, :] = halves(x_ref[at, :])
 
     covariance = [c_ref.at[k] for k in range(3)]
-    test = stack(test_ref[...])
+    test = stack(test_ref[:RANK, :])
     image = times(test, [part[...] for part in covariance])
     gram = times(test, split(image), 1)
-    copy.wait()
-    first = inverse_factor(gram, lambda g: part_rows(128 * g, 128))
+    first = inverse_factor(gram, lambda g: None)
     spanned = times(stack(first), split(image))
     spanned_stack = stack(spanned)
     reach = times(spanned_stack, [part[...] for part in covariance])
     gram = times(spanned_stack, split(reach), 1)
-    done = 128 * (RANK // 8)
-    second = inverse_factor(gram, lambda g: part_rows(done, x_ref.shape[0] - done) if g == 0 else None)
+    x_copy.wait()
+    step = x_ref.shape[0] // 7
+    second = inverse_factor(gram, lambda g: part_rows(step * g, step) if g < 7 else None)
     second_stack = stack(second)
     projected_ref[...] = times(second_stack, split(reach)) * (1.0 / factor)
     weight = jnp.concatenate(halves(times(second_stack, split(spanned)) * factor), axis=0)
@@ -250,7 +264,7 @@
         ],
         compiler_params=pltpu.CompilerParams(vmem_limit_bytes=50 * 2 ** 20),
         cost_estimate=pl.CostEstimate(flops=2 * rows * D * RANK * 8, bytes_accessed=4 * rows * D, transcendentals=0),
-    )(flat, test_matrix.T, embeddings)
+    )(flat, jnp.pad(test_matrix.T, ((0, 8), (0, 0))), embeddings)
     return basis.T, projected
 
 

time: 104 us -> 103 us (level)
  no operation moved by 1% of the time
where the time goes in v5:
time: 103 us
  blocking collectives  62.5 us (61%)
  Pallas kernels  17.9 us (17%)
  starting transfers between devices  17.6 us (17%)
  waiting for transfers between devices  3.18 us (3%)
    all_to_all x3, blocking collectives, everyone(): lax.all_to_all(jnp.broadcast_to(value, (size,) + value.shape), axis, 0, 0)  38.7 us
    all_to_all x1, blocking collectives, total(): value = stacked_sum(lax.all_to_all(value.reshape(SX, -1, BLOCK), 'x', 0, 0))  13 us
    pallas_call x1, Pallas kernels, local(): pl.pallas_call(lambda *refs: finish_kernel(factor, *refs), in_specs=[pl.B...  12 us
    all_to_all x1, blocking collectives, total(): value = stacked_sum(lax.all_to_all(value.reshape(SY, -1, BLOCK), 'y', 0, 0))  10.8 us
    ppermute x1, starting transfers between devices, total(): other = lax.ppermute(value, 'core', swap)  8.84 us
    ppermute x1, starting transfers between devices, total(): value = pick(pair, core) + lax.ppermute(pick(pair, 1 - core), 'core', swap)  8.78 us
    pallas_call x1, Pallas kernels, local(): pl.pallas_call(gram_kernel, in_specs=[pl.BlockSpec(memory_space=pl.ANY)],...  5.89 us
  transfers between devices with their start and end apart: 2, of which 2 were waited for; matrix products, arithmetic and copies ran while one was open for 0% of the time, Pallas kernels for 0%

profile of v5, /device:TPU:1, one launch (start us, length us, event | category | flops | bytes accessed | tf_op | source)
XLA Modules:
  0.0 102.5 jit_solution(14326181536196159125)
XLA Ops:
  0.6 5.9 %shard_map.41 = f32[2560,128]{1,0:T(8,128)S(1)} custom-call(f32[1344,768]{1,0:T(8,128)} %refs_2_.1), custom_call_target="tpu_custom_call" | custom-call | flops 3170893824 | bytes 4128768 | tf_op jit(solution)/shard_map/pallas_call | solution.py:241
  6.5 0.1 dynamic-slice_bitcast_fusion
  6.6 8.8 %collective-permute-start = (f32[1280,128]{1,0:T(8,128)S(1)}, f32[1280,128]{1,0:T(8,128)S(1)}, u32[]{:S(2)}, u32[]{:S(2)}) collective-permute-start(f32[1280,128]{1,0:T(8,128)S(1)} %dynamic-slice_bitcast_fusion), channel_id=1, source_target_pairs={{0,1},{1,0},{2,3},{3,2},{4,5},{5,4},{6,7},{7,6},{8,9},{9,8},{10,11... | collective-permute-start | bytes 1966088 | tf_op jit(solution)/shard_map/ppermute | solution.py:226
  15.4 1.7 %collective-permute-done = f32[1280,128]{1,0:T(8,128)S(1)} collective-permute-done((f32[1280,128]{1,0:T(8,128)S(1)}, f32[1280,128]{1,0:T(8,128)S(1)}, u32[]{:S(2)}, u32[]{:S(2)}) %collective-permute-start) | collective-permute-done | bytes 655392 | tf_op jit(solution)/shard_map/ppermute | solution.py:226
  17.1 0.1 bitcast_add_fusion
  17.2 13.0 %all_to_all.25 = f32[4,320,128]{2,1,0:T(8,128)S(1)} all-to-all(f32[4,320,128]{2,1,0:T(8,128)S(1)} %bitcast.19), channel_id=1, replica_groups=mesh['x'=4,'y'=8,'z'=8,'core'=2] {'x'}, dimensions={0} | all-to-all | bytes 1310720 | tf_op jit(solution)/shard_map/all_to_all | solution.py:227
  30.2 10.8 %all_to_all.26 = f32[8,40,128]{2,1,0:T(8,128)S(1)} all-to-all(f32[8,40,128]{2,1,0:T(8,128)S(1)} %bitcast.21), channel_id=1, replica_groups=mesh['x'=4,'y'=8,'z'=8,'core'=2] {'y'}, dimensions={0} | all-to-all | bytes 327680 | tf_op jit(solution)/shard_map/all_to_all | solution.py:228
  41.0 17.9 %all_to_all.27 = f32[8,40,128]{2,1,0:T(8,128)S(1)} all-to-all(f32[8,40,128]{2,1,0:T(8,128)S(1)} %broadcast_in_dim.9), channel_id=1, replica_groups=mesh['x'=4,'y'=8,'z'=8,'core'=2] {'z'}, dimensions={0} | all-to-all | bytes 327680 | tf_op jit(solution)/shard_map/all_to_all | solution.py:211
  58.9 0.0 copy-start
  59.0 10.8 %all_to_all.28 = f32[8,40,128]{2,1,0:T(8,128)S(1)} all-to-all(f32[8,40,128]{2,1,0:T(8,128)S(1)} %broadcast_in_dim.10), channel_id=1, replica_groups=mesh['x'=4,'y'=8,'z'=8,'core'=2] {'y'}, dimensions={0} | all-to-all | bytes 327680 | tf_op jit(solution)/shard_map/all_to_all | solution.py:211
  69.8 10.0 %all_to_all.29 = f32[4,320,128]{2,1,0:T(8,128)S(1)} all-to-all(f32[4,320,128]{2,1,0:T(8,128)S(1)} %broadcast_in_dim.11), channel_id=1, replica_groups=mesh['x'=4,'y'=8,'z'=8,'core'=2] {'x'}, dimensions={0} | all-to-all | bytes 1310720 | tf_op jit(solution)/shard_map/all_to_all | solution.py:211
  79.8 8.8 %collective-permute-start.1 = (f32[1280,128]{1,0:T(8,128)S(1)}, f32[1280,128]{1,0:T(8,128)S(1)}, u32[]{:S(2)}, u32[]{:S(2)}) collective-permute-start(f32[1280,128]{1,0:T(8,128)S(1)} %bitcast.20), channel_id=1, source_target_pairs={{0,1},{1,0},{2,3},{3,2},{4,5},{5,4},{6,7},{7,6},{8,9},{9,8},{10,11... | collective-permute-start | bytes 1966088 | tf_op jit(solution)/shard_map/ppermute | solution.py:232
  88.7 0.0 copy-done
  88.7 1.5 %collective-permute-done.1 = f32[1280,128]{1,0:T(8,128)S(1)} collective-permute-done((f32[1280,128]{1,0:T(8,128)S(1)}, f32[1280,128]{1,0:T(8,128)S(1)}, u32[]{:S(2)}, u32[]{:S(2)}) %collective-permute-start.1) | collective-permute-done | bytes 655392 | tf_op jit(solution)/shard_map/ppermute | solution.py:232
  90.2 0.1 broadcast_select_fusion.1
  90.3 0.1 pad_maximum_fusion.refs_0_
  90.4 12.0 %shard_map.42 = (f32[80,1344]{1,0:T(8,128)}, f32[80,768]{1,0:T(8,128)}) custom-call(f32[2560,128]{1,0:T(8,128)S(1)} %pad_maximum_fusion.refs_0_, f32[88,768]{1,0:T(8,128)S(1)} %pad.4.refs_1_, f32[1344,768]{1,0:T(8,128)} %refs_2_.1), custom_call_target="tpu_custom_call" | custom-call | flops 1321205760 | bytes 4128768 | tf_op jit(solution)/shard_map/pallas_call | solution.py:254
  (7 shorter events, 0.1 us)
Async XLA Ops:
  6.6 10.5 %collective-permute-start = (f32[1280,128]{1,0:T(8,128)S(1)}, f32[1280,128]{1,0:T(8,128)S(1)}, u32[]{:S(2)}, u32[]{:S(2)}) collective-permute-start(f32[1280,128]{1,0:T(8,128)S(1)} %dynamic-slice_bitcast_fusion), channel_id=1, source_target_pairs={{0,1},{1,0},{2,3},{3,2},{4,5},{5,4},{6,7},{7,6},{8,9},{9,8},{10,11... | collective-permute-start | bytes 1966088 | tf_op jit(solution)/shard_map/ppermute | solution.py:226
  58.9 29.8 %copy-start = (f32[768,80]{0,1:T(8,128)S(1)}, f32[768,80]{0,1:T(8,128)}, u32[]{:S(2)}) copy-start(f32[768,80]{0,1:T(8,128)} %param.3) | copy-start | bytes 737284
  79.8 10.4 %collective-permute-start.1 = (f32[1280,128]{1,0:T(8,128)S(1)}, f32[1280,128]{1,0:T(8,128)S(1)}, u32[]{:S(2)}, u32[]{:S(2)}) collective-permute-start(f32[1280,128]{1,0:T(8,128)S(1)} %bitcast.20), channel_id=1, source_target_pairs={{0,1},{1,0},{2,3},{3,2},{4,5},{5,4},{6,7},{7,6},{8,9},{9,8},{10,11... | collective-permute-start | bytes 1966088 | tf_op jit(solution)/shard_map/ppermute | solution.py:232

commit v6 on v5

--- a/solution.py
+++ b/solution.py
@@ -14,7 +14,8 @@
 PACKED = len(UPPER) * BLOCK
 DIAGS = PACKED + NB // 2 * BLOCK
 FLAT = 2560
-CHUNKS = ((0, 512), (512, 512), (1024, 320))
+CHUNKS = ((0, 256), (256, 512), (768, 576))
+LIMIT = 45 * 2 ** 20
 
 
 def split(value):
@@ -38,7 +39,7 @@
     return lax.broadcasted_iota(jnp.int32, (BLOCK, BLOCK), axis)
 
 
-def gram_kernel(x_hbm, flat_ref, x_ref, high_ref, mid_ref, even_ref, odd_ref, sem):
+def gram_kernel(x_hbm, flat_ref, high_ref, mid_ref, x_ref, even_ref, odd_ref, sem):
     copies = []
     for n, (start, size) in enumerate(CHUNKS):
         at = pl.ds(start, size)
@@ -48,8 +49,14 @@
     for ref in (high_ref, mid_ref):
         ref[used:, :] = jnp.zeros((ref.shape[0] - used, D), jnp.bfloat16)
 
-    def products(n):
+    def arrive(n):
         start, size = CHUNKS[n]
+        copies[n].wait()
+        at = slice(start, start + size)
+        high_ref[at, :], mid_ref[at, :] = halves(x_ref[at, :])
+
+    arrive(0)
+    for n, (start, size) in enumerate(CHUNKS):
         deep = slice(start, start + (size + 127) // 128 * 128)
         for i in range(3):
             high_t = high_ref[deep, 256 * i:256 * (i + 1)].T
@@ -60,14 +67,8 @@
                     even_ref[3 * i + j] = value if n == 0 else even_ref[3 * i + j] + value
                 value = dot(high_t, mid_ref[deep, cols])
                 odd_ref[3 * i + j] = value if n == 0 else odd_ref[3 * i + j] + value
-
-    for n, (start, size) in enumerate(CHUNKS):
-        copies[n].wait()
-        at = slice(start, start + size)
-        high_ref[at, :], mid_ref[at, :] = halves(x_ref[at, :])
-        if n:
-            products(n - 1)
-    products(len(CHUNKS) - 1)
+            if i == 0 and n + 1 < len(CHUNKS):
+                arrive(n + 1)
 
     row, col = iota(0), iota(1)
     flat_ref[DIAGS:, :] = jnp.zeros((FLAT - DIAGS, BLOCK), jnp.float32)
@@ -87,7 +88,7 @@
                 flat_ref[DIAGS + i:DIAGS + i + 1, :] = jnp.sum(jnp.where(row == col, second, 0.0), axis=0, keepdims=True)
 
 
-def inverse_factor(gram, beside):
+def inverse_factor(gram):
     groups, shape = RANK // 8, (8, RANK)
     lane = lax.broadcasted_iota(jnp.int32, shape, 1)
     sub = lax.broadcasted_iota(jnp.int32, shape, 0)
@@ -99,24 +100,28 @@
     def column(h, j):
         return jnp.broadcast_to(state[h][:, j:j + 1], shape)
 
+    def line(value, i):
+        return jnp.broadcast_to(value[i:i + 1, :], shape)
+
     scales = []
+    coming = [column(0, k) for k in range(8)]
     for g in range(groups):
         at = 8 * g
-        head = [column(g, at + k) for k in range(8)]
+        head = coming
         own, pivots, steps = state[g], None, []
         for k in range(0, 8, 2):
             u, v = head[k], head[k + 1]
-            a, b, c = u[k:k + 1, :], v[k:k + 1, :], v[k + 1:k + 2, :]
+            a, b, c = line(u, k), line(v, k), line(v, k + 1)
             inverse = 1.0 / (a * c - b * b)
             rest = sub > k + 1
             first = jnp.where(rest, u * c - v * b, 0.0) * inverse
             second = jnp.where(rest, v * a - u * b, 0.0) * inverse
             here, there = lane == at + k, lane == at + k + 1
-            lines = own[k:k + 1, :], own[k + 1:k + 2, :]
-            rows = (jnp.where(here, 1.0, jnp.where(there, 0.0, lines[0])),
-                    jnp.where(here, 0.0, jnp.where(there, 1.0, lines[1])))
+            rows = (jnp.where(here, 1.0, jnp.where(there, 0.0, line(own, k))),
+                    jnp.where(here, 0.0, jnp.where(there, 1.0, line(own, k + 1))))
+            pairs = {m: (line(head[m], k), line(head[m], k + 1)) for m in range(k + 2, 8)}
             for m in range(k + 2, 8):
-                head[m] = head[m] - (first * head[m][k:k + 1, :] + second * head[m][k + 1:k + 2, :])
+                head[m] = head[m] - (first * pairs[m][0] + second * pairs[m][1])
             own = jnp.where(rest & (here | there), 0.0, own) - (first * rows[0] + second * rows[1])
             ratio = b / a
             own = jnp.where(sub == k + 1, rows[1] - ratio * rows[0], own)
@@ -124,21 +129,24 @@
             pivots = jnp.where(sub > k, c - b * ratio, pivots)
             later = (lane > at + k + 1) & (lane < at + 8)
             rows = [jnp.where(later, 0.0, row) for row in rows]
-            steps.append((k, c * inverse, b * inverse, a * inverse, rows))
+            steps.append((k, c * inverse, b * inverse, a * inverse, rows, pairs))
         state[g] = own
         scales.append(lax.rsqrt(pivots))
         inside = (lane >= at) & (lane < at + 8)
         for h in range(g + 1, groups):
             below = [column(h, at + k) for k in range(8)]
             value = jnp.where(inside, 0.0, state[h])
-            for k, p, q, r, rows in steps:
+            if h == g + 1:
+                coming = [column(h, at + 8 + k) for k in range(8)]
+            for k, p, q, r, rows, pairs in steps:
                 u, v = below[k], below[k + 1]
                 first, second = u * p - v * q, v * r - u * q
+                if h == g + 1:
+                    coming = [coming[m] - (first * line(u, m) + second * line(v, m)) for m in range(8)]
                 for m in range(k + 2, 8):
-                    below[m] = below[m] - (first * head[m][k:k + 1, :] + second * head[m][k + 1:k + 2, :])
+                    below[m] = below[m] - (first * pairs[m][0] + second * pairs[m][1])
                 value = value - (first * rows[0] + second * rows[1])
             state[h] = value
-        beside(g)
     result = []
     for g in range(groups):
         value = jnp.where(lane < 8 * g + sub, state[g], jnp.where(lane == 8 * g + sub, 1.0, 0.0))
@@ -158,47 +166,50 @@
     return first[:n] + (first[n:2 * n] + second[:n] + small)
 
 
-def finish_kernel(factor, flat_ref, test_ref, x_hbm, basis_ref, projected_ref, x_ref, c_ref, parts_ref, sem):
-    x_copy = pltpu.make_async_copy(x_hbm, x_ref, sem)
-    x_copy.start()
+def finish_kernel(factor, flat_ref, test_ref, high_ref, mid_ref, basis_ref, projected_ref, c_ref):
     row, col = iota(0), iota(1)
 
     def place(a, b, value):
         for k, part in enumerate(split(value)):
             c_ref[k, a * BLOCK:(a + 1) * BLOCK, b * BLOCK:(b + 1) * BLOCK] = part
 
-    for n, (a, b) in enumerate(UPPER):
-        value = flat_ref[n * BLOCK:(n + 1) * BLOCK, :]
-        place(a, b, value)
-        place(b, a, value.T)
+    test = stack(test_ref[:RANK, :])
+    image = None
     for i in range(NB // 2):
+        for n, (a, b) in enumerate(UPPER):
+            if a // 2 == i:
+                value = flat_ref[n * BLOCK:(n + 1) * BLOCK, :]
+                place(a, b, value)
+                place(b, a, value.T)
         value = flat_ref[PACKED + i * BLOCK:PACKED + (i + 1) * BLOCK, :]
         flipped = value.T
         place(2 * i, 2 * i, jnp.where(row <= col, value, flipped))
         other = jnp.where(row > col, value, flipped)
         place(2 * i + 1, 2 * i + 1, jnp.where(row == col, flat_ref[DIAGS + i:DIAGS + i + 1, :], other))
-
-    def part_rows(start, size):
-        at = slice(start, start + size)
-        parts_ref[0, at, :], parts_ref[1, at, :] = halves(x_ref[at, :])
+        deep = slice(256 * i, 256 * (i + 1))
+        value = times(test[:, deep], [c_ref[k, deep, :] for k in range(3)])
+        image = value if i == 0 else image + value
 
     covariance = [c_ref.at[k] for k in range(3)]
-    test = stack(test_ref[:RANK, :])
-    image = times(test, [part[...] for part in covariance])
     gram = times(test, split(image), 1)
-    first = inverse_factor(gram, lambda g: None)
+    first = inverse_factor(gram)
     spanned = times(stack(first), split(image))
     spanned_stack = stack(spanned)
     reach = times(spanned_stack, [part[...] for part in covariance])
     gram = times(spanned_stack, split(reach), 1)
-    x_copy.wait()
-    step = x_ref.shape[0] // 7
-    second = inverse_factor(gram, lambda g: part_rows(step * g, step) if g < 7 else None)
+    second = inverse_factor(gram)
     second_stack = stack(second)
     projected_ref[...] = times(second_stack, split(reach)) * (1.0 / factor)
-    weight = jnp.concatenate(halves(times(second_stack, split(spanned)) * factor), axis=0)
-    main, rest = dot(weight, parts_ref[0], 1), dot(weight, parts_ref[1], 1)
-    basis_ref[...] = main[:RANK] + (main[RANK:] + rest[:RANK] + rest[RANK:])
+    empty = jnp.zeros((BLOCK - RANK, D), jnp.float32)
+    weight = jnp.concatenate([times(second_stack, split(spanned)) * factor, empty], axis=0)
+    weight = jnp.concatenate(halves(weight), axis=0).T
+    total_rows = basis_ref.shape[1]
+    for start in range(0, total_rows, 256):
+        size = min(256, total_rows - start)
+        at = slice(start, start + size)
+        main, rest = dot(high_ref[at, :], weight), dot(mid_ref[at, :], weight)
+        value = main[:, :BLOCK] + (main[:, BLOCK:] + (rest[:, :BLOCK] + rest[:, BLOCK:]))
+        basis_ref[:, at] = value.T[:RANK, :]
 
 
 def tree(parts):
@@ -238,33 +249,28 @@
 def local(embeddings, test_matrix):
     rows = embeddings.shape[0]
     factor = float(np.sqrt(np.float32(rows * 2 * SX * SY * SZ)))
-    flat = pl.pallas_call(
+    held = CHUNKS[-1][0] + (CHUNKS[-1][1] + 127) // 128 * 128
+    flat, high, mid = pl.pallas_call(
         gram_kernel,
         in_specs=[pl.BlockSpec(memory_space=pl.ANY)],
-        out_specs=pl.BlockSpec(memory_space=pltpu.VMEM),
-        out_shape=jax.ShapeDtypeStruct((FLAT, BLOCK), jnp.float32),
+        out_specs=[pl.BlockSpec(memory_space=pltpu.VMEM)] * 3,
+        out_shape=[jax.ShapeDtypeStruct((FLAT, BLOCK), jnp.float32)] + [jax.ShapeDtypeStruct((held, D), jnp.bfloat16)] * 2,
         scratch_shapes=[pltpu.VMEM((rows, D), jnp.float32)]
-        + [pltpu.VMEM((CHUNKS[-1][0] + 512, D), jnp.bfloat16)] * 2
         + [pltpu.VMEM((9, 256, 256), jnp.float32)] * 2
         + [pltpu.SemaphoreType.DMA((len(CHUNKS),))],
-        compiler_params=pltpu.CompilerParams(vmem_limit_bytes=50 * 2 ** 20),
+        compiler_params=pltpu.CompilerParams(vmem_limit_bytes=LIMIT),
         cost_estimate=pl.CostEstimate(flops=2 * rows * D * D * 2, bytes_accessed=4 * rows * D, transcendentals=0),
     )(embeddings)
     flat = total(flat)
     basis, projected = pl.pallas_call(
         lambda *refs: finish_kernel(factor, *refs),
-        in_specs=[pl.BlockSpec(memory_space=pltpu.VMEM)] * 2 + [pl.BlockSpec(memory_space=pl.ANY)],
+        in_specs=[pl.BlockSpec(memory_space=pltpu.VMEM)] * 4,
         out_specs=[pl.BlockSpec(memory_space=pltpu.VMEM)] * 2,
         out_shape=[jax.ShapeDtypeStruct((RANK, rows), jnp.float32), jax.ShapeDtypeStruct((RANK, D), jnp.float32)],
-        scratch_shapes=[
-            pltpu.VMEM((rows, D), jnp.float32),
-            pltpu.VMEM((3, D, D), jnp.bfloat16),
-            pltpu.VMEM((2, rows, D), jnp.bfloat16),
-            pltpu.SemaphoreType.DMA,
-        ],
-        compiler_params=pltpu.CompilerParams(vmem_limit_bytes=50 * 2 ** 20),
+        scratch_shapes=[pltpu.VMEM((3, D, D), jnp.bfloat16)],
+        compiler_params=pltpu.CompilerParams(vmem_limit_bytes=LIMIT),
         cost_estimate=pl.CostEstimate(flops=2 * rows * D * RANK * 8, bytes_accessed=4 * rows * D, transcendentals=0),
-    )(flat, jnp.pad(test_matrix.T, ((0, 8), (0, 0))), embeddings)
+    )(flat, jnp.pad(test_matrix.T, ((0, 8), (0, 0))), high, mid)
     return basis.T, projected
 
 

time: 103 us -> 105 us (1.019)
  local copies, waits for them, and re-layouts: 0.15 us -> 4.78 us
  Pallas kernels: 17.9 us -> 14.9 us
  other arithmetic: 0.3 us -> 1.39 us
    unnamed x2 -> x4, local copies, waits for them, and re-layouts: 0.01 us -> 2.85 us
    pallas_call x1, Pallas kernels: 12 us -> 9.66 us  [local(): pl.pallas_call(lambda *refs: finish_kernel(factor, *refs), in_specs=[pl.B...]
    add x1, other arithmetic: 0.07 us -> 1.15 us  [total(): value = pick(pair, core) + lax.ppermute(pick(pair, 1 - core), 'core', swap)]
  transfers between devices with their start and end apart: 2 -> 2, of which waited for: 2 -> 2; matrix products, arithmetic and copies ran while one was open for 0% -> 1% of each run, Pallas kernels for 0% -> 0%
where the time goes in v6:
time: 105 us; the launch traced here: 104 us
  blocking collectives  62.4 us (59%)
  starting transfers between devices  17.4 us (17%)
  Pallas kernels  14.9 us (14%)
  local copies, waits for them, and re-layouts  4.78 us (5%)
  waiting for transfers between devices  2.77 us (3%)
  other arithmetic  1.39 us (1%)
    all_to_all x3, blocking collectives, everyone(): lax.all_to_all(jnp.broadcast_to(value, (size,) + value.shape), axis, 0, 0)  38.6 us
    all_to_all x1, blocking collectives, total(): value = stacked_sum(lax.all_to_all(value.reshape(SX, -1, BLOCK), 'x', 0, 0))  13 us
    all_to_all x1, blocking collectives, total(): value = stacked_sum(lax.all_to_all(value.reshape(SY, -1, BLOCK), 'y', 0, 0))  10.8 us
    pallas_call x1, Pallas kernels, local(): pl.pallas_call(lambda *refs: finish_kernel(factor, *refs), in_specs=[pl.B...  9.66 us
    ppermute x1, starting transfers between devices, total(): value = pick(pair, core) + lax.ppermute(pick(pair, 1 - core), 'core', swap)  8.78 us
    ppermute x1, starting transfers between devices, total(): other = lax.ppermute(value, 'core', swap)  8.66 us
    pallas_call x1, Pallas kernels, local(): pl.pallas_call(gram_kernel, in_specs=[pl.BlockSpec(memory_space=pl.ANY)],...  5.28 us
    unnamed x4, local copies, waits for them, and re-layouts  2.85 us
  transfers between devices with their start and end apart: 2, of which 2 were waited for; matrix products, arithmetic and copies ran while one was open for 1% of the time, Pallas kernels for 0%

profile of v6, /device:TPU:1, one launch (start us, length us, event | category | flops | bytes accessed | tf_op | source)
XLA Modules:
  0.0 104.4 jit_solution(12379169288234876773)
XLA Ops:
  0.6 5.3 %shard_map.41 = (f32[2560,128]{1,0:T(8,128)S(1)}, bf16[1408,768]{1,0:T(8,128)(2,1)S(1)}, bf16[1408,768]{1,0:T(8,128)(2,1)S(1)}) custom-call(f32[1344,768]{1,0:T(8,128)} %x_hbm.1), custom_call_target="tpu_custom_call" | custom-call | flops 3170893824 | bytes 4128768 | tf_op jit(solution)/shard_map/pallas_call | solution.py:253
  5.9 0.0 copy-start
  5.9 1.3 %copy-done = bf16[1408,768]{1,0:T(8,128)(2,1)} copy-done((bf16[1408,768]{1,0:T(8,128)(2,1)}, bf16[1408,768]{1,0:T(8,128)(2,1)S(1)}, u32[]{:S(2)}) %copy-start) | copy-done | bytes 2162712
  7.3 0.9 dynamic-slice_bitcast_fusion
  8.2 8.8 %collective-permute-start = (f32[1280,128]{1,0:T(8,128)}, f32[1280,128]{1,0:T(8,128)}, u32[]{:S(2)}, u32[]{:S(2)}) collective-permute-start(f32[1280,128]{1,0:T(8,128)} %dynamic-slice_bitcast_fusion), channel_id=1, source_target_pairs={{0,1},{1,0},{2,3},{3,2},{4,5},{5,4},{6,7},{7,6},{8,9},{9,8},{10,11... | collective-permute-start | bytes 1966088 | tf_op jit(solution)/shard_map/ppermute | solution.py:237
  17.0 2.0 %collective-permute-done = f32[1280,128]{1,0:T(8,128)} collective-permute-done((f32[1280,128]{1,0:T(8,128)}, f32[1280,128]{1,0:T(8,128)}, u32[]{:S(2)}, u32[]{:S(2)}) %collective-permute-start) | collective-permute-done | bytes 655392 | tf_op jit(solution)/shard_map/ppermute | solution.py:237
  19.0 1.2 %bitcast_add_fusion = f32[1280,128]{1,0:T(8,128)S(1)} fusion(f32[1280,128]{1,0:T(8,128)} %collective-permute-done, f32[2,1280,128]{2,1,0:T(8,128)S(1)} %bitcast.18, s32[]{:T(128)S(6)} %select_n.20), kind=kLoop, calls=%fused_computation.1 | loop fusion | flops 163840 | bytes 1966084 | tf_op jit(solution)/shard_map/add | solution.py:237
  20.2 13.0 %all_to_all.25 = f32[4,320,128]{2,1,0:T(8,128)S(1)} all-to-all(f32[4,320,128]{2,1,0:T(8,128)S(1)} %bitcast.19), channel_id=1, replica_groups=mesh['x'=4,'y'=8,'z'=8,'core'=2] {'x'}, dimensions={0} | all-to-all | bytes 1310720 | tf_op jit(solution)/shard_map/all_to_all | solution.py:238
  33.2 10.8 %all_to_all.26 = f32[8,40,128]{2,1,0:T(8,128)S(1)} all-to-all(f32[8,40,128]{2,1,0:T(8,128)S(1)} %bitcast.21), channel_id=1, replica_groups=mesh['x'=4,'y'=8,'z'=8,'core'=2] {'y'}, dimensions={0} | all-to-all | bytes 327680 | tf_op jit(solution)/shard_map/all_to_all | solution.py:239
  44.0 17.9 %all_to_all.27 = f32[8,40,128]{2,1,0:T(8,128)S(1)} all-to-all(f32[8,40,128]{2,1,0:T(8,128)S(1)} %broadcast_in_dim.9), channel_id=1, replica_groups=mesh['x'=4,'y'=8,'z'=8,'core'=2] {'z'}, dimensions={0} | all-to-all | bytes 327680 | tf_op jit(solution)/shard_map/all_to_all | solution.py:222
  62.0 10.7 %all_to_all.28 = f32[8,40,128]{2,1,0:T(8,128)S(1)} all-to-all(f32[8,40,128]{2,1,0:T(8,128)S(1)} %broadcast_in_dim.10), channel_id=1, replica_groups=mesh['x'=4,'y'=8,'z'=8,'core'=2] {'y'}, dimensions={0} | all-to-all | bytes 327680 | tf_op jit(solution)/shard_map/all_to_all | solution.py:222
  72.7 10.0 %all_to_all.29 = f32[4,320,128]{2,1,0:T(8,128)S(1)} all-to-all(f32[4,320,128]{2,1,0:T(8,128)S(1)} %broadcast_in_dim.11), channel_id=1, replica_groups=mesh['x'=4,'y'=8,'z'=8,'core'=2] {'x'}, dimensions={0} | all-to-all | bytes 1310720 | tf_op jit(solution)/shard_map/all_to_all | solution.py:222
  82.7 8.7 %collective-permute-start.1 = (f32[1280,128]{1,0:T(8,128)S(1)}, f32[1280,128]{1,0:T(8,128)S(1)}, u32[]{:S(2)}, u32[]{:S(2)}) collective-permute-start(f32[1280,128]{1,0:T(8,128)S(1)} %bitcast.20), channel_id=1, source_target_pairs={{0,1},{1,0},{2,3},{3,2},{4,5},{5,4},{6,7},{7,6},{8,9},{9,8},{10,11... | collective-permute-start | bytes 1966088 | tf_op jit(solution)/shard_map/ppermute | solution.py:243
  91.4 1.0 pad.4.refs_1_
  92.4 0.7 collective-permute-done.1
  93.1 0.1 broadcast_select_fusion.1
  93.2 0.0 copy-start.1
  93.2 0.1 pad_maximum_fusion.refs_0_
  93.3 1.5 %copy-done.1 = bf16[1408,768]{1,0:T(8,128)(2,1)S(1)} copy-done((bf16[1408,768]{1,0:T(8,128)(2,1)S(1)}, bf16[1408,768]{1,0:T(8,128)(2,1)}, u32[]{:S(2)}) %copy-start.1) | copy-done | bytes 2162712
  94.8 9.7 %shard_map.42 = (f32[80,1344]{1,0:T(8,128)}, f32[80,768]{1,0:T(8,128)}) custom-call(f32[2560,128]{1,0:T(8,128)S(1)} %pad_maximum_fusion.refs_0_, f32[88,768]{1,0:T(8,128)S(1)} %pad.4.refs_1_, bf16[1408,768]{1,0:T(8,128)(2,1)S(1)} %get-tuple-element.8.refs_2_, bf16[1408,768]{1,0:T(8,128)(2,1)S(1)} %copy-done.1), custom_call_target="tpu_custom_call" | custom-call | flops 1321205760 | bytes 4128768 | tf_op jit(solution)/shard_map/pallas_call | solution.py:265
  (6 shorter events, 0.1 us)
Async XLA Ops:
  5.9 1.4 %copy-start = (bf16[1408,768]{1,0:T(8,128)(2,1)}, bf16[1408,768]{1,0:T(8,128)(2,1)S(1)}, u32[]{:S(2)}) copy-start(bf16[1408,768]{1,0:T(8,128)(2,1)S(1)} %get-tuple-element.9.refs_3_) | copy-start | bytes 6488068
  8.2 10.8 %collective-permute-start = (f32[1280,128]{1,0:T(8,128)}, f32[1280,128]{1,0:T(8,128)}, u32[]{:S(2)}, u32[]{:S(2)}) collective-permute-start(f32[1280,128]{1,0:T(8,128)} %dynamic-slice_bitcast_fusion), channel_id=1, source_target_pairs={{0,1},{1,0},{2,3},{3,2},{4,5},{5,4},{6,7},{7,6},{8,9},{9,8},{10,11... | collective-permute-start | bytes 1966088 | tf_op jit(solution)/shard_map/ppermute | solution.py:237
  82.7 10.4 %collective-permute-start.1 = (f32[1280,128]{1,0:T(8,128)S(1)}, f32[1280,128]{1,0:T(8,128)S(1)}, u32[]{:S(2)}, u32[]{:S(2)}) collective-permute-start(f32[1280,128]{1,0:T(8,128)S(1)} %bitcast.20), channel_id=1, source_target_pairs={{0,1},{1,0},{2,3},{3,2},{4,5},{5,4},{6,7},{7,6},{8,9},{9,8},{10,11... | collective-permute-start | bytes 1966088 | tf_op jit(solution)/shard_map/ppermute | solution.py:243
  93.2 1.6 %copy-start.1 = (bf16[1408,768]{1,0:T(8,128)(2,1)S(1)}, bf16[1408,768]{1,0:T(8,128)(2,1)}, u32[]{:S(2)}) copy-start(bf16[1408,768]{1,0:T(8,128)(2,1)} %copy-done) | copy-start | bytes 6488068

commit v7 on v6

--- a/solution.py
+++ b/solution.py
@@ -15,7 +15,7 @@
 DIAGS = PACKED + NB // 2 * BLOCK
 FLAT = 2560
 CHUNKS = ((0, 256), (256, 512), (768, 576))
-LIMIT = 45 * 2 ** 20
+LIMIT = 50 * 2 ** 20
 
 
 def split(value):
@@ -39,7 +39,7 @@
     return lax.broadcasted_iota(jnp.int32, (BLOCK, BLOCK), axis)
 
 
-def gram_kernel(x_hbm, flat_ref, high_ref, mid_ref, x_ref, even_ref, odd_ref, sem):
+def gram_kernel(x_hbm, flat_ref, high_hbm, mid_hbm, x_ref, high_ref, mid_ref, even_ref, odd_ref, sem, out_sem):
     copies = []
     for n, (start, size) in enumerate(CHUNKS):
         at = pl.ds(start, size)
@@ -54,7 +54,11 @@
         copies[n].wait()
         at = slice(start, start + size)
         high_ref[at, :], mid_ref[at, :] = halves(x_ref[at, :])
-
+        for k, (part, hbm) in enumerate(((high_ref, high_hbm), (mid_ref, mid_hbm))):
+            keeps.append(pltpu.make_async_copy(part.at[at, :], hbm.at[at, :], out_sem.at[n, k]))
+            keeps[-1].start()
+
+    keeps = []
     arrive(0)
     for n, (start, size) in enumerate(CHUNKS):
         deep = slice(start, start + (size + 127) // 128 * 128)
@@ -86,6 +90,8 @@
                 at = PACKED + i * BLOCK
                 flat_ref[at:at + BLOCK, :] = jnp.where(row <= col, first, second)
                 flat_ref[DIAGS + i:DIAGS + i + 1, :] = jnp.sum(jnp.where(row == col, second, 0.0), axis=0, keepdims=True)
+    for copy in keeps:
+        copy.wait()
 
 
 def inverse_factor(gram):
@@ -166,7 +172,11 @@
     return first[:n] + (first[n:2 * n] + second[:n] + small)
 
 
-def finish_kernel(factor, flat_ref, test_ref, high_ref, mid_ref, basis_ref, projected_ref, c_ref):
+def finish_kernel(factor, flat_ref, test_ref, high_hbm, mid_hbm, basis_ref, projected_ref, high_ref, mid_ref, c_ref, sem):
+    copies = [pltpu.make_async_copy(hbm, ref, sem.at[k])
+              for k, (hbm, ref) in enumerate(((high_hbm, high_ref), (mid_hbm, mid_ref)))]
+    for copy in copies:
+        copy.start()
     row, col = iota(0), iota(1)
 
     def place(a, b, value):
@@ -200,6 +210,8 @@
     second = inverse_factor(gram)
     second_stack = stack(second)
     projected_ref[...] = times(second_stack, split(reach)) * (1.0 / factor)
+    for copy in copies:
+        copy.wait()
     empty = jnp.zeros((BLOCK - RANK, D), jnp.float32)
     weight = jnp.concatenate([times(second_stack, split(spanned)) * factor, empty], axis=0)
     weight = jnp.concatenate(halves(weight), axis=0).T
@@ -253,21 +265,23 @@
     flat, high, mid = pl.pallas_call(
         gram_kernel,
         in_specs=[pl.BlockSpec(memory_space=pl.ANY)],
-        out_specs=[pl.BlockSpec(memory_space=pltpu.VMEM)] * 3,
-        out_shape=[jax.ShapeDtypeStruct((FLAT, BLOCK), jnp.float32)] + [jax.ShapeDtypeStruct((held, D), jnp.bfloat16)] * 2,
+        out_specs=[pl.BlockSpec(memory_space=pltpu.VMEM)] + [pl.BlockSpec(memory_space=pl.ANY)] * 2,
+        out_shape=[jax.ShapeDtypeStruct((FLAT, BLOCK), jnp.float32)] + [jax.ShapeDtypeStruct((rows, D), jnp.bfloat16)] * 2,
         scratch_shapes=[pltpu.VMEM((rows, D), jnp.float32)]
+        + [pltpu.VMEM((held, D), jnp.bfloat16)] * 2
         + [pltpu.VMEM((9, 256, 256), jnp.float32)] * 2
-        + [pltpu.SemaphoreType.DMA((len(CHUNKS),))],
+        + [pltpu.SemaphoreType.DMA((len(CHUNKS),)), pltpu.SemaphoreType.DMA((len(CHUNKS), 2))],
         compiler_params=pltpu.CompilerParams(vmem_limit_bytes=LIMIT),
         cost_estimate=pl.CostEstimate(flops=2 * rows * D * D * 2, bytes_accessed=4 * rows * D, transcendentals=0),
     )(embeddings)
     flat = total(flat)
     basis, projected = pl.pallas_call(
         lambda *refs: finish_kernel(factor, *refs),
-        in_specs=[pl.BlockSpec(memory_space=pltpu.VMEM)] * 4,
+        in_specs=[pl.BlockSpec(memory_space=pltpu.VMEM)] * 2 + [pl.BlockSpec(memory_space=pl.ANY)] * 2,
         out_specs=[pl.BlockSpec(memory_space=pltpu.VMEM)] * 2,
         out_shape=[jax.ShapeDtypeStruct((RANK, rows), jnp.float32), jax.ShapeDtypeStruct((RANK, D), jnp.float32)],
-        scratch_shapes=[pltpu.VMEM((3, D, D), jnp.bfloat16)],
+        scratch_shapes=[pltpu.VMEM((rows, D), jnp.bfloat16)] * 2
+        + [pltpu.VMEM((3, D, D), jnp.bfloat16), pltpu.SemaphoreType.DMA((2,))],
         compiler_params=pltpu.CompilerParams(vmem_limit_bytes=LIMIT),
         cost_estimate=pl.CostEstimate(flops=2 * rows * D * RANK * 8, bytes_accessed=4 * rows * D, transcendentals=0),
     )(flat, jnp.pad(test_matrix.T, ((0, 8), (0, 0))), high, mid)

time: 105 us -> 105 us (level)
  local copies, waits for them, and re-layouts: 4.78 us -> 1.93 us
  Pallas kernels: 14.9 us -> 17.7 us
    unnamed x4 -> x0, local copies, waits for them, and re-layouts: 2.85 us -> none
    pallas_call x1, Pallas kernels: 9.66 us -> 11.4 us  [local(): pl.pallas_call(lambda *refs: finish_kernel(factor, *refs), in_specs=[pl.B...]
where the time goes in v7:
time: 105 us; the launch traced here: 104 us
  blocking collectives  62.4 us (59%)
  Pallas kernels  17.7 us (17%)
  starting transfers between devices  17.4 us (17%)
  waiting for transfers between devices  2.77 us (3%)
  local copies, waits for them, and re-layouts  1.93 us (2%)
  other arithmetic  1.39 us (1%)
    all_to_all x3, blocking collectives, everyone(): lax.all_to_all(jnp.broadcast_to(value, (size,) + value.shape), axis, 0, 0)  38.6 us
    all_to_all x1, blocking collectives, total(): value = stacked_sum(lax.all_to_all(value.reshape(SX, -1, BLOCK), 'x', 0, 0))  13 us
    pallas_call x1, Pallas kernels, local(): pl.pallas_call(lambda *refs: finish_kernel(factor, *refs), in_specs=[pl.B...  11.4 us
    all_to_all x1, blocking collectives, total(): value = stacked_sum(lax.all_to_all(value.reshape(SY, -1, BLOCK), 'y', 0, 0))  10.8 us
    ppermute x1, starting transfers between devices, total(): value = pick(pair, core) + lax.ppermute(pick(pair, 1 - core), 'core', swap)  8.78 us
    ppermute x1, starting transfers between devices, total(): other = lax.ppermute(value, 'core', swap)  8.66 us
    pallas_call x1, Pallas kernels, local(): pl.pallas_call(gram_kernel, in_specs=[pl.BlockSpec(memory_space=pl.ANY)],...  6.23 us
  transfers between devices with their start and end apart: 2, of which 2 were waited for; matrix products, arithmetic and copies ran while one was open for 1% of the time, Pallas kernels for 0%

profile of v7, /device:TPU:1, one launch (start us, length us, event | category | flops | bytes accessed | tf_op | source)
XLA Modules:
  0.0 104.3 jit_solution(13738978620491044146)
XLA Ops:
  0.6 6.2 %shard_map.41 = (f32[2560,128]{1,0:T(8,128)S(1)}, bf16[1344,768]{1,0:T(8,128)(2,1)S(1)}, bf16[1344,768]{1,0:T(8,128)(2,1)}) custom-call(f32[1344,768]{1,0:T(8,128)} %x_hbm.1), custom_call_target="tpu_custom_call" | custom-call | flops 3170893824 | bytes 4128768 | tf_op jit(solution)/shard_map/pallas_call | solution.py:265
  6.9 0.9 dynamic-slice_bitcast_fusion
  7.8 8.8 %collective-permute-start = (f32[1280,128]{1,0:T(8,128)}, f32[1280,128]{1,0:T(8,128)}, u32[]{:S(2)}, u32[]{:S(2)}) collective-permute-start(f32[1280,128]{1,0:T(8,128)} %dynamic-slice_bitcast_fusion), channel_id=1, source_target_pairs={{0,1},{1,0},{2,3},{3,2},{4,5},{5,4},{6,7},{7,6},{8,9},{9,8},{10,11... | collective-permute-start | bytes 1966088 | tf_op jit(solution)/shard_map/ppermute | solution.py:249
  16.6 2.0 %collective-permute-done = f32[1280,128]{1,0:T(8,128)} collective-permute-done((f32[1280,128]{1,0:T(8,128)}, f32[1280,128]{1,0:T(8,128)}, u32[]{:S(2)}, u32[]{:S(2)}) %collective-permute-start) | collective-permute-done | bytes 655392 | tf_op jit(solution)/shard_map/ppermute | solution.py:249
  18.6 1.2 %bitcast_add_fusion = f32[1280,128]{1,0:T(8,128)S(1)} fusion(f32[1280,128]{1,0:T(8,128)} %collective-permute-done, f32[2,1280,128]{2,1,0:T(8,128)S(1)} %bitcast.18, s32[]{:T(128)S(6)} %select_n.20), kind=kLoop, calls=%fused_computation.1 | loop fusion | flops 163840 | bytes 1966084 | tf_op jit(solution)/shard_map/add | solution.py:249
  19.8 13.0 %all_to_all.25 = f32[4,320,128]{2,1,0:T(8,128)S(1)} all-to-all(f32[4,320,128]{2,1,0:T(8,128)S(1)} %bitcast.19), channel_id=1, replica_groups=mesh['x'=4,'y'=8,'z'=8,'core'=2] {'x'}, dimensions={0} | all-to-all | bytes 1310720 | tf_op jit(solution)/shard_map/all_to_all | solution.py:250
  32.8 10.8 %all_to_all.26 = f32[8,40,128]{2,1,0:T(8,128)S(1)} all-to-all(f32[8,40,128]{2,1,0:T(8,128)S(1)} %bitcast.21), channel_id=1, replica_groups=mesh['x'=4,'y'=8,'z'=8,'core'=2] {'y'}, dimensions={0} | all-to-all | bytes 327680 | tf_op jit(solution)/shard_map/all_to_all | solution.py:251
  43.6 17.9 %all_to_all.27 = f32[8,40,128]{2,1,0:T(8,128)S(1)} all-to-all(f32[8,40,128]{2,1,0:T(8,128)S(1)} %broadcast_in_dim.9), channel_id=1, replica_groups=mesh['x'=4,'y'=8,'z'=8,'core'=2] {'z'}, dimensions={0} | all-to-all | bytes 327680 | tf_op jit(solution)/shard_map/all_to_all | solution.py:234
  61.6 10.7 %all_to_all.28 = f32[8,40,128]{2,1,0:T(8,128)S(1)} all-to-all(f32[8,40,128]{2,1,0:T(8,128)S(1)} %broadcast_in_dim.10), channel_id=1, replica_groups=mesh['x'=4,'y'=8,'z'=8,'core'=2] {'y'}, dimensions={0} | all-to-all | bytes 327680 | tf_op jit(solution)/shard_map/all_to_all | solution.py:234
  72.3 10.0 %all_to_all.29 = f32[4,320,128]{2,1,0:T(8,128)S(1)} all-to-all(f32[4,320,128]{2,1,0:T(8,128)S(1)} %broadcast_in_dim.11), channel_id=1, replica_groups=mesh['x'=4,'y'=8,'z'=8,'core'=2] {'x'}, dimensions={0} | all-to-all | bytes 1310720 | tf_op jit(solution)/shard_map/all_to_all | solution.py:234
  82.3 8.7 %collective-permute-start.1 = (f32[1280,128]{1,0:T(8,128)S(1)}, f32[1280,128]{1,0:T(8,128)S(1)}, u32[]{:S(2)}, u32[]{:S(2)}) collective-permute-start(f32[1280,128]{1,0:T(8,128)S(1)} %bitcast.20), channel_id=1, source_target_pairs={{0,1},{1,0},{2,3},{3,2},{4,5},{5,4},{6,7},{7,6},{8,9},{9,8},{10,11... | collective-permute-start | bytes 1966088 | tf_op jit(solution)/shard_map/ppermute | solution.py:255
  91.0 1.0 pad.4.refs_1_
  92.0 0.7 collective-permute-done.1
  92.7 0.1 broadcast_select_fusion.1
  92.8 0.1 pad_maximum_fusion.refs_0_
  92.9 11.4 %shard_map.42 = (f32[80,1344]{1,0:T(8,128)}, f32[80,768]{1,0:T(8,128)}) custom-call(f32[2560,128]{1,0:T(8,128)S(1)} %pad_maximum_fusion.refs_0_, f32[88,768]{1,0:T(8,128)S(1)} %pad.4.refs_1_, bf16[1344,768]{1,0:T(8,128)(2,1)S(1)} %get-tuple-element.8.refs_2_, bf16[1344,768]{1,0:T(8,128)(2,1)} %get-tuple-element.9.refs_3_), custom_call_target="tpu_custom_call" | custom-call | flops 1321205760 | bytes 4128768 | tf_op jit(solution)/shard_map/pallas_call | solution.py:278
  (6 shorter events, 0.1 us)
Async XLA Ops:
  7.8 10.8 %collective-permute-start = (f32[1280,128]{1,0:T(8,128)}, f32[1280,128]{1,0:T(8,128)}, u32[]{:S(2)}, u32[]{:S(2)}) collective-permute-start(f32[1280,128]{1,0:T(8,128)} %dynamic-slice_bitcast_fusion), channel_id=1, source_target_pairs={{0,1},{1,0},{2,3},{3,2},{4,5},{5,4},{6,7},{7,6},{8,9},{9,8},{10,11... | collective-permute-start | bytes 1966088 | tf_op jit(solution)/shard_map/ppermute | solution.py:249
  82.3 10.4 %collective-permute-start.1 = (f32[1280,128]{1,0:T(8,128)S(1)}, f32[1280,128]{1,0:T(8,128)S(1)}, u32[]{:S(2)}, u32[]{:S(2)}) collective-permute-start(f32[1280,128]{1,0:T(8,128)S(1)} %bitcast.20), channel_id=1, source_target_pairs={{0,1},{1,0},{2,3},{3,2},{4,5},{5,4},{6,7},{7,6},{8,9},{9,8},{10,11... | collective-permute-start | bytes 1966088 | tf_op jit(solution)/shard_map/ppermute | solution.py:255

commit v8 on v6

--- a/solution.py
+++ b/solution.py
@@ -15,7 +15,7 @@
 DIAGS = PACKED + NB // 2 * BLOCK
 FLAT = 2560
 CHUNKS = ((0, 256), (256, 512), (768, 576))
-LIMIT = 45 * 2 ** 20
+LIMITS = 45 * 2 ** 20, 45 * 2 ** 20
 
 
 def split(value):
@@ -222,33 +222,35 @@
     return lax.all_to_all(jnp.broadcast_to(value, (size,) + value.shape), axis, 0, 0)
 
 
-def pick(array, i):
-    return lax.dynamic_index_in_dim(array, i, 0, keepdims=False)
+def pick(pair, i):
+    size = (1,) + pair.shape[1:]
+    return lax.dynamic_slice(pair, (i, np.int32(0), np.int32(0)), size, allow_negative_indices=False)[0]
 
 
 def stacked_sum(values):
     return tree([values[i] for i in range(values.shape[0])])
 
 
-def total(flat):
-    core = lax.axis_index("core")
+def total(flat, mine, theirs, low_core):
     swap = [(0, 1), (1, 0)]
     pair = flat.reshape(2, FLAT // 2, BLOCK)
-    value = pick(pair, core) + lax.ppermute(pick(pair, 1 - core), "core", swap)
+    value = pick(pair, mine) + lax.ppermute(pick(pair, theirs), "core", swap)
     value = stacked_sum(lax.all_to_all(value.reshape(SX, -1, BLOCK), "x", 0, 0))
     value = stacked_sum(lax.all_to_all(value.reshape(SY, -1, BLOCK), "y", 0, 0))
     value = stacked_sum(everyone(value, "z", SZ))
     value = everyone(value, "y", SY).reshape(-1, BLOCK)
     value = everyone(value, "x", SX).reshape(-1, BLOCK)
     other = lax.ppermute(value, "core", swap)
-    low = jnp.where(core == 0, value, other)
-    high = jnp.where(core == 0, other, value)
+    low = jnp.where(low_core, value, other)
+    high = jnp.where(low_core, other, value)
     return jnp.concatenate([low, high])
 
 
 def local(embeddings, test_matrix):
     rows = embeddings.shape[0]
     factor = float(np.sqrt(np.float32(rows * 2 * SX * SY * SZ)))
+    core = lax.axis_index("core")
+    embeddings, *where = lax.optimization_barrier((embeddings, core, 1 - core, core == 0))
     held = CHUNKS[-1][0] + (CHUNKS[-1][1] + 127) // 128 * 128
     flat, high, mid = pl.pallas_call(
         gram_kernel,
@@ -258,17 +260,17 @@
         scratch_shapes=[pltpu.VMEM((rows, D), jnp.float32)]
         + [pltpu.VMEM((9, 256, 256), jnp.float32)] * 2
         + [pltpu.SemaphoreType.DMA((len(CHUNKS),))],
-        compiler_params=pltpu.CompilerParams(vmem_limit_bytes=LIMIT),
+        compiler_params=pltpu.CompilerParams(vmem_limit_bytes=LIMITS[0]),
         cost_estimate=pl.CostEstimate(flops=2 * rows * D * D * 2, bytes_accessed=4 * rows * D, transcendentals=0),
     )(embeddings)
-    flat = total(flat)
+    flat = total(flat, *where)
     basis, projected = pl.pallas_call(
         lambda *refs: finish_kernel(factor, *refs),
         in_specs=[pl.BlockSpec(memory_space=pltpu.VMEM)] * 4,
         out_specs=[pl.BlockSpec(memory_space=pltpu.VMEM)] * 2,
         out_shape=[jax.ShapeDtypeStruct((RANK, rows), jnp.float32), jax.ShapeDtypeStruct((RANK, D), jnp.float32)],
         scratch_shapes=[pltpu.VMEM((3, D, D), jnp.bfloat16)],
-        compiler_params=pltpu.CompilerParams(vmem_limit_bytes=LIMIT),
+        compiler_params=pltpu.CompilerParams(vmem_limit_bytes=LIMITS[1]),
         cost_estimate=pl.CostEstimate(flops=2 * rows * D * RANK * 8, bytes_accessed=4 * rows * D, transcendentals=0),
     )(flat, jnp.pad(test_matrix.T, ((0, 8), (0, 0))), high, mid)
     return basis.T, projected

time: 105 us -> 99.8 us (0.950)
  local copies, waits for them, and re-layouts: 4.78 us -> 0.15 us
  other arithmetic: 1.39 us -> 0.3 us
    unnamed x4 -> x2, local copies, waits for them, and re-layouts: 2.85 us -> 0.01 us
    add x1, other arithmetic: 1.15 us -> 0.07 us  [total(): value = pick(pair, mine) + lax.ppermute(pick(pair, theirs), 'core', swap)]
  transfers between devices with their start and end apart: 2 -> 2, of which waited for: 2 -> 2; matrix products, arithmetic and copies ran while one was open for 1% -> 0% of each run, Pallas kernels for 0% -> 0%
where the time goes in v8:
time: 99.8 us; the launch traced here: 99.5 us
  blocking collectives  62.5 us (63%)
  starting transfers between devices  17.4 us (17%)
  Pallas kernels  15 us (15%)
  waiting for transfers between devices  3.37 us (3%)
    all_to_all x3, blocking collectives, everyone(): lax.all_to_all(jnp.broadcast_to(value, (size,) + value.shape), axis, 0, 0)  38.7 us
    all_to_all x1, blocking collectives, total(): value = stacked_sum(lax.all_to_all(value.reshape(SX, -1, BLOCK), 'x', 0, 0))  13 us
    all_to_all x1, blocking collectives, total(): value = stacked_sum(lax.all_to_all(value.reshape(SY, -1, BLOCK), 'y', 0, 0))  10.8 us
    pallas_call x1, Pallas kernels, local(): pl.pallas_call(lambda *refs: finish_kernel(factor, *refs), in_specs=[pl.B...  9.64 us
    ppermute x1, starting transfers between devices, total(): value = pick(pair, mine) + lax.ppermute(pick(pair, theirs), 'core', swap)  8.78 us
    ppermute x1, starting transfers between devices, total(): other = lax.ppermute(value, 'core', swap)  8.66 us
    pallas_call x1, Pallas kernels, local(): pl.pallas_call(gram_kernel, in_specs=[pl.BlockSpec(memory_space=pl.ANY)],...  5.35 us
  transfers between devices with their start and end apart: 2, of which 2 were waited for; matrix products, arithmetic and copies ran while one was open for 0% of the time, Pallas kernels for 0%

profile of v8, /device:TPU:1, one launch (start us, length us, event | category | flops | bytes accessed | tf_op | source)
XLA Modules:
  0.0 99.5 jit_solution(10222290644382934250)
XLA Ops:
  0.6 5.3 %shard_map.41 = (f32[2560,128]{1,0:T(8,128)S(1)}, bf16[1408,768]{1,0:T(8,128)(2,1)S(1)}, bf16[1408,768]{1,0:T(8,128)(2,1)S(1)}) custom-call(f32[1344,768]{1,0:T(8,128)} %x_hbm), custom_call_target="tpu_custom_call" | custom-call | flops 3170893824 | bytes 4128768 | tf_op jit(solution)/shard_map/pallas_call | solution.py:255
  6.0 0.1 dynamic-slice_bitcast_fusion
  6.1 8.8 %collective-permute-start = (f32[1280,128]{1,0:T(8,128)S(1)}, f32[1280,128]{1,0:T(8,128)S(1)}, u32[]{:S(2)}, u32[]{:S(2)}) collective-permute-start(f32[1280,128]{1,0:T(8,128)S(1)} %dynamic-slice_bitcast_fusion), channel_id=1, source_target_pairs={{0,1},{1,0},{2,3},{3,2},{4,5},{5,4},{6,7},{7,6},{8,9},{9,8},{10,11... | collective-permute-start | bytes 1966088 | tf_op jit(solution)/shard_map/ppermute | solution.py:237
  14.8 1.7 %collective-permute-done = f32[1280,128]{1,0:T(8,128)S(1)} collective-permute-done((f32[1280,128]{1,0:T(8,128)S(1)}, f32[1280,128]{1,0:T(8,128)S(1)}, u32[]{:S(2)}, u32[]{:S(2)}) %collective-permute-start) | collective-permute-done | bytes 655392 | tf_op jit(solution)/shard_map/ppermute | solution.py:237
  16.5 0.1 bitcast_add_fusion
  16.6 13.0 %all_to_all.25 = f32[4,320,128]{2,1,0:T(8,128)S(1)} all-to-all(f32[4,320,128]{2,1,0:T(8,128)S(1)} %bitcast.19), channel_id=1, replica_groups=mesh['x'=4,'y'=8,'z'=8,'core'=2] {'x'}, dimensions={0} | all-to-all | bytes 1310720 | tf_op jit(solution)/shard_map/all_to_all | solution.py:238
  29.7 10.8 %all_to_all.26 = f32[8,40,128]{2,1,0:T(8,128)S(1)} all-to-all(f32[8,40,128]{2,1,0:T(8,128)S(1)} %bitcast.21), channel_id=1, replica_groups=mesh['x'=4,'y'=8,'z'=8,'core'=2] {'y'}, dimensions={0} | all-to-all | bytes 327680 | tf_op jit(solution)/shard_map/all_to_all | solution.py:239
  40.5 17.9 %all_to_all.27 = f32[8,40,128]{2,1,0:T(8,128)S(1)} all-to-all(f32[8,40,128]{2,1,0:T(8,128)S(1)} %broadcast_in_dim.9), channel_id=1, replica_groups=mesh['x'=4,'y'=8,'z'=8,'core'=2] {'z'}, dimensions={0} | all-to-all | bytes 327680 | tf_op jit(solution)/shard_map/all_to_all | solution.py:222
  58.4 0.0 copy-start
  58.4 10.8 %all_to_all.28 = f32[8,40,128]{2,1,0:T(8,128)S(1)} all-to-all(f32[8,40,128]{2,1,0:T(8,128)S(1)} %broadcast_in_dim.10), channel_id=1, replica_groups=mesh['x'=4,'y'=8,'z'=8,'core'=2] {'y'}, dimensions={0} | all-to-all | bytes 327680 | tf_op jit(solution)/shard_map/all_to_all | solution.py:222
  69.3 10.0 %all_to_all.29 = f32[4,320,128]{2,1,0:T(8,128)S(1)} all-to-all(f32[4,320,128]{2,1,0:T(8,128)S(1)} %broadcast_in_dim.11), channel_id=1, replica_groups=mesh['x'=4,'y'=8,'z'=8,'core'=2] {'x'}, dimensions={0} | all-to-all | bytes 1310720 | tf_op jit(solution)/shard_map/all_to_all | solution.py:222
  79.3 8.7 %collective-permute-start.1 = (f32[1280,128]{1,0:T(8,128)S(1)}, f32[1280,128]{1,0:T(8,128)S(1)}, u32[]{:S(2)}, u32[]{:S(2)}) collective-permute-start(f32[1280,128]{1,0:T(8,128)S(1)} %bitcast.20), channel_id=1, source_target_pairs={{0,1},{1,0},{2,3},{3,2},{4,5},{5,4},{6,7},{7,6},{8,9},{9,8},{10,11... | collective-permute-start | bytes 1966088 | tf_op jit(solution)/shard_map/ppermute | solution.py:243
  88.0 0.0 copy-done
  88.0 1.7 %collective-permute-done.1 = f32[1280,128]{1,0:T(8,128)S(1)} collective-permute-done((f32[1280,128]{1,0:T(8,128)S(1)}, f32[1280,128]{1,0:T(8,128)S(1)}, u32[]{:S(2)}, u32[]{:S(2)}) %collective-permute-start.1) | collective-permute-done | bytes 655392 | tf_op jit(solution)/shard_map/ppermute | solution.py:243
  89.7 0.1 broadcast_select_fusion.1
  89.8 0.1 pad_maximum_fusion.refs_0_
  89.9 9.6 %shard_map.42 = (f32[80,1344]{1,0:T(8,128)}, f32[80,768]{1,0:T(8,128)}) custom-call(f32[2560,128]{1,0:T(8,128)S(1)} %pad_maximum_fusion.refs_0_, f32[88,768]{1,0:T(8,128)S(1)} %pad.4.refs_1_, bf16[1408,768]{1,0:T(8,128)(2,1)S(1)} %get-tuple-element.16.refs_2_, bf16[1408,768]{1,0:T(8,128)(2,1)S(1)} %get-tuple-element.17.refs_3_), custom_call_target="tpu_custom_call" | custom-call | flops 1321205760 | bytes 4128768 | tf_op jit(solution)/shard_map/pallas_call | solution.py:267
  (7 shorter events, 0.1 us)
Async XLA Ops:
  6.1 10.5 %collective-permute-start = (f32[1280,128]{1,0:T(8,128)S(1)}, f32[1280,128]{1,0:T(8,128)S(1)}, u32[]{:S(2)}, u32[]{:S(2)}) collective-permute-start(f32[1280,128]{1,0:T(8,128)S(1)} %dynamic-slice_bitcast_fusion), channel_id=1, source_target_pairs={{0,1},{1,0},{2,3},{3,2},{4,5},{5,4},{6,7},{7,6},{8,9},{9,8},{10,11... | collective-permute-start | bytes 1966088 | tf_op jit(solution)/shard_map/ppermute | solution.py:237
  58.4 29.6 %copy-start = (f32[768,80]{0,1:T(8,128)S(1)}, f32[768,80]{0,1:T(8,128)}, u32[]{:S(2)}) copy-start(f32[768,80]{0,1:T(8,128)} %param.3) | copy-start | bytes 737284
  79.3 10.4 %collective-permute-start.1 = (f32[1280,128]{1,0:T(8,128)S(1)}, f32[1280,128]{1,0:T(8,128)S(1)}, u32[]{:S(2)}, u32[]{:S(2)}) collective-permute-start(f32[1280,128]{1,0:T(8,128)S(1)} %bitcast.20), channel_id=1, source_target_pairs={{0,1},{1,0},{2,3},{3,2},{4,5},{5,4},{6,7},{7,6},{8,9},{9,8},{10,11... | collective-permute-start | bytes 1966088 | tf_op jit(solution)/shard_map/ppermute | solution.py:243

commit v9 on v8

--- a/solution.py
+++ b/solution.py
@@ -13,7 +13,7 @@
 UPPER = [(a, b) for a in range(NB) for b in range(a + 1, NB)]
 PACKED = len(UPPER) * BLOCK
 DIAGS = PACKED + NB // 2 * BLOCK
-FLAT = 2560
+FLAT = 2368
 CHUNKS = ((0, 256), (256, 512), (768, 576))
 LIMITS = 45 * 2 ** 20, 45 * 2 ** 20
 
@@ -166,7 +166,7 @@
     return first[:n] + (first[n:2 * n] + second[:n] + small)
 
 
-def finish_kernel(factor, flat_ref, test_ref, high_ref, mid_ref, basis_ref, projected_ref, c_ref):
+def finish_kernel(factor, flat_ref, test_ref, high_ref, mid_ref, basis_hbm, projected_hbm, basis_ref, projected_ref, c_ref, sem):
     row, col = iota(0), iota(1)
 
     def place(a, b, value):
@@ -200,6 +200,8 @@
     second = inverse_factor(gram)
     second_stack = stack(second)
     projected_ref[...] = times(second_stack, split(reach)) * (1.0 / factor)
+    copies = [pltpu.make_async_copy(projected_ref, projected_hbm, sem.at[0])]
+    copies[0].start()
     empty = jnp.zeros((BLOCK - RANK, D), jnp.float32)
     weight = jnp.concatenate([times(second_stack, split(spanned)) * factor, empty], axis=0)
     weight = jnp.concatenate(halves(weight), axis=0).T
@@ -210,6 +212,12 @@
         main, rest = dot(high_ref[at, :], weight), dot(mid_ref[at, :], weight)
         value = main[:, :BLOCK] + (main[:, BLOCK:] + (rest[:, :BLOCK] + rest[:, BLOCK:]))
         basis_ref[:, at] = value.T[:RANK, :]
+        if start + size == total_rows or start == 512:
+            piece = pl.ds(0, 768) if start == 512 else pl.ds(768, total_rows - 768)
+            copies.append(pltpu.make_async_copy(basis_ref.at[:, piece], basis_hbm.at[:, piece], sem.at[len(copies)]))
+            copies[-1].start()
+    for copy in copies:
+        copy.wait()
 
 
 def tree(parts):
@@ -236,9 +244,11 @@
     pair = flat.reshape(2, FLAT // 2, BLOCK)
     value = pick(pair, mine) + lax.ppermute(pick(pair, theirs), "core", swap)
     value = stacked_sum(lax.all_to_all(value.reshape(SX, -1, BLOCK), "x", 0, 0))
+    rows = value.shape[0]
+    value = jnp.pad(value, ((0, -rows % (8 * SY)), (0, 0)))
     value = stacked_sum(lax.all_to_all(value.reshape(SY, -1, BLOCK), "y", 0, 0))
     value = stacked_sum(everyone(value, "z", SZ))
-    value = everyone(value, "y", SY).reshape(-1, BLOCK)
+    value = everyone(value, "y", SY).reshape(-1, BLOCK)[:rows]
     value = everyone(value, "x", SX).reshape(-1, BLOCK)
     other = lax.ppermute(value, "core", swap)
     low = jnp.where(low_core, value, other)
@@ -267,9 +277,14 @@
     basis, projected = pl.pallas_call(
         lambda *refs: finish_kernel(factor, *refs),
         in_specs=[pl.BlockSpec(memory_space=pltpu.VMEM)] * 4,
-        out_specs=[pl.BlockSpec(memory_space=pltpu.VMEM)] * 2,
+        out_specs=[pl.BlockSpec(memory_space=pl.ANY)] * 2,
         out_shape=[jax.ShapeDtypeStruct((RANK, rows), jnp.float32), jax.ShapeDtypeStruct((RANK, D), jnp.float32)],
-        scratch_shapes=[pltpu.VMEM((3, D, D), jnp.bfloat16)],
+        scratch_shapes=[
+            pltpu.VMEM((RANK, rows), jnp.float32),
+            pltpu.VMEM((RANK, D), jnp.float32),
+            pltpu.VMEM((3, D, D), jnp.bfloat16),
+            pltpu.SemaphoreType.DMA((3,)),
+        ],
         compiler_params=pltpu.CompilerParams(vmem_limit_bytes=LIMITS[1]),
         cost_estimate=pl.CostEstimate(flops=2 * rows * D * RANK * 8, bytes_accessed=4 * rows * D, transcendentals=0),
     )(flat, jnp.pad(test_matrix.T, ((0, 8), (0, 0))), high, mid)

time: 99.8 us -> 98.8 us (0.990)
  no operation moved by 1% of the time
where the time goes in v9:
time: 98.8 us; the launch traced here: 98.5 us
  blocking collectives  61.9 us (63%)
  starting transfers between devices  17.3 us (18%)
  Pallas kernels  14.9 us (15%)
  waiting for transfers between devices  3.23 us (3%)
    all_to_all x3, blocking collectives, everyone(): lax.all_to_all(jnp.broadcast_to(value, (size,) + value.shape), axis, 0, 0)  38.8 us
    all_to_all x1, blocking collectives, total(): value = stacked_sum(lax.all_to_all(value.reshape(SX, -1, BLOCK), 'x', 0, 0))  12.2 us
    all_to_all x1, blocking collectives, total(): value = stacked_sum(lax.all_to_all(value.reshape(SY, -1, BLOCK), 'y', 0, 0))  10.9 us
    pallas_call x1, Pallas kernels, local(): pl.pallas_call(lambda *refs: finish_kernel(factor, *refs), in_specs=[pl.B...  9.58 us
    ppermute x1, starting transfers between devices, total(): value = pick(pair, mine) + lax.ppermute(pick(pair, theirs), 'core', swap)  8.78 us
    ppermute x1, starting transfers between devices, total(): other = lax.ppermute(value, 'core', swap)  8.47 us
    pallas_call x1, Pallas kernels, local(): pl.pallas_call(gram_kernel, in_specs=[pl.BlockSpec(memory_space=pl.ANY)],...  5.34 us
  transfers between devices with their start and end apart: 2, of which 2 were waited for; matrix products, arithmetic and copies ran while one was open for 0% of the time, Pallas kernels for 0%

profile of v9, /device:TPU:1, one launch (start us, length us, event | category | flops | bytes accessed | tf_op | source)
XLA Modules:
  0.0 98.5 jit_solution(17791789886866430898)
XLA Ops:
  0.6 5.3 %shard_map.41 = (f32[2368,128]{1,0:T(8,128)S(1)}, bf16[1408,768]{1,0:T(8,128)(2,1)S(1)}, bf16[1408,768]{1,0:T(8,128)(2,1)S(1)}) custom-call(f32[1344,768]{1,0:T(8,128)} %x_hbm), custom_call_target="tpu_custom_call" | custom-call | flops 3170893824 | bytes 4128768 | tf_op jit(solution)/shard_map/pallas_call | solution.py:265
  6.0 0.1 dynamic-slice_bitcast_fusion
  6.0 8.8 %collective-permute-start = (f32[1184,128]{1,0:T(8,128)S(1)}, f32[1184,128]{1,0:T(8,128)S(1)}, u32[]{:S(2)}, u32[]{:S(2)}) collective-permute-start(f32[1184,128]{1,0:T(8,128)S(1)} %dynamic-slice_bitcast_fusion), channel_id=1, source_target_pairs={{0,1},{1,0},{2,3},{3,2},{4,5},{5,4},{6,7},{7,6},{8,9},{9,8},{10,11... | collective-permute-start | bytes 1818632 | tf_op jit(solution)/shard_map/ppermute | solution.py:245
  14.8 1.6 %collective-permute-done = f32[1184,128]{1,0:T(8,128)S(1)} collective-permute-done((f32[1184,128]{1,0:T(8,128)S(1)}, f32[1184,128]{1,0:T(8,128)S(1)}, u32[]{:S(2)}, u32[]{:S(2)}) %collective-permute-start) | collective-permute-done | bytes 606240 | tf_op jit(solution)/shard_map/ppermute | solution.py:245
  16.5 0.1 bitcast_add_fusion
  16.5 12.2 %all_to_all.25 = f32[4,296,128]{2,1,0:T(8,128)S(1)} all-to-all(f32[4,296,128]{2,1,0:T(8,128)S(1)} %bitcast.22), channel_id=1, replica_groups=mesh['x'=4,'y'=8,'z'=8,'core'=2] {'x'}, dimensions={0} | all-to-all | bytes 1212416 | tf_op jit(solution)/shard_map/all_to_all | solution.py:246
  28.8 10.9 %all_to_all.26 = f32[8,40,128]{2,1,0:T(8,128)S(1)} all-to-all(f32[8,40,128]{2,1,0:T(8,128)S(1)} %bitcast.23), channel_id=1, replica_groups=mesh['x'=4,'y'=8,'z'=8,'core'=2] {'y'}, dimensions={0} | all-to-all | bytes 327680 | tf_op jit(solution)/shard_map/all_to_all | solution.py:249
  39.8 18.2 %all_to_all.27 = f32[8,40,128]{2,1,0:T(8,128)S(1)} all-to-all(f32[8,40,128]{2,1,0:T(8,128)S(1)} %broadcast_in_dim.9), channel_id=1, replica_groups=mesh['x'=4,'y'=8,'z'=8,'core'=2] {'z'}, dimensions={0} | all-to-all | bytes 327680 | tf_op jit(solution)/shard_map/all_to_all | solution.py:230
  58.0 10.7 %all_to_all.28 = f32[8,40,128]{2,1,0:T(8,128)S(1)} all-to-all(f32[8,40,128]{2,1,0:T(8,128)S(1)} %broadcast_in_dim.10), channel_id=1, replica_groups=mesh['x'=4,'y'=8,'z'=8,'core'=2] {'y'}, dimensions={0} | all-to-all | bytes 327680 | tf_op jit(solution)/shard_map/all_to_all | solution.py:230
  68.7 0.0 copy-start
  68.7 9.9 %all_to_all.29 = f32[4,296,128]{2,1,0:T(8,128)S(1)} all-to-all(f32[4,296,128]{2,1,0:T(8,128)S(1)} %broadcast_in_dim.11), channel_id=1, replica_groups=mesh['x'=4,'y'=8,'z'=8,'core'=2] {'x'}, dimensions={0} | all-to-all | bytes 1212416 | tf_op jit(solution)/shard_map/all_to_all | solution.py:230
  78.6 8.5 %collective-permute-start.1 = (f32[1184,128]{1,0:T(8,128)S(1)}, f32[1184,128]{1,0:T(8,128)S(1)}, u32[]{:S(2)}, u32[]{:S(2)}) collective-permute-start(f32[1184,128]{1,0:T(8,128)S(1)} %bitcast.21), channel_id=1, source_target_pairs={{0,1},{1,0},{2,3},{3,2},{4,5},{5,4},{6,7},{7,6},{8,9},{9,8},{10,11... | collective-permute-start | bytes 1818632 | tf_op jit(solution)/shard_map/ppermute | solution.py:253
  87.1 0.0 copy-done
  87.2 1.6 %collective-permute-done.1 = f32[1184,128]{1,0:T(8,128)S(1)} collective-permute-done((f32[1184,128]{1,0:T(8,128)S(1)}, f32[1184,128]{1,0:T(8,128)S(1)}, u32[]{:S(2)}, u32[]{:S(2)}) %collective-permute-start.1) | collective-permute-done | bytes 606240 | tf_op jit(solution)/shard_map/ppermute | solution.py:253
  88.7 0.1 broadcast_select_fusion.1
  88.8 0.1 pad_maximum_fusion.refs_0_
  88.9 9.6 %shard_map.42 = (f32[80,1344]{1,0:T(8,128)}, f32[80,768]{1,0:T(8,128)}) custom-call(f32[2368,128]{1,0:T(8,128)S(1)} %pad_maximum_fusion.refs_0_, f32[88,768]{1,0:T(8,128)S(1)} %pad.9.refs_1_, bf16[1408,768]{1,0:T(8,128)(2,1)S(1)} %get-tuple-element.16.refs_2_, bf16[1408,768]{1,0:T(8,128)(2,1)S(1)} %get-tuple-element.17.refs_3_), custom_call_target="tpu_custom_call" | custom-call | flops 1321205760 | bytes 4128768 | tf_op jit(solution)/shard_map/pallas_call | solution.py:277
  (9 shorter events, 0.2 us)
Async XLA Ops:
  6.0 10.4 %collective-permute-start = (f32[1184,128]{1,0:T(8,128)S(1)}, f32[1184,128]{1,0:T(8,128)S(1)}, u32[]{:S(2)}, u32[]{:S(2)}) collective-permute-start(f32[1184,128]{1,0:T(8,128)S(1)} %dynamic-slice_bitcast_fusion), channel_id=1, source_target_pairs={{0,1},{1,0},{2,3},{3,2},{4,5},{5,4},{6,7},{7,6},{8,9},{9,8},{10,11... | collective-permute-start | bytes 1818632 | tf_op jit(solution)/shard_map/ppermute | solution.py:245
  68.7 18.4 %copy-start = (f32[768,80]{0,1:T(8,128)S(1)}, f32[768,80]{0,1:T(8,128)}, u32[]{:S(2)}) copy-start(f32[768,80]{0,1:T(8,128)} %param.3) | copy-start | bytes 737284
  78.6 10.1 %collective-permute-start.1 = (f32[1184,128]{1,0:T(8,128)S(1)}, f32[1184,128]{1,0:T(8,128)S(1)}, u32[]{:S(2)}, u32[]{:S(2)}) collective-permute-start(f32[1184,128]{1,0:T(8,128)S(1)} %bitcast.21), channel_id=1, source_target_pairs={{0,1},{1,0},{2,3},{3,2},{4,5},{5,4},{6,7},{7,6},{8,9},{9,8},{10,11... | collective-permute-start | bytes 1818632 | tf_op jit(solution)/shard_map/ppermute | solution.py:253

commit v10 on v9

--- a/solution.py
+++ b/solution.py
@@ -60,13 +60,11 @@
         deep = slice(start, start + (size + 127) // 128 * 128)
         for i in range(3):
             high_t = high_ref[deep, 256 * i:256 * (i + 1)].T
-            for j in range(3):
-                cols = slice(256 * j, 256 * (j + 1))
-                if i <= j:
-                    value = dot(high_t, high_ref[deep, cols])
-                    even_ref[3 * i + j] = value if n == 0 else even_ref[3 * i + j] + value
-                value = dot(high_t, mid_ref[deep, cols])
-                odd_ref[3 * i + j] = value if n == 0 else odd_ref[3 * i + j] + value
+            cols = slice(256 * i, D)
+            value = dot(high_t, high_ref[deep, cols])
+            even_ref[i, :, cols] = value if n == 0 else even_ref[i, :, cols] + value
+            value = dot(high_t, mid_ref[deep, :])
+            odd_ref[i] = value if n == 0 else odd_ref[i] + value
             if i == 0 and n + 1 < len(CHUNKS):
                 arrive(n + 1)
 
@@ -74,7 +72,8 @@
     flat_ref[DIAGS:, :] = jnp.zeros((FLAT - DIAGS, BLOCK), jnp.float32)
     for i in range(3):
         for j in range(i, 3):
-            value = even_ref[3 * i + j] + (odd_ref[3 * i + j] + odd_ref[3 * j + i].T)
+            left, right = slice(256 * i, 256 * (i + 1)), slice(256 * j, 256 * (j + 1))
+            value = even_ref[i, :, right] + (odd_ref[i, :, right] + odd_ref[j, :, left].T)
             for p in range(2):
                 for q in range(2):
                     a, b = 2 * i + p, 2 * j + q
@@ -166,8 +165,16 @@
     return first[:n] + (first[n:2 * n] + second[:n] + small)
 
 
-def finish_kernel(factor, flat_ref, test_ref, high_ref, mid_ref, basis_hbm, projected_hbm, basis_ref, projected_ref, c_ref, sem):
+def finish_kernel(factor, low_ref, upper_ref, test_ref, high_ref, mid_ref, basis_hbm, projected_hbm, basis_ref, projected_ref, c_ref, sem):
     row, col = iota(0), iota(1)
+
+    def flat(start, size):
+        end, middle = start + size, FLAT // 2
+        if end <= middle:
+            return low_ref[start:end, :]
+        if start >= middle:
+            return upper_ref[start - middle:end - middle, :]
+        return jnp.concatenate([low_ref[start:, :], upper_ref[:end - middle, :]], axis=0)
 
     def place(a, b, value):
         for k, part in enumerate(split(value)):
@@ -178,14 +185,14 @@
     for i in range(NB // 2):
         for n, (a, b) in enumerate(UPPER):
             if a // 2 == i:
-                value = flat_ref[n * BLOCK:(n + 1) * BLOCK, :]
+                value = flat(n * BLOCK, BLOCK)
                 place(a, b, value)
                 place(b, a, value.T)
-        value = flat_ref[PACKED + i * BLOCK:PACKED + (i + 1) * BLOCK, :]
+        value = flat(PACKED + i * BLOCK, BLOCK)
         flipped = value.T
         place(2 * i, 2 * i, jnp.where(row <= col, value, flipped))
         other = jnp.where(row > col, value, flipped)
-        place(2 * i + 1, 2 * i + 1, jnp.where(row == col, flat_ref[DIAGS + i:DIAGS + i + 1, :], other))
+        place(2 * i + 1, 2 * i + 1, jnp.where(row == col, flat(DIAGS + i, 1), other))
         deep = slice(256 * i, 256 * (i + 1))
         value = times(test[:, deep], [c_ref[k, deep, :] for k in range(3)])
         image = value if i == 0 else image + value
@@ -253,7 +260,7 @@
     other = lax.ppermute(value, "core", swap)
     low = jnp.where(low_core, value, other)
     high = jnp.where(low_core, other, value)
-    return jnp.concatenate([low, high])
+    return low, high
 
 
 def local(embeddings, test_matrix):
@@ -268,15 +275,15 @@
         out_specs=[pl.BlockSpec(memory_space=pltpu.VMEM)] * 3,
         out_shape=[jax.ShapeDtypeStruct((FLAT, BLOCK), jnp.float32)] + [jax.ShapeDtypeStruct((held, D), jnp.bfloat16)] * 2,
         scratch_shapes=[pltpu.VMEM((rows, D), jnp.float32)]
-        + [pltpu.VMEM((9, 256, 256), jnp.float32)] * 2
+        + [pltpu.VMEM((3, 256, D), jnp.float32)] * 2
         + [pltpu.SemaphoreType.DMA((len(CHUNKS),))],
         compiler_params=pltpu.CompilerParams(vmem_limit_bytes=LIMITS[0]),
         cost_estimate=pl.CostEstimate(flops=2 * rows * D * D * 2, bytes_accessed=4 * rows * D, transcendentals=0),
     )(embeddings)
-    flat = total(flat, *where)
+    low, upper = total(flat, *where)
     basis, projected = pl.pallas_call(
         lambda *refs: finish_kernel(factor, *refs),
-        in_specs=[pl.BlockSpec(memory_space=pltpu.VMEM)] * 4,
+        in_specs=[pl.BlockSpec(memory_space=pltpu.VMEM)] * 5,
         out_specs=[pl.BlockSpec(memory_space=pl.ANY)] * 2,
         out_shape=[jax.ShapeDtypeStruct((RANK, rows), jnp.float32), jax.ShapeDtypeStruct((RANK, D), jnp.float32)],
         scratch_shapes=[
@@ -287,7 +294,7 @@
         ],
         compiler_params=pltpu.CompilerParams(vmem_limit_bytes=LIMITS[1]),
         cost_estimate=pl.CostEstimate(flops=2 * rows * D * RANK * 8, bytes_accessed=4 * rows * D, transcendentals=0),
-    )(flat, jnp.pad(test_matrix.T, ((0, 8), (0, 0))), high, mid)
+    )(low, upper, jnp.pad(test_matrix.T, ((0, 8), (0, 0))), high, mid)
     return basis.T, projected
 
 

time: 98.8 us -> 98.8 us (level)
  no operation moved by 1% of the time
where the time goes in v10:
time: 98.8 us; the launch traced here: 98.5 us
  blocking collectives  61.9 us (63%)
  starting transfers between devices  17.3 us (18%)
  Pallas kernels  15 us (15%)
  waiting for transfers between devices  3.23 us (3%)
    all_to_all x3, blocking collectives, everyone(): lax.all_to_all(jnp.broadcast_to(value, (size,) + value.shape), axis, 0, 0)  38.6 us
    all_to_all x1, blocking collectives, total(): value = stacked_sum(lax.all_to_all(value.reshape(SX, -1, BLOCK), 'x', 0, 0))  12.2 us
    all_to_all x1, blocking collectives, total(): value = stacked_sum(lax.all_to_all(value.reshape(SY, -1, BLOCK), 'y', 0, 0))  11.1 us
    pallas_call x1, Pallas kernels, local(): pl.pallas_call(lambda *refs: finish_kernel(factor, *refs), in_specs=[pl.B...  9.58 us
    ppermute x1, starting transfers between devices, total(): value = pick(pair, mine) + lax.ppermute(pick(pair, theirs), 'core', swap)  8.79 us
    ppermute x1, starting transfers between devices, total(): other = lax.ppermute(value, 'core', swap)  8.47 us
    pallas_call x1, Pallas kernels, local(): pl.pallas_call(gram_kernel, in_specs=[pl.BlockSpec(memory_space=pl.ANY)],...  5.43 us
  transfers between devices with their start and end apart: 2, of which 2 were waited for; matrix products, arithmetic and copies ran while one was open for 0% of the time, Pallas kernels for 0%

profile of v10, /device:TPU:1, one launch (start us, length us, event | category | flops | bytes accessed | tf_op | source)
XLA Modules:
  0.0 98.5 jit_solution(9287557584902895949)
XLA Ops:
  0.6 5.4 %shard_map.41 = (f32[2368,128]{1,0:T(8,128)S(1)}, bf16[1408,768]{1,0:T(8,128)(2,1)S(1)}, bf16[1408,768]{1,0:T(8,128)(2,1)S(1)}) custom-call(f32[1344,768]{1,0:T(8,128)} %x_hbm), custom_call_target="tpu_custom_call" | custom-call | flops 3170893824 | bytes 4128768 | tf_op jit(solution)/shard_map/pallas_call | solution.py:272
  6.1 0.1 dynamic-slice_bitcast_fusion
  6.1 8.8 %collective-permute-start = (f32[1184,128]{1,0:T(8,128)S(1)}, f32[1184,128]{1,0:T(8,128)S(1)}, u32[]{:S(2)}, u32[]{:S(2)}) collective-permute-start(f32[1184,128]{1,0:T(8,128)S(1)} %dynamic-slice_bitcast_fusion), channel_id=1, source_target_pairs={{0,1},{1,0},{2,3},{3,2},{4,5},{5,4},{6,7},{7,6},{8,9},{9,8},{10,11... | collective-permute-start | bytes 1818632 | tf_op jit(solution)/shard_map/ppermute | solution.py:252
  14.9 1.6 %collective-permute-done = f32[1184,128]{1,0:T(8,128)S(1)} collective-permute-done((f32[1184,128]{1,0:T(8,128)S(1)}, f32[1184,128]{1,0:T(8,128)S(1)}, u32[]{:S(2)}, u32[]{:S(2)}) %collective-permute-start) | collective-permute-done | bytes 606240 | tf_op jit(solution)/shard_map/ppermute | solution.py:252
  16.6 0.1 bitcast_add_fusion
  16.6 12.2 %all_to_all.25 = f32[4,296,128]{2,1,0:T(8,128)S(1)} all-to-all(f32[4,296,128]{2,1,0:T(8,128)S(1)} %bitcast.22), channel_id=1, replica_groups=mesh['x'=4,'y'=8,'z'=8,'core'=2] {'x'}, dimensions={0} | all-to-all | bytes 1212416 | tf_op jit(solution)/shard_map/all_to_all | solution.py:253
  28.9 0.0 copy-start
  28.9 11.1 %all_to_all.26 = f32[8,40,128]{2,1,0:T(8,128)S(1)} all-to-all(f32[8,40,128]{2,1,0:T(8,128)S(1)} %bitcast.23), channel_id=1, replica_groups=mesh['x'=4,'y'=8,'z'=8,'core'=2] {'y'}, dimensions={0} | all-to-all | bytes 327680 | tf_op jit(solution)/shard_map/all_to_all | solution.py:256
  40.0 18.2 %all_to_all.27 = f32[8,40,128]{2,1,0:T(8,128)S(1)} all-to-all(f32[8,40,128]{2,1,0:T(8,128)S(1)} %broadcast_in_dim.9), channel_id=1, replica_groups=mesh['x'=4,'y'=8,'z'=8,'core'=2] {'z'}, dimensions={0} | all-to-all | bytes 327680 | tf_op jit(solution)/shard_map/all_to_all | solution.py:237
  58.2 10.7 %all_to_all.28 = f32[8,40,128]{2,1,0:T(8,128)S(1)} all-to-all(f32[8,40,128]{2,1,0:T(8,128)S(1)} %broadcast_in_dim.10), channel_id=1, replica_groups=mesh['x'=4,'y'=8,'z'=8,'core'=2] {'y'}, dimensions={0} | all-to-all | bytes 327680 | tf_op jit(solution)/shard_map/all_to_all | solution.py:237
  69.0 9.8 %all_to_all.29 = f32[4,296,128]{2,1,0:T(8,128)S(1)} all-to-all(f32[4,296,128]{2,1,0:T(8,128)S(1)} %broadcast_in_dim.11), channel_id=1, replica_groups=mesh['x'=4,'y'=8,'z'=8,'core'=2] {'x'}, dimensions={0} | all-to-all | bytes 1212416 | tf_op jit(solution)/shard_map/all_to_all | solution.py:237
  78.7 8.5 %collective-permute-start.1 = (f32[1184,128]{1,0:T(8,128)S(1)}, f32[1184,128]{1,0:T(8,128)S(1)}, u32[]{:S(2)}, u32[]{:S(2)}) collective-permute-start(f32[1184,128]{1,0:T(8,128)S(1)} %bitcast.21), channel_id=1, source_target_pairs={{0,1},{1,0},{2,3},{3,2},{4,5},{5,4},{6,7},{7,6},{8,9},{9,8},{10,11... | collective-permute-start | bytes 1818632 | tf_op jit(solution)/shard_map/ppermute | solution.py:260
  87.2 0.0 copy-done
  87.2 1.6 %collective-permute-done.1 = f32[1184,128]{1,0:T(8,128)S(1)} collective-permute-done((f32[1184,128]{1,0:T(8,128)S(1)}, f32[1184,128]{1,0:T(8,128)S(1)}, u32[]{:S(2)}, u32[]{:S(2)}) %collective-permute-start.1) | collective-permute-done | bytes 606240 | tf_op jit(solution)/shard_map/ppermute | solution.py:260
  88.8 0.1 broadcast_select_fusion
  88.9 9.6 %shard_map.42 = (f32[80,1344]{1,0:T(8,128)}, f32[80,768]{1,0:T(8,128)}) custom-call(f32[1184,128]{1,0:T(8,128)S(1)} %get-tuple-element.21.refs_0_, f32[1184,128]{1,0:T(8,128)S(1)} %get-tuple-element.20.refs_1_, f32[88,768]{1,0:T(8,128)S(1)} %pad.9.refs_2_, bf16[1408,768]{1,0:T(8,128)(2,1)S(1)} %get-tuple-element.16.refs_3_, ...), custom_call_target="tpu_custom_call" | custom-call | flops 1321205760 | bytes 4128768 | tf_op jit(solution)/shard_map/pallas_call | solution.py:284
  (9 shorter events, 0.2 us)
Async XLA Ops:
  6.1 10.4 %collective-permute-start = (f32[1184,128]{1,0:T(8,128)S(1)}, f32[1184,128]{1,0:T(8,128)S(1)}, u32[]{:S(2)}, u32[]{:S(2)}) collective-permute-start(f32[1184,128]{1,0:T(8,128)S(1)} %dynamic-slice_bitcast_fusion), channel_id=1, source_target_pairs={{0,1},{1,0},{2,3},{3,2},{4,5},{5,4},{6,7},{7,6},{8,9},{9,8},{10,11... | collective-permute-start | bytes 1818632 | tf_op jit(solution)/shard_map/ppermute | solution.py:252
  28.9 58.4 %copy-start = (f32[768,80]{0,1:T(8,128)S(1)}, f32[768,80]{0,1:T(8,128)}, u32[]{:S(2)}) copy-start(f32[768,80]{0,1:T(8,128)} %param.3) | copy-start | bytes 737284
  78.7 10.1 %collective-permute-start.1 = (f32[1184,128]{1,0:T(8,128)S(1)}, f32[1184,128]{1,0:T(8,128)S(1)}, u32[]{:S(2)}, u32[]{:S(2)}) collective-permute-start(f32[1184,128]{1,0:T(8,128)S(1)} %bitcast.21), channel_id=1, source_target_pairs={{0,1},{1,0},{2,3},{3,2},{4,5},{5,4},{6,7},{7,6},{8,9},{9,8},{10,11... | collective-permute-start | bytes 1818632 | tf_op jit(solution)/shard_map/ppermute | solution.py:260
